TPU v7x, 32 devices: a whole 2x2x4 slice. The times are simulated.
32 devices in a mesh: expert: 8 (over y, x, core), dp: 4 (over z).
Axes of the slice: x: 2, y: 2, z: 4, core: 2. Of those that a mesh axis runs over, the one named last changes fastest.
Arguments:
- tokens: bfloat16 [4, 1024, 1536], P('dp', 'expert'), may hold values from -6 to 6
- out_cotangent: bfloat16 [4, 1024, 1536], P('dp', 'expert'), may hold values from -6 to 6
- chosen_rows: int32 [4, 8, 8, 16], P('dp', 'expert'), may hold values from 0 to 127, as said below
- counts: int32 [4, 8, 8], P('dp', 'expert'), may hold values from 0 to 16, as said below
- gate_weights: bfloat16 [4, 8, 8, 16], P('dp', 'expert'), may hold values from 0.099609375 to 1
- in_weights: bfloat16 [8, 1536, 1536], P('expert'), may hold values from -0.15625 to 0.15625
- down_weights: bfloat16 [8, 768, 1536], P('expert'), may hold values from -0.21875 to 0.21875
Outputs:
- token_grad: bfloat16 [4, 1024, 1536], P('dp', 'expert')
- gate_grad: bfloat16 [4, 8, 8, 16], P('dp', 'expert')
- in_grad: bfloat16 [8, 1536, 1536], P('expert', 'dp')
- down_grad: bfloat16 [8, 768, 1536], P('expert', None, 'dp')
Inputs may be any that keep to these rules, and one draw needn't show every extreme that they name: `chosen_rows`: the entries of one device for one expert are distinct local token rows. For each expert and replica the counts over the 8 source devices sum to 64.
All inputs are finite; a program needn't handle non-finite values.
Results may differ from a plain program's by a relative error of at most 0.0095.
Values may be sent and summed in bfloat16 or wider, within the bound.
No kernel may reach another device: no remote copies, remote signals or barrier semaphores. Data moves between devices by JAX's collectives and lax.ppermute only.
A program may use at most 64 MiB of HBM per device.

v0:
```python
import jax
import jax.numpy as jnp
from jax import lax
from jax.sharding import PartitionSpec as P


def expert_pass(x_rows, cot_rows, gated, w_first, w_second):
    inner = w_second.shape[0]
    pre = jnp.dot(x_rows, w_first, preferred_element_type=jnp.float32)
    gate_pre = pre[:, :inner]
    up_pre = pre[:, inner:]
    squash = jax.nn.sigmoid(gate_pre)
    swished = gate_pre * squash
    hidden = (swished * up_pre).astype(jnp.bfloat16)
    slot_out = jnp.dot(hidden, w_second, preferred_element_type=jnp.float32)
    slot_gate = jnp.sum(slot_out * cot_rows.astype(jnp.float32), axis=-1).astype(jnp.bfloat16)
    scaled = (gated.astype(jnp.float32)[:, None] * cot_rows.astype(jnp.float32)).astype(
        jnp.bfloat16
    )
    hidden_grad = lax.dot_general(
        scaled, w_second, (((1,), (1,)), ((), ())), preferred_element_type=jnp.float32
    )
    pre_gate_grad = hidden_grad * up_pre * (squash * (1.0 + gate_pre * (1.0 - squash)))
    pre_up_grad = hidden_grad * swished
    in_rows = jnp.concatenate([pre_gate_grad, pre_up_grad], axis=1).astype(jnp.bfloat16)
    slot_grad = lax.dot_general(
        in_rows, w_first, (((1,), (1,)), ((), ())), preferred_element_type=jnp.float32
    ).astype(jnp.bfloat16)
    return (slot_grad, slot_gate, in_rows, hidden, scaled)


def column_term(left, right):
    return lax.dot_general(
        left, right, (((0,), (0,)), ((), ())), preferred_element_type=jnp.float32
    )


def on_device(tokens, out_cotangent, chosen_rows, counts, gate_weights, in_weights, down_weights):
    local_tokens = tokens[0]
    local_cot = out_cotangent[0]
    local_rows = chosen_rows[0, 0]
    peers, most = local_rows.shape
    slots = peers * most
    width = local_tokens.shape[1]
    slot_iota = lax.broadcasted_iota(jnp.int32, (peers, most), 1)
    usable = slot_iota < counts[0, 0][:, None]
    gate_rows = jnp.where(usable, gate_weights[0, 0], jnp.zeros_like(gate_weights[0, 0]))
    x_sent = jnp.take(local_tokens, local_rows, axis=0)
    cot_sent = jnp.take(local_cot, local_rows, axis=0)
    arrived = (
        lax.all_to_all(x_sent, "expert", split_axis=0, concat_axis=0, tiled=True),
        lax.all_to_all(cot_sent, "expert", split_axis=0, concat_axis=0, tiled=True),
        lax.all_to_all(gate_rows, "expert", split_axis=0, concat_axis=0, tiled=True),
    )
    x_rows = arrived[0].reshape(slots, width)
    cot_rows = arrived[1].reshape(slots, width)
    gated = arrived[2].reshape(slots)
    w_first = in_weights[0]
    w_second = down_weights[0]
    slot_grad, slot_gate, in_rows, hidden, scaled = expert_pass(
        x_rows, cot_rows, gated, w_first, w_second
    )
    returned = (
        lax.all_to_all(
            slot_grad.reshape(peers, most, width), "expert", split_axis=0, concat_axis=0, tiled=True
        ),
        lax.all_to_all(
            slot_gate.reshape(peers, most), "expert", split_axis=0, concat_axis=0, tiled=True
        ),
    )
    token_iota = lax.broadcasted_iota(jnp.int32, (local_tokens.shape[0], slots), 0)
    one_hot = (local_rows.reshape(1, slots) == token_iota).astype(jnp.bfloat16)
    summed = jnp.dot(one_hot, returned[0].reshape(slots, width), preferred_element_type=jnp.float32)
    gate_part = jnp.where(usable, returned[1], jnp.zeros_like(returned[1]))
    token_grad = summed.astype(jnp.bfloat16)[None]
    gate_grad = gate_part[None, None]
    in_share = lax.psum_scatter(
        column_term(x_rows, in_rows).astype(jnp.bfloat16), "dp", scatter_dimension=0, tiled=True
    )
    down_share = lax.psum_scatter(
        column_term(scaled, hidden).astype(jnp.bfloat16), "dp", scatter_dimension=0, tiled=True
    )
    in_grad = in_share[None]
    down_grad = down_share.T[None]
    return (token_grad, gate_grad, in_grad, down_grad)


def solution(mesh):
    return jax.shard_map(
        on_device,
        mesh=mesh,
        in_specs=(
            P("dp", "expert", None),
            P("dp", "expert", None),
            P("dp", "expert", None, None),
            P("dp", "expert", None),
            P("dp", "expert", None, None),
            P("expert", None, None),
            P("expert", None, None),
        ),
        out_specs=(
            P("dp", "expert", None),
            P("dp", "expert", None, None),
            P("expert", "dp", None),
            P("expert", None, "dp"),
        ),
        check_vma=False,
    )
```

profile of v0, /device:TPU:0, one launch (start us, length us, event | category | flops | bytes accessed | tf_op | source)
XLA Modules:
  0.0 191.1 jit_solution(11298831429075883490)
XLA Ops:
  7.2 0.0 copy-start
  7.2 0.0 copy-start.1
  7.2 0.9 fusion.17
  8.1 0.6 copy.16
  8.7 5.2 %all-to-all-start = ((bf16[8,1,16]{2,1,0:T(2,128)(2,1)}), bf16[8,1,16]{2,1,0:T(2,128)(2,1)S(1)}, u32[]{:S(2)}, u32[]{:S(2)}) async-start(bf16[8,1,16]{2,1,0:T(2,128)(2,1)} %copy.16), calls=%async_computation | async-start | bytes 8192 | tf_op jit(solution)/shard_map/all_to_all | solution.py:53
  13.9 0.7 compare_and_fusion
  14.6 0.7 compare_select_fusion
  15.3 0.1 reshape.174
  15.3 2.3 %gather_fusion.1 = bf16[128,1536]{1,0:T(8,128)(2,1)S(1)} fusion(bf16[128,1536]{1,0:T(8,128)(2,1)} %bitcast.57, s32[1024]{0:T(1024)S(1)} %pad_clamp_fusion), kind=kCustom, calls=%fused_computation.1.clone | custom fusion | bytes 786944 | tf_op jit(solution)/shard_map/jit(_take)/gather | solution.py:48
  17.7 0.0 copy-done.1
  17.7 0.9 gather_fusion
  18.6 1.0 broadcast_select_fusion
  19.6 0.0 all-to-all-done
  19.6 4.2 %all-to-all-start.2 = ((bf16[8,16,1536]{2,1,0:T(8,128)(2,1)}), bf16[8,16,1536]{2,1,0:T(8,128)(2,1)S(1)}, u32[]{:S(2)}, u32[]{:S(2)}) async-start(bf16[8,16,1536]{2,1,0:T(8,128)(2,1)} %get-tuple-element.22), calls=%async_computation.2 | async-start | bytes 786432 | tf_op jit(solution)/shard_map/all_to_all | solution.py:51
  23.8 0.1 reshape.153
  23.9 8.3 %all-to-all-done.2 = bf16[8,16,1536]{2,1,0:T(8,128)(2,1)S(1)} async-done(((bf16[8,16,1536]{2,1,0:T(8,128)(2,1)}), bf16[8,16,1536]{2,1,0:T(8,128)(2,1)S(1)}, u32[]{:S(2)}, u32[]{:S(2)}) %all-to-all-start.2) | async-done | bytes 393248 | tf_op jit(solution)/shard_map/all_to_all | solution.py:51
  32.1 3.5 %all-to-all-start.1 = ((bf16[8,16,1536]{2,1,0:T(8,128)(2,1)}), bf16[8,16,1536]{2,1,0:T(8,128)(2,1)S(1)}, u32[]{:S(2)}, u32[]{:S(2)}) async-start(bf16[8,16,1536]{2,1,0:T(8,128)(2,1)} %get-tuple-element.23), calls=%async_computation.1 | async-start | bytes 786432 | tf_op jit(solution)/shard_map/all_to_all | solution.py:52
  35.6 0.0 reduce-scatter.5.cloned.1.call-start
  35.6 4.0 %fusion.2 = f32[128,1536]{1,0:T(8,128)} fusion(bf16[128,1536]{1,0:T(8,128)(2,1)S(1)} %bitcast.60, bf16[1,1536,1536]{2,1,0:T(8,128)(2,1)} %param.14), kind=kOutput, calls=%fused_computation.5 | convolution fusion | flops 603979776 | bytes 5898240 | tf_op jit(solution)/shard_map/dot_general | solution.py:9
  39.6 4.2 %all-to-all-done.1 = bf16[8,16,1536]{2,1,0:T(8,128)(2,1)S(1)} async-done(((bf16[8,16,1536]{2,1,0:T(8,128)(2,1)}), bf16[8,16,1536]{2,1,0:T(8,128)(2,1)S(1)}, u32[]{:S(2)}, u32[]{:S(2)}) %all-to-all-start.1) | async-done | bytes 393248 | tf_op jit(solution)/shard_map/all_to_all | solution.py:52
  43.9 0.1 multiply_convert_fusion
  44.0 0.0 copy-done
  44.0 2.0 %multiply_convert_fusion.3 = (bf16[128,768]{1,0:T(8,128)(2,1)S(1)}, bf16[128,768]{1,0:T(8,128)(2,1)S(1)}, bf16[128,768]{1,0:T(8,128)(2,1)S(1)}) fusion(f32[128,1536]{1,0:T(8,128)} %fusion.2, bf16[128,1536]{1,0:T(8,128)(2,1)S(1)} %bitcast.66, bf16[1,768,1536]{2,1,0:T(8,128)(2,1)S(1)} %copy-done), kind=kOutput, calls=%fused_computation.22 | convolution fusion | flops 303464448 | bytes 4128768 | tf_op jit(solution)/shard_map/dot_general | solution.py:20
  46.1 0.0 copy-start.2
  46.1 0.1 fusion.14
  46.2 0.5 copy-done.2
  46.7 2.2 %convolution_convert_fusion.1 = bf16[1536,768]{1,0:T(8,128)(2,1)} fusion(bf16[128,1536]{1,0:T(8,128)(2,1)S(1)} %fusion.14, bf16[128,768]{1,0:T(8,128)(2,1)S(1)} %get-tuple-element.19), kind=kOutput, calls=%fused_computation.7 | convolution fusion | flops 303169536 | bytes 2949120 | tf_op jit(solution)/shard_map/dot_general | solution.py:33
  49.0 0.0 reduce-scatter.5.cloned.1.call-update
  49.0 0.0 reduce-scatter.3.cloned.1.call-start
  49.0 3.5 %convolution_convert_fusion = bf16[1536,1536]{1,0:T(8,128)(2,1)} fusion(bf16[128,1536]{1,0:T(8,128)(2,1)S(1)} %bitcast.61, bf16[128,768]{1,0:T(8,128)(2,1)S(1)} %get-tuple-element.18, bf16[128,768]{1,0:T(8,128)(2,1)S(1)} %get-tuple-element.17), kind=kOutput, calls=%fused_computation.2 | convolution fusion | flops 607125504 | bytes 5505024 | tf_op jit(solution)/shard_map/dot_general | solution.py:33
  52.6 0.0 copy-start.3
  52.6 0.0 reduce-scatter.3.cloned.1.call-update
  52.6 0.0 copy-start.4
  52.6 0.0 copy-start.5
  52.6 0.9 copy-done.3
  53.5 0.6 fusion.11
  54.1 0.7 convert_element_type.85
  54.8 3.3 %all-to-all-start.4 = ((bf16[8,1,16]{2,1,0:T(2,128)(2,1)}), bf16[8,1,16]{2,1,0:T(2,128)(2,1)S(1)}, u32[]{:S(2)}, u32[]{:S(2)}) async-start(bf16[8,1,16]{2,1,0:T(2,128)(2,1)} %convert_element_type.85), calls=%async_computation.4 | async-start | bytes 8192 | tf_op jit(solution)/shard_map/all_to_all | solution.py:67
  58.1 4.7 %fusion.4 = bf16[128,1536]{1,0:T(8,128)(2,1)} fusion(bf16[1,1536,1536]{2,1,0:T(8,128)(2,1)} %param.14, bf16[128,768]{1,0:T(8,128)(2,1)S(1)} %get-tuple-element.18, bf16[128,768]{1,0:T(8,128)(2,1)S(1)} %get-tuple-element.17), kind=kOutput, calls=%fused_computation.9 | convolution fusion | flops 604962816 | bytes 5505024 | tf_op jit(solution)/shard_map/dot_general | solution.py:26
  62.8 0.0 all-to-all-done.4
  62.8 4.1 %all-to-all-start.3 = ((bf16[8,16,1536]{2,1,0:T(8,128)(2,1)}), bf16[8,16,1536]{2,1,0:T(8,128)(2,1)S(1)}, u32[]{:S(2)}, u32[]{:S(2)}) async-start(bf16[8,16,1536]{2,1,0:T(8,128)(2,1)} %bitcast.12), calls=%async_computation.3 | async-start | bytes 786432 | tf_op jit(solution)/shard_map/all_to_all | solution.py:64
  66.9 0.0 copy-done.4
  67.0 0.1 eq.10
  67.0 0.0 copy-done.5
  67.0 0.7 fusion.18
  67.7 7.6 %all-to-all-done.3 = bf16[8,16,1536]{2,1,0:T(8,128)(2,1)S(1)} async-done(((bf16[8,16,1536]{2,1,0:T(8,128)(2,1)}), bf16[8,16,1536]{2,1,0:T(8,128)(2,1)S(1)}, u32[]{:S(2)}, u32[]{:S(2)}) %all-to-all-start.3) | async-done | bytes 393248 | tf_op jit(solution)/shard_map/all_to_all | solution.py:64
  75.3 1.0 fusion.10
  76.3 20.3 %reduce-scatter.5.cloned.1.call-done = bf16[384,768]{1,0:T(8,128)(2,1)} async-done(((bf16[1536,768]{1,0:T(8,128)(2,1)}), bf16[384,768]{1,0:T(8,128)(2,1)}) %reduce-scatter.5.cloned.1.call-update) | async-done | bytes 589840 | tf_op jit(solution)/shard_map/reduce_scatter | solution.py:80
  96.6 2.1 %copy.19 = bf16[1,768,384]{2,1,0:T(8,128)(2,1)} copy(bf16[1,768,384]{1,2,0:T(8,128)(2,1)} %bitcast.65) | data formatting | bytes 1179648
  98.7 85.5 %reduce-scatter.3.cloned.1.call-done = bf16[384,1536]{1,0:T(8,128)(2,1)} async-done(((bf16[1536,1536]{1,0:T(8,128)(2,1)}), bf16[384,1536]{1,0:T(8,128)(2,1)}) %reduce-scatter.3.cloned.1.call-update) | async-done | bytes 1179664 | tf_op jit(solution)/shard_map/reduce_scatter | solution.py:77
  (2 shorter events, 0.0 us)
Async XLA Ops:
  7.2 36.8 %copy-start = (bf16[1,768,1536]{2,1,0:T(8,128)(2,1)S(1)}, bf16[1,768,1536]{2,1,0:T(8,128)(2,1)}, u32[]{:S(2)}) copy-start(bf16[1,768,1536]{2,1,0:T(8,128)(2,1)} %param.15) | copy-start | bytes 7077892
  7.2 10.5 %copy-start.1 = (bf16[1,128,1536]{2,1,0:T(8,128)(2,1)S(1)}, bf16[1,128,1536]{2,1,0:T(8,128)(2,1)}, u32[]{:S(2)}) copy-start(bf16[1,128,1536]{2,1,0:T(8,128)(2,1)} %param.10) | copy-start | bytes 1179652
  8.7 10.9 %all-to-all-start = ((bf16[8,1,16]{2,1,0:T(2,128)(2,1)}), bf16[8,1,16]{2,1,0:T(2,128)(2,1)S(1)}, u32[]{:S(2)}, u32[]{:S(2)}) async-start(bf16[8,1,16]{2,1,0:T(2,128)(2,1)} %copy.16), calls=%async_computation | async-start | bytes 8192 | tf_op jit(solution)/shard_map/all_to_all | solution.py:53
  19.6 12.5 %all-to-all-start.2 = ((bf16[8,16,1536]{2,1,0:T(8,128)(2,1)}), bf16[8,16,1536]{2,1,0:T(8,128)(2,1)S(1)}, u32[]{:S(2)}, u32[]{:S(2)}) async-start(bf16[8,16,1536]{2,1,0:T(8,128)(2,1)} %get-tuple-element.22), calls=%async_computation.2 | async-start | bytes 786432 | tf_op jit(solution)/shard_map/all_to_all | solution.py:51
  32.1 11.7 %all-to-all-start.1 = ((bf16[8,16,1536]{2,1,0:T(8,128)(2,1)}), bf16[8,16,1536]{2,1,0:T(8,128)(2,1)S(1)}, u32[]{:S(2)}, u32[]{:S(2)}) async-start(bf16[8,16,1536]{2,1,0:T(8,128)(2,1)} %get-tuple-element.23), calls=%async_computation.1 | async-start | bytes 786432 | tf_op jit(solution)/shard_map/all_to_all | solution.py:52
  35.6 61.0 %reduce-scatter.5.cloned.1.call-start = ((), (), s32[]{:S(2)}) async-start(), calls=%async_computation.8 | async-start | bytes 2949120 | tf_op jit(solution)/shard_map/reduce_scatter | solution.py:80
  46.1 0.7 copy-start.2
  49.0 135.2 %reduce-scatter.3.cloned.1.call-start = ((), (), s32[]{:S(2)}) async-start(), calls=%async_computation.7 | async-start | bytes 5898240 | tf_op jit(solution)/shard_map/reduce_scatter | solution.py:77
  52.6 0.9 copy-start.3
  52.6 14.3 %copy-start.4 = (s32[1,1,8,16]{3,2,1,0:T(8,128)S(1)}, s32[1,1,8,16]{3,2,1,0:T(8,128)}, u32[]{:S(2)}) copy-start(s32[1,1,8,16]{3,2,1,0:T(8,128)} %param.11) | copy-start | bytes 1540
  52.6 14.4 %copy-start.5 = (s32[1,1,8]{2,1,0:T(1,128)S(1)}, s32[1,1,8]{2,1,0:T(1,128)}, u32[]{:S(2)}) copy-start(s32[1,1,8]{2,1,0:T(1,128)} %param.12) | copy-start | bytes 100
  54.8 8.0 %all-to-all-start.4 = ((bf16[8,1,16]{2,1,0:T(2,128)(2,1)}), bf16[8,1,16]{2,1,0:T(2,128)(2,1)S(1)}, u32[]{:S(2)}, u32[]{:S(2)}) async-start(bf16[8,1,16]{2,1,0:T(2,128)(2,1)} %convert_element_type.85), calls=%async_computation.4 | async-start | bytes 8192 | tf_op jit(solution)/shard_map/all_to_all | solution.py:67
  62.8 12.5 %all-to-all-start.3 = ((bf16[8,16,1536]{2,1,0:T(8,128)(2,1)}), bf16[8,16,1536]{2,1,0:T(8,128)(2,1)S(1)}, u32[]{:S(2)}, u32[]{:S(2)}) async-start(bf16[8,16,1536]{2,1,0:T(8,128)(2,1)} %bitcast.12), calls=%async_computation.3 | async-start | bytes 786432 | tf_op jit(solution)/shard_map/all_to_all | solution.py:64
Sparse Core Ops, SparseCore 0:
  49.1 47.4 reduce-scatter.4
  99.4 84.7 reduce-scatter.2
where the time goes:
time: 192 us; the launch traced here: 191 us
  waiting for transfers between devices  126 us (66%)
  starting transfers between devices  20.3 us (11%)
  matrix products  18.1 us (9%)
  between operations  14.2 us (7%)
  local copies, waits for them, and re-layouts  8.28 us (4%)
  other arithmetic  4.24 us (2%)
    reduce_scatter x1, waiting for transfers between devices, on_device(): lax.psum_scatter(column_term(x_rows, in_rows).astype(jnp.bfloat16), 'dp',...  85.5 us
    reduce_scatter x1, waiting for transfers between devices, on_device(): lax.psum_scatter(column_term(scaled, hidden).astype(jnp.bfloat16), 'dp',...  20.3 us
    all_to_all x1, waiting for transfers between devices, on_device(): lax.all_to_all(x_sent, 'expert', split_axis=0, concat_axis=0, tiled=True)  8.26 us
    all_to_all x1, waiting for transfers between devices, on_device(): lax.all_to_all(slot_grad.reshape(peers, most, width), 'expert', split_axi...  7.6 us
    dot_general x2, matrix products, column_term(): lax.dot_general(left, right, (((0,), (0,)), ((), ())), preferred_element_...  5.79 us
    all_to_all x1, starting transfers between devices, on_device(): lax.all_to_all(gate_rows, 'expert', split_axis=0, concat_axis=0, tiled=True)  5.17 us
    dot_general x1, matrix products, expert_pass(): lax.dot_general(in_rows, w_first, (((1,), (1,)), ((), ())), preferred_ele...  4.71 us
    all_to_all x1, waiting for transfers between devices, on_device(): lax.all_to_all(cot_sent, 'expert', split_axis=0, concat_axis=0, tiled=True)  4.22 us
  transfers between devices with their start and end apart: 7, of which 5 were waited for; matrix products, arithmetic and copies ran while one was open for 12% of the time, Pallas kernels for 0%

commit v1 on v0

v1 whole, which is shorter than its diff:
```python
import functools

import jax
import jax.numpy as jnp
from jax import lax
from jax.experimental import pallas as pl
from jax.experimental.pallas import tpu as pltpu
from jax.sharding import PartitionSpec as P

F32 = jnp.float32
BF16 = jnp.bfloat16
USED = 64
LANES = 128

NEAR = ((0, 1), (1, 0), (2, 3), (3, 2))
MIDDLE = ((1, 2), (2, 1))
FAR = ((0, 2), (2, 0), (1, 3), (3, 1))
ONWARD = ((1, 0), (2, 3))


def dot_nn(left, right):
    return lax.dot_general(left, right, (((1,), (0,)), ((), ())), preferred_element_type=F32)


def dot_nt(left, right):
    return lax.dot_general(left, right, (((1,), (1,)), ((), ())), preferred_element_type=F32)


def dot_tn(left, right):
    return lax.dot_general(left, right, (((0,), (0,)), ((), ())), preferred_element_type=F32)


def iota(shape, dim):
    return lax.broadcasted_iota(jnp.int32, shape, dim)


def call(body, outs, args, flops, vmem=48):
    size = sum(a.size * a.dtype.itemsize for a in args) + sum(
        o.size * jnp.dtype(o.dtype).itemsize for o in outs
    )
    return pl.pallas_call(
        body,
        out_shape=tuple(outs),
        in_specs=[pl.BlockSpec(memory_space=pltpu.VMEM)] * len(args),
        out_specs=tuple(pl.BlockSpec(memory_space=pltpu.VMEM) for _ in outs),
        compiler_params=pltpu.CompilerParams(vmem_limit_bytes=vmem * 1024 * 1024),
        cost_estimate=pl.CostEstimate(flops=int(flops), bytes_accessed=int(size), transcendentals=0),
    )(*args)


def slot_maps(peers, most):
    slots = peers * most
    peer_hot = iota((slots, peers), 0) // most == iota((slots, peers), 1)
    k_hot = iota((slots, most), 0) % most == iota((slots, most), 1)
    return peer_hot, k_hot


def slot_column(values, peer_hot, k_hot):
    spread = dot_nn(peer_hot.astype(BF16), values)
    return jnp.sum(jnp.where(k_hot, spread, 0.0), axis=1, keepdims=True)


def token_hot(rows_ref, peer_hot, k_hot, tokens):
    column = slot_column(rows_ref[...].astype(F32).astype(BF16), peer_hot, k_hot)
    return iota((column.shape[0], tokens), 1) == column.astype(jnp.int32)


def used_column(counts_ref, peer_hot, most):
    slots = peer_hot.shape[0]
    count = jnp.sum(
        jnp.where(peer_hot, counts_ref[...].astype(F32), 0.0), axis=1, keepdims=True
    )
    return (iota((slots, 1), 0) % most).astype(F32) < count


def pick_tokens(rows_ref, counts_ref, tokens_ref, out_ref):
    peers, most = rows_ref.shape
    width = tokens_ref.shape[1]
    peer_hot, k_hot = slot_maps(peers, most)
    hot = token_hot(rows_ref, peer_hot, k_hot, tokens_ref.shape[0])
    used = used_column(counts_ref, peer_hot, most)
    out_ref[:, :width] = dot_nn(hot.astype(BF16), tokens_ref[...]).astype(BF16)
    out_ref[:, width:] = jnp.broadcast_to(
        jnp.where(used, 1.0, 0.0), (peers * most, LANES)
    ).astype(BF16)


def pick_scaled(rows_ref, counts_ref, gates_ref, cot_ref, out_ref):
    peers, most = rows_ref.shape
    peer_hot, k_hot = slot_maps(peers, most)
    hot = token_hot(rows_ref, peer_hot, k_hot, cot_ref.shape[0])
    used = used_column(counts_ref, peer_hot, most)
    gate = jnp.where(used, slot_column(gates_ref[...], peer_hot, k_hot), 0.0)
    out_ref[...] = (dot_nn(hot.astype(BF16), cot_ref[...]) * gate).astype(BF16)


def pack_tokens(arrived_ref, rows_ref, pack_ref):
    slots = arrived_ref.shape[0]
    width = rows_ref.shape[1]
    flags = arrived_ref[:, width:]
    before = (iota((slots, slots), 0) < iota((slots, slots), 1)).astype(BF16)
    same = (iota((slots, slots), 0) == iota((slots, slots), 1)).astype(BF16)
    place = dot_tn(flags, before)[:USED]
    used = dot_tn(flags, same)[:USED]
    row = iota((USED, slots), 0).astype(F32)
    pack = jnp.where(used > 0.5, jnp.where(place == row, 1.0, 0.0), 0.0).astype(BF16)
    pack_ref[...] = pack
    rows_ref[...] = dot_nn(pack, arrived_ref[:, :width]).astype(BF16)


def pack_scaled(arrived_ref, pack_ref, rows_ref):
    rows_ref[...] = dot_nn(pack_ref[...], arrived_ref[...]).astype(BF16)


def hidden_parts(x_rows, scaled, w_in, w_down):
    inner = w_down.shape[0]
    pre = dot_nn(x_rows, w_in)
    gate_pre = pre[:, :inner]
    up_pre = pre[:, inner:]
    squash = jax.nn.sigmoid(gate_pre)
    swished = gate_pre * squash
    hidden = (swished * up_pre).astype(BF16)
    hidden_grad = dot_nt(scaled, w_down)
    gate_grad = hidden_grad * up_pre * (squash * (1.0 + gate_pre * (1.0 - squash)))
    up_grad = hidden_grad * swished
    return hidden, hidden_grad, gate_grad.astype(BF16), up_grad.astype(BF16)


def own_rows(x_ref, scaled_ref, pack_ref, w_in_ref, w_down_ref, out_ref):
    inner = w_down_ref.shape[0]
    width = x_ref.shape[1]
    hidden, hidden_grad, gate_rows, up_rows = hidden_parts(
        x_ref[...], scaled_ref[...], w_in_ref[...], w_down_ref[...]
    )
    value = jnp.sum(hidden.astype(F32) * hidden_grad, axis=1, keepdims=True)
    high = value.astype(BF16).astype(F32)
    low = value - high
    lane = iota((x_ref.shape[0], LANES), 1)
    tail = jnp.where(lane == 0, high, jnp.where(lane == 1, low, 0.0)).astype(BF16)
    slot_grad = (
        dot_nt(gate_rows, w_in_ref[:, :inner]) + dot_nt(up_rows, w_in_ref[:, inner:])
    ).astype(BF16)
    pack = pack_ref[...]
    out_ref[:, :width] = dot_tn(pack, slot_grad).astype(BF16)
    out_ref[:, width:] = dot_tn(pack, tail).astype(BF16)


def combine_tokens(rows_ref, counts_ref, gates_ref, back_ref, token_ref, gate_ref):
    peers, most = rows_ref.shape
    tokens, width = token_ref.shape
    peer_hot, k_hot = slot_maps(peers, most)
    hot = token_hot(rows_ref, peer_hot, k_hot, tokens)
    used = used_column(counts_ref, peer_hot, most)
    token_ref[...] = dot_tn(hot.astype(BF16), back_ref[:, :width]).astype(BF16)
    tail = back_ref[:, width:].astype(F32)
    value = tail[:, 0:1] + tail[:, 1:2]
    gate = jnp.where(used, slot_column(gates_ref[...], peer_hot, k_hot), 1.0)
    value = jnp.where(used, value / gate, 0.0).astype(BF16).astype(F32)
    spread = jnp.where(k_hot, value, 0.0).astype(BF16)
    gate_ref[...] = dot_tn(peer_hot.astype(BF16), spread).astype(BF16)


def weight_grads(share, *refs):
    x_refs, s_refs = refs[:5], refs[5:10]
    index_ref, w_in_ref, w_down_ref, in_ref, down_ref, x_all, s_all = refs[10:]
    for held, blocks in ((x_all, x_refs), (s_all, s_refs)):
        for place in range(3):
            held[place * USED : (place + 1) * USED, :] = blocks[place][...]
        held[3 * USED :, :] = blocks[3][...] + blocks[4][...]
    inner = w_down_ref.shape[0]
    hidden, _, gate_rows, up_rows = hidden_parts(
        x_all[...], s_all[...], w_in_ref[...], w_down_ref[...]
    )
    start = pl.multiple_of(index_ref[0] * share, LANES)
    x_share = x_all[:, pl.ds(start, share)]
    s_share = s_all[:, pl.ds(start, share)]
    down_ref[...] = dot_tn(hidden, s_share).astype(BF16)
    in_ref[:, :inner] = dot_tn(x_share, gate_rows).astype(BF16)
    in_ref[:, inner:] = dot_tn(x_share, up_rows).astype(BF16)


def line_exchange(block):
    near = lax.ppermute(block, "dp", NEAR)
    far = lax.ppermute(block, "dp", FAR)
    middle = lax.ppermute(block, "dp", MIDDLE)
    onward = lax.ppermute(far, "dp", ONWARD)
    return block, near, far, middle, onward


def share_grads_on_line(x_rows, scaled, w_in, w_down, share):
    inner, width = w_down.shape
    x_blocks = line_exchange(x_rows)
    s_blocks = line_exchange(scaled)
    index = lax.axis_index("dp").astype(jnp.int32).reshape(1)
    args = (*x_blocks, *s_blocks, index, w_in, w_down)
    vmem = pl.BlockSpec(memory_space=pltpu.VMEM)
    rows = 4 * USED
    return pl.pallas_call(
        functools.partial(weight_grads, share),
        out_shape=(
            jax.ShapeDtypeStruct((share, 2 * inner), BF16),
            jax.ShapeDtypeStruct((inner, share), BF16),
        ),
        in_specs=[vmem] * 10 + [pl.BlockSpec(memory_space=pltpu.SMEM)] + [vmem] * 2,
        out_specs=(vmem, vmem),
        scratch_shapes=[pltpu.VMEM((rows, width), BF16)] * 2,
        compiler_params=pltpu.CompilerParams(vmem_limit_bytes=48 * 1024 * 1024),
        cost_estimate=pl.CostEstimate(
            flops=2 * rows * inner * (3 * width + 3 * share),
            bytes_accessed=2 * (3 * inner * width + 2 * rows * width + 3 * inner * share),
            transcendentals=rows * inner,
        ),
    )(*args)


def share_grads(x_rows, scaled, w_in, w_down, share):
    width = w_down.shape[1]
    x_all = lax.all_gather(x_rows, "dp", axis=0, tiled=True)
    s_all = lax.all_gather(scaled, "dp", axis=0, tiled=True)
    hidden, _, gate_rows, up_rows = hidden_parts(x_all, s_all, w_in, w_down)
    start = lax.axis_index("dp") * share
    x_share = lax.dynamic_slice_in_dim(x_all, start, share, axis=1)
    s_share = lax.dynamic_slice_in_dim(s_all, start, share, axis=1)
    in_grad = dot_tn(x_share, jnp.concatenate([gate_rows, up_rows], axis=1)).astype(BF16)
    return in_grad, dot_tn(hidden, s_share).astype(BF16)


def to_experts(block, peers):
    slots, width = block.shape
    moved = lax.all_to_all(
        block.reshape(peers, slots // peers, width), "expert", split_axis=0, concat_axis=0, tiled=True
    )
    return moved.reshape(slots, width)


def on_device(
    replicas, tokens, out_cotangent, chosen_rows, counts, gate_weights, in_weights, down_weights
):
    tokens, cot, w_in, w_down = tokens[0], out_cotangent[0], in_weights[0], down_weights[0]
    rows, count, gates = chosen_rows[0, 0], counts[0], gate_weights[0, 0]
    peers, most = rows.shape
    slots = peers * most
    n_tokens, width = tokens.shape
    inner = w_down.shape[0]
    shape = jax.ShapeDtypeStruct
    pick_flops = 2 * slots * n_tokens * width

    (x_sent,) = call(
        pick_tokens, [shape((slots, width + LANES), BF16)], (rows, count, tokens), pick_flops
    )
    x_arrived = to_experts(x_sent, peers)
    (s_sent,) = call(
        pick_scaled, [shape((slots, width), BF16)], (rows, count, gates, cot), pick_flops
    )
    s_arrived = to_experts(s_sent, peers)
    x_rows, pack = call(
        pack_tokens,
        [shape((USED, width), BF16), shape((USED, slots), BF16)],
        (x_arrived,),
        2 * USED * slots * width,
    )
    (scaled,) = call(
        pack_scaled, [shape((USED, width), BF16)], (s_arrived, pack), 2 * USED * slots * width
    )
    (sent_back,) = call(
        own_rows,
        [shape((slots, width + LANES), BF16)],
        (x_rows, scaled, pack, w_in, w_down),
        2 * USED * inner * width * 5,
    )
    back = to_experts(sent_back, peers)
    token_grad, gate_grad = call(
        combine_tokens,
        [shape((n_tokens, width), BF16), shape((peers, most), BF16)],
        (rows, count, gates, back),
        pick_flops,
    )
    share = width // replicas
    on_line = replicas == 4 and share % LANES == 0
    share_of = share_grads_on_line if on_line else share_grads
    in_grad, down_grad = share_of(x_rows, scaled, w_in, w_down, share)
    return (token_grad[None], gate_grad[None, None], in_grad[None], down_grad[None])


def solution(mesh):
    return jax.shard_map(
        functools.partial(on_device, mesh.shape["dp"]),
        mesh=mesh,
        in_specs=(
            P("dp", "expert", None),
            P("dp", "expert", None),
            P("dp", "expert", None, None),
            P("dp", "expert", None),
            P("dp", "expert", None, None),
            P("expert", None, None),
            P("expert", None, None),
        ),
        out_specs=(
            P("dp", "expert", None),
            P("dp", "expert", None, None),
            P("expert", "dp", None),
            P("expert", None, "dp"),
        ),
        check_vma=False,
    )
```

time: 192 us -> 79.1 us (0.41)
  waiting for transfers between devices: 126 us -> 29.1 us
  matrix products: 18.1 us -> 0 us
  Pallas kernels: 0 us -> 16.9 us
  between operations: 14.2 us -> 0.78 us
  starting transfers between devices: 20.3 us -> 25.4 us
  other arithmetic: 4.24 us -> 0 us
  local copies, waits for them, and re-layouts: 8.28 us -> 6.25 us
    reduce_scatter x2 -> x0, waiting for transfers between devices: 106 us -> none  [the longest x1 85.5 us: on_device(): lax.psum_scatter(column_term(x_rows, in_rows).astype(jnp.bfloat16), 'dp',...]
    dot_general x7 -> x0, matrix products: 18.1 us -> none  [the longest x2 5.79 us: column_term(): lax.dot_general(left, right, (((0,), (0,)), ((), ())), preferred_element_...]
    pallas_call x0 -> x7, Pallas kernels: none -> 16.9 us  [the longest x6 10.3 us: call(): pl.pallas_call(body, out_shape=tuple(outs), in_specs=[pl.BlockSpec(memory...]
    ppermute x0 -> x8, waiting for transfers between devices: none -> 16.7 us  [the longest x2 8.4 us: line_exchange(): onward = lax.ppermute(far, 'dp', ONWARD)]
    ppermute x0 -> x8, starting transfers between devices: none -> 13.3 us  [the longest x2 4.42 us: line_exchange(): far = lax.ppermute(block, 'dp', FAR)]
    all_to_all x5 -> x3, starting transfers between devices: 20.3 us -> 12.1 us  [to_experts(): lax.all_to_all(block.reshape(peers, slots // peers, width), 'expert', spl...]
    all_to_all x5 -> x3, waiting for transfers between devices: 20.1 us -> 12.4 us  [to_experts(): lax.all_to_all(block.reshape(peers, slots // peers, width), 'expert', spl...]
    select_n x4 -> x0, other arithmetic: 3.27 us -> none  [the longest x1 1.02 us: on_device(): x_sent = jnp.take(local_tokens, local_rows, axis=0)]
  transfers between devices with their start and end apart: 7 -> 11, of which waited for: 5 -> 7; matrix products, arithmetic and copies ran while one was open for 12% -> 0% of each run, Pallas kernels for 0% -> 11%
where the time goes in v1:
time: 79.1 us; the launch traced here: 78.5 us
  waiting for transfers between devices  29.1 us (37%)
  starting transfers between devices  25.4 us (32%)
  Pallas kernels  16.9 us (21%)
  local copies, waits for them, and re-layouts  6.25 us (8%)
    all_to_all x3, waiting for transfers between devices, to_experts(): lax.all_to_all(block.reshape(peers, slots // peers, width), 'expert', spl...  12.4 us
    all_to_all x3, starting transfers between devices, to_experts(): lax.all_to_all(block.reshape(peers, slots // peers, width), 'expert', spl...  12.1 us
    pallas_call x6, Pallas kernels, call(): pl.pallas_call(body, out_shape=tuple(outs), in_specs=[pl.BlockSpec(memory...  10.3 us
    ppermute x2, waiting for transfers between devices, line_exchange(): onward = lax.ppermute(far, 'dp', ONWARD)  8.4 us
    pallas_call x1, Pallas kernels, share_grads_on_line(): pl.pallas_call(functools.partial(weight_grads, share), out_shape=(jax.Sha...  6.62 us
    unnamed x24, local copies, waits for them, and re-layouts  6.25 us
    ppermute x2, waiting for transfers between devices, line_exchange(): far = lax.ppermute(block, 'dp', FAR)  4.69 us
    ppermute x2, starting transfers between devices, line_exchange(): far = lax.ppermute(block, 'dp', FAR)  4.42 us
  transfers between devices with their start and end apart: 11, of which 7 were waited for; matrix products, arithmetic and copies ran while one was open for 0% of the time, Pallas kernels for 11%

profile of v1, /device:TPU:0, one launch (start us, length us, event | category | flops | bytes accessed | tf_op | source)
XLA Modules:
  0.0 78.5 jit_solution(10065456839560103331)
XLA Ops:
  0.6 0.0 copy-start
  0.6 0.0 copy-start.2
  0.7 1.1 %copy-done.2 = bf16[1,128,1536]{2,1,0:T(8,128)(2,1)S(1)} copy-done((bf16[1,128,1536]{2,1,0:T(8,128)(2,1)S(1)}, bf16[1,128,1536]{2,1,0:T(8,128)(2,1)}, u32[]{:S(2)}) %copy-start.2) | copy-done | bytes 393240
  1.8 0.0 copy-start.4
  1.8 0.7 copy-done.4
  2.5 0.0 copy-start.9
  2.5 0.7 copy-done.9
  3.1 1.2 %shard_map.102 = bf16[128,1664]{1,0:T(8,128)(2,1)} custom-call(s32[8,16]{1,0:T(8,128)S(1)} %bitcast.26, s32[1,8]{1,0:T(1,128)S(1)} %bitcast.31, bf16[128,1536]{1,0:T(8,128)(2,1)S(1)} %bitcast.24), custom_call_target="tpu_custom_call" | custom-call | flops 50331648 | bytes 819744 | tf_op jit(solution)/shard_map/pallas_call | solution.py:41
  4.3 5.2 %all-to-all-start = ((bf16[8,16,1664]{2,1,0:T(8,128)(2,1)}), bf16[8,16,1664]{2,1,0:T(8,128)(2,1)S(1)}, u32[]{:S(2)}, u32[]{:S(2)}) async-start(bf16[8,16,1664]{2,1,0:T(8,128)(2,1)} %bitcast.4), calls=%async_computation | async-start | bytes 851968 | tf_op jit(solution)/shard_map/all_to_all | solution.py:230
  9.5 0.0 copy-start.3
  9.5 1.0 %copy-done.3 = bf16[1,128,1536]{2,1,0:T(8,128)(2,1)S(1)} copy-done((bf16[1,128,1536]{2,1,0:T(8,128)(2,1)S(1)}, bf16[1,128,1536]{2,1,0:T(8,128)(2,1)}, u32[]{:S(2)}) %copy-start.3) | copy-done | bytes 393240
  10.5 0.0 copy-start.5
  10.5 0.7 copy-done.5
  11.2 0.0 copy-start.7
  11.2 0.7 copy-done.7
  11.9 0.0 copy-start.10
  11.9 0.7 copy-done.10
  12.5 0.4 shard_map.104
  13.0 0.0 copy-start.1
  13.0 0.7 copy-done.1
  13.7 4.5 %all-to-all-done = bf16[8,16,1664]{2,1,0:T(8,128)(2,1)S(1)} async-done(((bf16[8,16,1664]{2,1,0:T(8,128)(2,1)}), bf16[8,16,1664]{2,1,0:T(8,128)(2,1)S(1)}, u32[]{:S(2)}, u32[]{:S(2)}) %all-to-all-start) | async-done | bytes 426016 | tf_op jit(solution)/shard_map/all_to_all | solution.py:230
  18.2 3.5 %all-to-all-start.1 = ((bf16[8,16,1536]{2,1,0:T(8,128)(2,1)}), bf16[8,16,1536]{2,1,0:T(8,128)(2,1)S(1)}, u32[]{:S(2)}, u32[]{:S(2)}) async-start(bf16[8,16,1536]{2,1,0:T(8,128)(2,1)} %bitcast.23), calls=%async_computation.1 | async-start | bytes 786432 | tf_op jit(solution)/shard_map/all_to_all | solution.py:230
  21.6 0.4 shard_map.103
  22.0 7.9 %all-to-all-done.1 = bf16[8,16,1536]{2,1,0:T(8,128)(2,1)S(1)} async-done(((bf16[8,16,1536]{2,1,0:T(8,128)(2,1)}), bf16[8,16,1536]{2,1,0:T(8,128)(2,1)S(1)}, u32[]{:S(2)}, u32[]{:S(2)}) %all-to-all-start.1) | async-done | bytes 393248 | tf_op jit(solution)/shard_map/all_to_all | solution.py:230
  29.9 0.2 shard_map.105.scaled_ref.refs_5_
  30.1 0.7 collective-permute-start.6
  30.8 4.3 %collective-permute-start.5 = (bf16[64,1536]{1,0:T(8,128)(2,1)S(1)}, bf16[64,1536]{1,0:T(8,128)(2,1)}, u32[]{:S(2)}, u32[]{:S(2)}) collective-permute-start(bf16[64,1536]{1,0:T(8,128)(2,1)S(1)} %shard_map.105.scaled_ref.refs_5_), channel_id=1, source_target_pairs={{0,2},{2,0},{1,3},{3,1},{4,6},{6,4},{5,7},{7,5},{8,10},{10,8},{9,1... | collective-permute-start | bytes 589832 | tf_op jit(solution)/shard_map/ppermute | solution.py:184
  35.1 0.1 collective-permute-start.1
  35.2 0.0 copy-done
  35.2 0.0 copy-start.6
  35.2 0.0 copy-start.8
  35.2 0.0 copy-start.11
  35.2 6.8 %shard_map.106 = bf16[128,1664]{1,0:T(8,128)(2,1)} custom-call(bf16[64,1536]{1,0:T(8,128)(2,1)S(1)} %get-tuple-element.10.x_ref.refs_0_, bf16[64,1536]{1,0:T(8,128)(2,1)S(1)} %shard_map.105.scaled_ref.refs_5_, bf16[64,128]{1,0:T(8,128)(2,1)S(1)} %get-tuple-element.11.pack_ref, bf16[1536,1536]{1,0:T(8,128)(2,1)} %bitcast.34, bf16[768,1536]{1,0:T(8,128)(2,1)S(1)} %bitcast.18), custom_call_target="tpu_custom_call" | custom-call | flops 754974720 | bytes 7913472 | tf_op jit(solution)/shard_map/pallas_call | solution.py:41
  42.0 3.5 %all-to-all-start.2 = ((bf16[8,16,1664]{2,1,0:T(8,128)(2,1)}), bf16[8,16,1664]{2,1,0:T(8,128)(2,1)S(1)}, u32[]{:S(2)}, u32[]{:S(2)}) async-start(bf16[8,16,1664]{2,1,0:T(8,128)(2,1)} %bitcast.11), calls=%async_computation.2 | async-start | bytes 851968 | tf_op jit(solution)/shard_map/all_to_all | solution.py:230
  45.5 3.0 %collective-permute-start.4 = (bf16[64,1536]{1,0:T(8,128)(2,1)S(1)}, bf16[64,1536]{1,0:T(8,128)(2,1)}, u32[]{:S(2)}, u32[]{:S(2)}) collective-permute-start(bf16[64,1536]{1,0:T(8,128)(2,1)S(1)} %shard_map.105.scaled_ref.refs_5_), channel_id=1, source_target_pairs={{0,1},{1,0},{2,3},{3,2},{4,5},{5,4},{6,7},{7,6},{8,9},{9,8},{10,11... | collective-permute-start | bytes 589832 | tf_op jit(solution)/shard_map/ppermute | solution.py:183
  48.5 1.3 %collective-permute-start.2 = (bf16[64,1536]{1,0:T(8,128)(2,1)S(1)}, bf16[64,1536]{1,0:T(8,128)(2,1)}, u32[]{:S(2)}, u32[]{:S(2)}) collective-permute-start(bf16[64,1536]{1,0:T(8,128)(2,1)S(1)} %get-tuple-element.10.x_ref.refs_0_), channel_id=1, source_target_pairs={{1,2},{2,1},{5,6},{6,5},{9,10},{10,9},{13,14},{14,13},{17,18},{18,... | collective-permute-start | bytes 589832 | tf_op jit(solution)/shard_map/ppermute | solution.py:185
  49.8 0.0 collective-permute-done.6.refs_8_
  49.8 1.3 %collective-permute-start = (bf16[64,1536]{1,0:T(8,128)(2,1)S(1)}, bf16[64,1536]{1,0:T(8,128)(2,1)}, u32[]{:S(2)}, u32[]{:S(2)}) collective-permute-start(bf16[64,1536]{1,0:T(8,128)(2,1)S(1)} %get-tuple-element.10.x_ref.refs_0_), channel_id=1, source_target_pairs={{0,1},{1,0},{2,3},{3,2},{4,5},{5,4},{6,7},{7,6},{8,9},{9,8},{10,11... | collective-permute-start | bytes 589832 | tf_op jit(solution)/shard_map/ppermute | solution.py:183
  51.1 1.8 %collective-permute-done.5.refs_7_ = bf16[64,1536]{1,0:T(8,128)(2,1)} collective-permute-done((bf16[64,1536]{1,0:T(8,128)(2,1)S(1)}, bf16[64,1536]{1,0:T(8,128)(2,1)}, u32[]{:S(2)}, u32[]{:S(2)}) %collective-permute-start.5) | collective-permute-done | bytes 196640 | tf_op jit(solution)/shard_map/ppermute | solution.py:184
  53.0 1.3 %collective-permute-start.7 = (bf16[64,1536]{1,0:T(8,128)(2,1)}, bf16[64,1536]{1,0:T(8,128)(2,1)}, u32[]{:S(2)}, u32[]{:S(2)}) collective-permute-start(bf16[64,1536]{1,0:T(8,128)(2,1)} %collective-permute-done.5.refs_7_), channel_id=1, source_target_pairs={{1,0},{2,3},{5,4},{6,7},{9,8},{10,11},{13,12},{14,15},{17,16},{18,... | collective-permute-start | bytes 589832 | tf_op jit(solution)/shard_map/ppermute | solution.py:186
  54.3 2.9 %collective-permute-done.1.refs_2_ = bf16[64,1536]{1,0:T(8,128)(2,1)} collective-permute-done((bf16[64,1536]{1,0:T(8,128)(2,1)S(1)}, bf16[64,1536]{1,0:T(8,128)(2,1)}, u32[]{:S(2)}, u32[]{:S(2)}) %collective-permute-start.1) | collective-permute-done | bytes 196640 | tf_op jit(solution)/shard_map/ppermute | solution.py:184
  57.1 1.3 %collective-permute-start.3 = (bf16[64,1536]{1,0:T(8,128)(2,1)}, bf16[64,1536]{1,0:T(8,128)(2,1)}, u32[]{:S(2)}, u32[]{:S(2)}) collective-permute-start(bf16[64,1536]{1,0:T(8,128)(2,1)} %collective-permute-done.1.refs_2_), channel_id=1, source_target_pairs={{1,0},{2,3},{5,4},{6,7},{9,8},{10,11},{13,12},{14,15},{17,16},{18,... | collective-permute-start | bytes 589832 | tf_op jit(solution)/shard_map/ppermute | solution.py:186
  58.4 0.0 all-to-all-done.2
  58.4 0.0 copy-done.6
  58.4 0.0 copy-done.8
  58.4 0.0 copy-done.11
  58.4 1.4 %shard_map.107 = (bf16[128,1536]{1,0:T(8,128)(2,1)}, bf16[8,16]{1,0:T(8,128)(2,1)}) custom-call(s32[8,16]{1,0:T(8,128)S(1)} %bitcast.28, s32[1,8]{1,0:T(1,128)S(1)} %bitcast.33, bf16[8,16]{1,0:T(8,128)(2,1)S(1)} %bitcast.30, bf16[128,1664]{1,0:T(8,128)(2,1)S(1)} %bitcast.20), custom_call_target="tpu_custom_call" | custom-call | flops 50331648 | bytes 820256 | tf_op jit(solution)/shard_map/pallas_call | solution.py:41
  59.8 0.0 collective-permute-done.4.refs_6_
  59.8 0.0 collective-permute-done.2.refs_3_
  59.8 3.6 %collective-permute-done.refs_1_ = bf16[64,1536]{1,0:T(8,128)(2,1)} collective-permute-done((bf16[64,1536]{1,0:T(8,128)(2,1)S(1)}, bf16[64,1536]{1,0:T(8,128)(2,1)}, u32[]{:S(2)}, u32[]{:S(2)}) %collective-permute-start) | collective-permute-done | bytes 196640 | tf_op jit(solution)/shard_map/ppermute | solution.py:183
  63.4 4.2 %collective-permute-done.7.refs_9_ = bf16[64,1536]{1,0:T(8,128)(2,1)} collective-permute-done((bf16[64,1536]{1,0:T(8,128)(2,1)}, bf16[64,1536]{1,0:T(8,128)(2,1)}, u32[]{:S(2)}, u32[]{:S(2)}) %collective-permute-start.7) | collective-permute-done | bytes 196640 | tf_op jit(solution)/shard_map/ppermute | solution.py:186
  67.6 4.2 %collective-permute-done.3.refs_4_ = bf16[64,1536]{1,0:T(8,128)(2,1)} collective-permute-done((bf16[64,1536]{1,0:T(8,128)(2,1)}, bf16[64,1536]{1,0:T(8,128)(2,1)}, u32[]{:S(2)}, u32[]{:S(2)}) %collective-permute-start.3) | collective-permute-done | bytes 196640 | tf_op jit(solution)/shard_map/ppermute | solution.py:186
  71.8 6.6 %shard_map.108 = (bf16[384,1536]{1,0:T(8,128)(2,1)}, bf16[768,384]{1,0:T(8,128)(2,1)}) custom-call(bf16[64,1536]{1,0:T(8,128)(2,1)S(1)} %get-tuple-element.10.x_ref.refs_0_, bf16[64,1536]{1,0:T(8,128)(2,1)} %collective-permute-done.refs_1_, bf16[64,1536]{1,0:T(8,128)(2,1)} %collective-permute-done.1.refs_2_, ...), custom_call_target="tpu_custom_call" | custom-call | flops 2264924160 | bytes 10420224 | tf_op jit(solution)/shard_map/pallas_call | solution.py:198
Async XLA Ops:
  0.6 34.6 %copy-start = (bf16[1,768,1536]{2,1,0:T(8,128)(2,1)S(1)}, bf16[1,768,1536]{2,1,0:T(8,128)(2,1)}, u32[]{:S(2)}) copy-start(bf16[1,768,1536]{2,1,0:T(8,128)(2,1)} %param.13) | copy-start | bytes 7077892
  0.6 1.1 %copy-start.2 = (bf16[1,128,1536]{2,1,0:T(8,128)(2,1)S(1)}, bf16[1,128,1536]{2,1,0:T(8,128)(2,1)}, u32[]{:S(2)}) copy-start(bf16[1,128,1536]{2,1,0:T(8,128)(2,1)} %param.7) | copy-start | bytes 1179652
  1.8 0.7 copy-start.4
  2.5 0.7 copy-start.9
  4.3 13.9 %all-to-all-start = ((bf16[8,16,1664]{2,1,0:T(8,128)(2,1)}), bf16[8,16,1664]{2,1,0:T(8,128)(2,1)S(1)}, u32[]{:S(2)}, u32[]{:S(2)}) async-start(bf16[8,16,1664]{2,1,0:T(8,128)(2,1)} %bitcast.4), calls=%async_computation | async-start | bytes 851968 | tf_op jit(solution)/shard_map/all_to_all | solution.py:230
  9.5 1.0 %copy-start.3 = (bf16[1,128,1536]{2,1,0:T(8,128)(2,1)S(1)}, bf16[1,128,1536]{2,1,0:T(8,128)(2,1)}, u32[]{:S(2)}) copy-start(bf16[1,128,1536]{2,1,0:T(8,128)(2,1)} %param.8) | copy-start | bytes 1179652
  10.5 0.7 copy-start.5
  11.2 0.7 copy-start.7
  11.9 0.7 copy-start.10
  13.0 0.7 copy-start.1
  18.2 11.7 %all-to-all-start.1 = ((bf16[8,16,1536]{2,1,0:T(8,128)(2,1)}), bf16[8,16,1536]{2,1,0:T(8,128)(2,1)S(1)}, u32[]{:S(2)}, u32[]{:S(2)}) async-start(bf16[8,16,1536]{2,1,0:T(8,128)(2,1)} %bitcast.23), calls=%async_computation.1 | async-start | bytes 786432 | tf_op jit(solution)/shard_map/all_to_all | solution.py:230
  30.1 19.7 %collective-permute-start.6 = (bf16[64,1536]{1,0:T(8,128)(2,1)S(1)}, bf16[64,1536]{1,0:T(8,128)(2,1)S(1)}, u32[]{:S(2)}, u32[]{:S(2)}) collective-permute-start(bf16[64,1536]{1,0:T(8,128)(2,1)S(1)} %shard_map.105.scaled_ref.refs_5_), channel_id=1, source_target_pairs={{1,2},{2,1},{5,6},{6,5},{9,10},{10,9},{13,14},{14,13},{17,18},{18,... | collective-permute-start | bytes 589832 | tf_op jit(solution)/shard_map/ppermute | solution.py:185
  30.8 22.2 %collective-permute-start.5 = (bf16[64,1536]{1,0:T(8,128)(2,1)S(1)}, bf16[64,1536]{1,0:T(8,128)(2,1)}, u32[]{:S(2)}, u32[]{:S(2)}) collective-permute-start(bf16[64,1536]{1,0:T(8,128)(2,1)S(1)} %shard_map.105.scaled_ref.refs_5_), channel_id=1, source_target_pairs={{0,2},{2,0},{1,3},{3,1},{4,6},{6,4},{5,7},{7,5},{8,10},{10,8},{9,1... | collective-permute-start | bytes 589832 | tf_op jit(solution)/shard_map/ppermute | solution.py:184
  35.1 22.0 %collective-permute-start.1 = (bf16[64,1536]{1,0:T(8,128)(2,1)S(1)}, bf16[64,1536]{1,0:T(8,128)(2,1)}, u32[]{:S(2)}, u32[]{:S(2)}) collective-permute-start(bf16[64,1536]{1,0:T(8,128)(2,1)S(1)} %get-tuple-element.10.x_ref.refs_0_), channel_id=1, source_target_pairs={{0,2},{2,0},{1,3},{3,1},{4,6},{6,4},{5,7},{7,5},{8,10},{10,8},{9,1... | collective-permute-start | bytes 589832 | tf_op jit(solution)/shard_map/ppermute | solution.py:184
  35.2 23.2 %copy-start.6 = (s32[1,1,8,16]{3,2,1,0:T(8,128)S(1)}, s32[1,1,8,16]{3,2,1,0:T(8,128)}, u32[]{:S(2)}) copy-start(s32[1,1,8,16]{3,2,1,0:T(8,128)} %param.9) | copy-start | bytes 1540
  35.2 23.2 %copy-start.8 = (bf16[1,1,8,16]{3,2,1,0:T(8,128)(2,1)S(1)}, bf16[1,1,8,16]{3,2,1,0:T(8,128)(2,1)}, u32[]{:S(2)}) copy-start(bf16[1,1,8,16]{3,2,1,0:T(8,128)(2,1)} %param.11) | copy-start | bytes 772
  35.2 23.2 %copy-start.11 = (s32[1,1,8]{2,1,0:T(1,128)S(1)}, s32[1,1,8]{2,1,0:T(1,128)}, u32[]{:S(2)}) copy-start(s32[1,1,8]{2,1,0:T(1,128)} %param.10) | copy-start | bytes 100
  42.0 16.4 %all-to-all-start.2 = ((bf16[8,16,1664]{2,1,0:T(8,128)(2,1)}), bf16[8,16,1664]{2,1,0:T(8,128)(2,1)S(1)}, u32[]{:S(2)}, u32[]{:S(2)}) async-start(bf16[8,16,1664]{2,1,0:T(8,128)(2,1)} %bitcast.11), calls=%async_computation.2 | async-start | bytes 851968 | tf_op jit(solution)/shard_map/all_to_all | solution.py:230
  45.5 14.3 %collective-permute-start.4 = (bf16[64,1536]{1,0:T(8,128)(2,1)S(1)}, bf16[64,1536]{1,0:T(8,128)(2,1)}, u32[]{:S(2)}, u32[]{:S(2)}) collective-permute-start(bf16[64,1536]{1,0:T(8,128)(2,1)S(1)} %shard_map.105.scaled_ref.refs_5_), channel_id=1, source_target_pairs={{0,1},{1,0},{2,3},{3,2},{4,5},{5,4},{6,7},{7,6},{8,9},{9,8},{10,11... | collective-permute-start | bytes 589832 | tf_op jit(solution)/shard_map/ppermute | solution.py:183
  48.5 11.3 %collective-permute-start.2 = (bf16[64,1536]{1,0:T(8,128)(2,1)S(1)}, bf16[64,1536]{1,0:T(8,128)(2,1)}, u32[]{:S(2)}, u32[]{:S(2)}) collective-permute-start(bf16[64,1536]{1,0:T(8,128)(2,1)S(1)} %get-tuple-element.10.x_ref.refs_0_), channel_id=1, source_target_pairs={{1,2},{2,1},{5,6},{6,5},{9,10},{10,9},{13,14},{14,13},{17,18},{18,... | collective-permute-start | bytes 589832 | tf_op jit(solution)/shard_map/ppermute | solution.py:185
  49.8 13.6 %collective-permute-start = (bf16[64,1536]{1,0:T(8,128)(2,1)S(1)}, bf16[64,1536]{1,0:T(8,128)(2,1)}, u32[]{:S(2)}, u32[]{:S(2)}) collective-permute-start(bf16[64,1536]{1,0:T(8,128)(2,1)S(1)} %get-tuple-element.10.x_ref.refs_0_), channel_id=1, source_target_pairs={{0,1},{1,0},{2,3},{3,2},{4,5},{5,4},{6,7},{7,6},{8,9},{9,8},{10,11... | collective-permute-start | bytes 589832 | tf_op jit(solution)/shard_map/ppermute | solution.py:183
  53.0 14.7 %collective-permute-start.7 = (bf16[64,1536]{1,0:T(8,128)(2,1)}, bf16[64,1536]{1,0:T(8,128)(2,1)}, u32[]{:S(2)}, u32[]{:S(2)}) collective-permute-start(bf16[64,1536]{1,0:T(8,128)(2,1)} %collective-permute-done.5.refs_7_), channel_id=1, source_target_pairs={{1,0},{2,3},{5,4},{6,7},{9,8},{10,11},{13,12},{14,15},{17,16},{18,... | collective-permute-start | bytes 589832 | tf_op jit(solution)/shard_map/ppermute | solution.py:186
  57.1 14.7 %collective-permute-start.3 = (bf16[64,1536]{1,0:T(8,128)(2,1)}, bf16[64,1536]{1,0:T(8,128)(2,1)}, u32[]{:S(2)}, u32[]{:S(2)}) collective-permute-start(bf16[64,1536]{1,0:T(8,128)(2,1)} %collective-permute-done.1.refs_2_), channel_id=1, source_target_pairs={{1,0},{2,3},{5,4},{6,7},{9,8},{10,11},{13,12},{14,15},{17,16},{18,... | collective-permute-start | bytes 589832 | tf_op jit(solution)/shard_map/ppermute | solution.py:186

commit v2 on v1

v2 whole, which is shorter than its diff:
```python
import functools
import math

import jax
import jax.numpy as jnp
from jax import lax
from jax.experimental import pallas as pl
from jax.experimental.pallas import tpu as pltpu
from jax.sharding import PartitionSpec as P

F32 = jnp.float32
BF16 = jnp.bfloat16
USED = 64
LANES = 128

NEAR = ((0, 1), (1, 0), (2, 3), (3, 2))
MIDDLE = ((1, 2), (2, 1))
FAR = ((0, 2), (2, 0), (1, 3), (3, 1))
ONWARD = ((1, 0), (2, 3))
LOADS = ((0,), (1,), (2, 3), (3,))


def dot_nn(left, right):
    return lax.dot_general(left, right, (((1,), (0,)), ((), ())), preferred_element_type=F32)


def dot_nt(left, right):
    return lax.dot_general(left, right, (((1,), (1,)), ((), ())), preferred_element_type=F32)


def dot_tn(left, right):
    return lax.dot_general(left, right, (((0,), (0,)), ((), ())), preferred_element_type=F32)


def iota(shape, dim):
    return lax.broadcasted_iota(jnp.int32, shape, dim)


def call(body, outs, args, flops, in_specs=None, scratch=(), vmem=24, out_specs=None):
    size = sum(math.prod(a.shape) * a.dtype.itemsize for a in (*args, *outs))
    return pl.pallas_call(
        body,
        out_shape=tuple(outs),
        in_specs=in_specs or [pl.BlockSpec(memory_space=pltpu.VMEM)] * len(args),
        out_specs=tuple(out_specs or [pl.BlockSpec(memory_space=pltpu.VMEM) for _ in outs]),
        scratch_shapes=scratch,
        compiler_params=pltpu.CompilerParams(vmem_limit_bytes=vmem * 1024 * 1024),
        cost_estimate=pl.CostEstimate(flops=int(flops), bytes_accessed=int(size), transcendentals=0),
    )(*args)


def slot_maps(peers, most):
    slots = peers * most
    peer_hot = iota((slots, peers), 0) // most == iota((slots, peers), 1)
    k_hot = iota((slots, most), 0) % most == iota((slots, most), 1)
    return peer_hot, k_hot


def slot_column(values, peer_hot, k_hot):
    spread = dot_nn(peer_hot.astype(BF16), values)
    return jnp.sum(jnp.where(k_hot, spread, 0.0), axis=1, keepdims=True)


def token_hot(rows_ref, peer_hot, k_hot, tokens):
    column = slot_column(rows_ref[...].astype(F32).astype(BF16), peer_hot, k_hot)
    return iota((column.shape[0], tokens), 1) == column.astype(jnp.int32)


def used_column(counts, peer_hot, most):
    slots = peer_hot.shape[0]
    count = jnp.sum(jnp.where(peer_hot, counts.astype(F32), 0.0), axis=1, keepdims=True)
    return (iota((slots, 1), 0) % most).astype(F32) < count


def pick_rows(*refs):
    sources, out_ref, held, sems = refs[:5], refs[5], refs[6:11], refs[11]
    copies = [
        pltpu.make_async_copy(source, target, sems.at[place])
        for place, (source, target) in enumerate(zip(sources, held))
    ]
    for copy in copies:
        copy.start()
    rows_ref, counts_ref, gates_ref, tokens_ref, cot_ref = held
    peers, most = rows_ref.shape
    slots = peers * most
    width = tokens_ref.shape[1]
    peer_hot, k_hot = slot_maps(peers, most)
    for copy in copies[:3]:
        copy.wait()
    hot = token_hot(rows_ref, peer_hot, k_hot, tokens_ref.shape[0]).astype(BF16)
    used = used_column(counts_ref[...], peer_hot, most)
    gate = jnp.where(used, slot_column(gates_ref[...], peer_hot, k_hot), 0.0)
    out_ref[:, 2 * width :] = jnp.broadcast_to(jnp.where(used, 1.0, 0.0), (slots, LANES)).astype(BF16)
    copies[3].wait()
    out_ref[:, :width] = dot_nn(hot, tokens_ref[...]).astype(BF16)
    copies[4].wait()
    out_ref[:, width : 2 * width] = (dot_nn(hot, cot_ref[...]) * gate).astype(BF16)


def pack_matrix(flags):
    slots = flags.shape[0]
    before = (iota((slots, slots), 0) < iota((slots, slots), 1)).astype(BF16)
    same = (iota((slots, slots), 0) == iota((slots, slots), 1)).astype(BF16)
    place = dot_tn(flags, before)[:USED]
    used = dot_tn(flags, same)[:USED]
    row = iota((USED, slots), 0).astype(F32)
    return jnp.where(used > 0.5, jnp.where(place == row, 1.0, 0.0), 0.0).astype(BF16)


def pack_rows(arrived_ref, x_ref, pack_ref, x_keep_hbm, sem):
    width = x_ref.shape[1]
    pack = pack_matrix(arrived_ref[:, 2 * width :])
    pack_ref[...] = pack
    x_ref[...] = dot_nn(pack, arrived_ref[:, :width]).astype(BF16)
    keep = pltpu.make_async_copy(x_ref, x_keep_hbm, sem)
    keep.start()
    keep.wait()


def own_hidden_grad(share, index_ref, arrived_ref, pack_ref, w_down_ref, grad_ref, *refs):
    *load_refs, scaled_ref, own_ref, sem = refs
    inner, width = w_down_ref.shape
    scaled_ref[...] = dot_nn(pack_ref[...], arrived_ref[:, width : 2 * width]).astype(BF16)
    hidden_grad = dot_nt(scaled_ref[...], w_down_ref[...])
    grad_ref[...] = hidden_grad
    if not load_refs:
        return
    for load_ref, steps in zip((own_ref, *load_refs[1:]), LOADS):
        load_ref[:, :inner] = hidden_grad.astype(BF16)
        for place, step in enumerate(steps):
            start = pl.multiple_of((index_ref[0] ^ step) * share, LANES)
            load_ref[:, pl.ds(inner + place * share, share)] = scaled_ref[:, pl.ds(start, share)]
    keep = pltpu.make_async_copy(own_ref, load_refs[0], sem)
    keep.start()
    keep.wait()


def activations(pre, inner):
    gate_pre = pre[:, :inner]
    up_pre = pre[:, inner:]
    squash = jax.nn.sigmoid(gate_pre)
    swished = gate_pre * squash
    hidden = (swished * up_pre).astype(BF16)
    return hidden, up_pre * (squash * (1.0 + gate_pre * (1.0 - squash))), swished


def start_parts(source, target, sems, parts=4):
    depth = source.shape[0] // parts
    copies = []
    for part in range(parts):
        span = pl.ds(part * depth, depth)
        copies.append(pltpu.make_async_copy(source.at[span], target.at[span], sems.at[part]))
        copies[-1].start()
    return copies


def project(x, w_ref, copies):
    depth = w_ref.shape[0] // len(copies)
    total = None
    for part, copy in enumerate(copies):
        copy.wait()
        span = slice(part * depth, (part + 1) * depth)
        term = dot_nn(x[:, span], w_ref[span, :])
        total = term if total is None else total + term
    return total


def own_rows(x_ref, grad_ref, pack_ref, w_in_hbm, out_ref, w_in_ref, sems):
    inner = grad_ref.shape[1]
    width = w_in_ref.shape[0]
    copies = start_parts(w_in_hbm, w_in_ref, sems)
    hidden_grad = grad_ref[...]
    hidden, gate_factor, up_factor = activations(project(x_ref, w_in_ref, copies), inner)
    gate_rows = (hidden_grad * gate_factor).astype(BF16)
    up_rows = (hidden_grad * up_factor).astype(BF16)
    value = jnp.sum(hidden.astype(F32) * hidden_grad, axis=1, keepdims=True)
    high = value.astype(BF16).astype(F32)
    low = value - high
    lane = iota((x_ref.shape[0], LANES), 1)
    tail = jnp.where(lane == 0, high, jnp.where(lane == 1, low, 0.0)).astype(BF16)
    slot_grad = (
        dot_nt(gate_rows, w_in_ref[:, :inner]) + dot_nt(up_rows, w_in_ref[:, inner:])
    ).astype(BF16)
    pack = pack_ref[...]
    out_ref[:, :width] = dot_tn(pack, slot_grad).astype(BF16)
    out_ref[:, width:] = dot_tn(pack, tail).astype(BF16)


def combine_tokens(rows_ref, counts_ref, gates_ref, back_ref, token_ref, gate_ref):
    peers, most = rows_ref.shape
    tokens, width = token_ref.shape
    peer_hot, k_hot = slot_maps(peers, most)
    hot = token_hot(rows_ref, peer_hot, k_hot, tokens)
    used = used_column(counts_ref[...], peer_hot, most)
    token_ref[...] = dot_tn(hot.astype(BF16), back_ref[:, :width]).astype(BF16)
    value = back_ref[:, width : width + 1].astype(F32) + back_ref[:, width + 1 : width + 2].astype(F32)
    gate = jnp.where(used, slot_column(gates_ref[...], peer_hot, k_hot), 1.0)
    value = jnp.where(used, value / gate, 0.0).astype(BF16).astype(F32)
    spread = jnp.where(k_hot, value, 0.0).astype(BF16)
    gate_ref[...] = dot_tn(peer_hot.astype(BF16), spread).astype(BF16)


def near_rows(share, *refs):
    x_refs, load_refs, index_ref, w_in_ref = refs[:3], refs[3:6], refs[6], refs[7]
    w_in_held, x_share_ref, s_share_ref, hidden_ref, in_rows_ref, held, sems = refs[8:]
    copies = start_parts(w_in_ref, w_in_held, sems)
    inner = hidden_ref.shape[1]
    for place, ref in enumerate(x_refs):
        held[place * USED : (place + 1) * USED, :] = ref[...]
    x_share_ref[...] = held[:, pl.ds(pl.multiple_of(index_ref[0] * share, LANES), share)]
    hidden, gate_factor, up_factor = activations(project(held, w_in_held, copies), inner)
    hidden_ref[...] = hidden
    for place, ref in enumerate(load_refs):
        rows = slice(place * USED, (place + 1) * USED)
        grad = ref[:, :inner].astype(F32)
        in_rows_ref[rows, :inner] = (grad * gate_factor[rows]).astype(BF16)
        in_rows_ref[rows, inner:] = (grad * up_factor[rows]).astype(BF16)
        s_share_ref[rows, :] = ref[:, inner : inner + share]


def third_rows(
    share, middle_ref, onward_ref, index_ref, w_in_ref, x_share_ref, hidden_ref, gate_factor_ref, up_factor_ref, held
):
    held[...] = middle_ref[...] + onward_ref[...]
    x_share_ref[...] = held[:, pl.ds(pl.multiple_of(index_ref[0] * share, LANES), share)]
    hidden, gate_factor, up_factor = activations(dot_nn(held[...], w_in_ref[...]), hidden_ref.shape[1])
    hidden_ref[...] = hidden
    gate_factor_ref[...] = gate_factor
    up_factor_ref[...] = up_factor


def grads(middle_ref, onward_ref, *refs):
    first, third = refs[:4], refs[4:8]
    in_ref, down_ref, x_share, s_share, hidden, in_rows = refs[8:]
    inner, most, share = hidden.shape[1], 3 * USED, x_share.shape[1]
    for whole, part in zip((x_share, s_share, hidden, in_rows), first):
        whole[:most, :] = part[...]
    third_x_ref, third_hidden_ref, gate_factor_ref, up_factor_ref = third
    x_share[most:, :] = third_x_ref[...]
    hidden[most:, :] = third_hidden_ref[...]
    s_share[most:, :] = middle_ref[:, inner:] + onward_ref[:, inner + share :]
    grad = (middle_ref[:, :inner] + onward_ref[:, :inner]).astype(F32)
    in_rows[most:, :inner] = (grad * gate_factor_ref[...]).astype(BF16)
    in_rows[most:, inner:] = (grad * up_factor_ref[...]).astype(BF16)
    down_ref[...] = dot_tn(hidden[...], s_share[...]).astype(BF16)
    in_ref[...] = dot_tn(x_share[...], in_rows[...]).astype(BF16)


def to_experts(block, peers):
    slots, width = block.shape
    moved = lax.all_to_all(
        block.reshape(peers, slots // peers, width), "expert", split_axis=0, concat_axis=0, tiled=True
    )
    return moved.reshape(slots, width)


def on_device(
    replicas, tokens, out_cotangent, chosen_rows, counts, gate_weights, in_weights, down_weights
):
    tokens, cot, w_in, w_down = tokens[0], out_cotangent[0], in_weights[0], down_weights[0]
    rows, count, gates = chosen_rows[0, 0], counts[0], gate_weights[0, 0]
    peers, most = rows.shape
    slots = peers * most
    n_tokens, width = tokens.shape
    inner = w_down.shape[0]
    share = width // replicas
    on_line = replicas == 4 and share % LANES == 0
    index = lax.axis_index("dp").astype(jnp.int32).reshape(1)
    shape = jax.ShapeDtypeStruct
    vmem = pl.BlockSpec(memory_space=pltpu.VMEM)
    smem = pl.BlockSpec(memory_space=pltpu.SMEM)
    hbm = pl.BlockSpec(memory_space=pltpu.HBM)

    w_in_far = pltpu.with_memory_space_constraint(w_in, pltpu.HBM)
    picked = (rows, count, gates, tokens, cot)
    (sent,) = call(
        pick_rows,
        [shape((slots, 2 * width + LANES), BF16)],
        picked,
        4 * slots * n_tokens * width,
        [hbm] * 5,
        [pltpu.VMEM(a.shape, a.dtype) for a in picked] + [pltpu.SemaphoreType.DMA((5,))],
        56,
    )
    arrived = to_experts(sent, peers)
    x_rows, pack, x_keep = call(
        pack_rows,
        [shape((USED, width), BF16), shape((USED, slots), BF16), pltpu.HBM((USED, width), BF16)],
        (arrived,),
        2 * USED * slots * width,
        None,
        [pltpu.SemaphoreType.DMA],
        6,
        [vmem, vmem, hbm],
    )
    sizes = [inner + len(steps) * share for steps in LOADS]
    hidden_grad, *loads = call(
        functools.partial(own_hidden_grad, share),
        [shape((USED, inner), F32)]
        + [pltpu.HBM((USED, sizes[0]), BF16)] * on_line
        + [shape((USED, size), BF16) for size in sizes[1:]] * on_line,
        (index, arrived, pack, w_down),
        2 * USED * width * (slots + inner),
        [smem, vmem, vmem, vmem],
        [pltpu.VMEM((USED, width), BF16), pltpu.VMEM((USED, sizes[0]), BF16), pltpu.SemaphoreType.DMA],
        8,
        [vmem] + ([hbm] + [vmem] * 3) * on_line,
    )
    if on_line:
        own, near_load, far_load, middle_load = loads
        x_far = lax.ppermute(x_rows, "dp", FAR)
        x_near = lax.ppermute(x_rows, "dp", NEAR)
        far = lax.ppermute(far_load, "dp", FAR)
        near = lax.ppermute(near_load, "dp", NEAR)
        x_near, pack = lax.optimization_barrier((x_near, pack))
    parts = 4
    (sent_back,) = call(
        own_rows,
        [shape((slots, width + LANES), BF16)],
        (x_rows, hidden_grad, pack, w_in_far),
        2 * USED * inner * width * 4,
        [vmem] * 3 + [hbm],
        [pltpu.VMEM(w_in.shape, BF16), pltpu.SemaphoreType.DMA((parts,))],
        16,
    )
    back = to_experts(sent_back, peers)
    if on_line:
        x_far, sent_back = lax.optimization_barrier((x_far, sent_back))
        x_middle = lax.ppermute(x_rows, "dp", MIDDLE)
        middle = lax.ppermute(middle_load, "dp", MIDDLE)
        x_onward = lax.ppermute(x_far, "dp", ONWARD)
        onward = lax.ppermute(far, "dp", ONWARD)
    token_grad, gate_grad = call(
        combine_tokens,
        [shape((n_tokens, width), BF16), shape((peers, most), BF16)],
        (rows, count, gates, back),
        2 * slots * n_tokens * width,
        vmem=8,
    )
    if on_line:
        everyone, first = replicas * USED, 3 * USED

        w_in_held, *first_parts = call(
            functools.partial(near_rows, share),
            [
                shape(w_in.shape, BF16),
                shape((first, share), BF16),
                shape((first, share), BF16),
                shape((first, inner), BF16),
                shape((first, 2 * inner), BF16),
            ],
            (x_keep, x_near, x_far, own, near, far, index, w_in_far),
            4 * first * inner * width,
            [vmem] * 6 + [smem, hbm],
            [pltpu.VMEM((first, width), BF16), pltpu.SemaphoreType.DMA((parts,))],
            16,
        )
        third_parts = call(
            functools.partial(third_rows, share),
            [
                shape((USED, share), BF16),
                shape((USED, inner), BF16),
                shape((USED, inner), F32),
                shape((USED, inner), F32),
            ],
            (x_middle, x_onward, index, w_in_held),
            4 * USED * inner * width,
            [vmem] * 2 + [smem, vmem],
            [pltpu.VMEM((USED, width), BF16)],
            16,
        )
        middle, token_grad = lax.optimization_barrier((middle, token_grad))
        in_grad, down_grad = call(
            grads,
            [shape((share, 2 * inner), BF16), shape((inner, share), BF16)],
            (middle, onward, *first_parts, *third_parts),
            6 * everyone * inner * share,
            None,
            [
                pltpu.VMEM((everyone, share), BF16),
                pltpu.VMEM((everyone, share), BF16),
                pltpu.VMEM((everyone, inner), BF16),
                pltpu.VMEM((everyone, 2 * inner), BF16),
            ],
            16,
        )
    else:
        x_all = lax.all_gather(x_rows, "dp", axis=0, tiled=True)
        hidden, gate_factor, up_factor = activations(dot_nn(x_all, w_in), inner)
        hidden_grad = lax.all_gather(hidden_grad, "dp", axis=0, tiled=True)
        in_rows = jnp.concatenate([hidden_grad * gate_factor, hidden_grad * up_factor], axis=1)
        x_share = lax.dynamic_slice_in_dim(x_all, index[0] * share, share, axis=1)
        scaled = dot_nn(pack, arrived[:, width : 2 * width]).astype(BF16)
        s_all = lax.all_gather(scaled, "dp", axis=0, tiled=True)
        s_share = lax.dynamic_slice_in_dim(s_all, index[0] * share, share, axis=1)
        in_grad = dot_tn(x_share, in_rows.astype(BF16)).astype(BF16)
        down_grad = dot_tn(hidden, s_share).astype(BF16)
    return (token_grad[None], gate_grad[None, None], in_grad[None], down_grad[None])


def solution(mesh):
    return jax.shard_map(
        functools.partial(on_device, mesh.shape["dp"]),
        mesh=mesh,
        in_specs=(
            P("dp", "expert", None),
            P("dp", "expert", None),
            P("dp", "expert", None, None),
            P("dp", "expert", None),
            P("dp", "expert", None, None),
            P("expert", None, None),
            P("expert", None, None),
        ),
        out_specs=(
            P("dp", "expert", None),
            P("dp", "expert", None, None),
            P("expert", "dp", None),
            P("expert", None, "dp"),
        ),
        check_vma=False,
    )
```

time: 79.1 us -> 60.2 us (0.76)
  waiting for transfers between devices: 29.1 us -> 8.91 us
  blocking collectives: 0 us -> 18.1 us
  starting transfers between devices: 25.4 us -> 12 us
  local copies, waits for them, and re-layouts: 6.25 us -> 0.68 us
  Pallas kernels: 16.9 us -> 19.3 us
    all_to_all x0 -> x1, blocking collectives: none -> 18.1 us  [to_experts(): lax.all_to_all(block.reshape(peers, slots // peers, width), 'expert', spl...]
    all_to_all x3 -> x1, waiting for transfers between devices: 12.4 us -> 0.01 us  [to_experts(): lax.all_to_all(block.reshape(peers, slots // peers, width), 'expert', spl...]
    all_to_all x3 -> x1, starting transfers between devices: 12.1 us -> 3.48 us  [to_experts(): lax.all_to_all(block.reshape(peers, slots // peers, width), 'expert', spl...]
    ppermute x8, waiting for transfers between devices: 16.7 us -> 8.91 us  [the longest x1 3.55 us: on_device(): x_near = lax.ppermute(x_rows, 'dp', NEAR)]
    unnamed x24 -> x16, local copies, waits for them, and re-layouts: 6.25 us -> 0.68 us
    ppermute x8, starting transfers between devices: 13.3 us -> 8.55 us  [the longest x1 2.59 us: on_device(): x_far = lax.ppermute(x_rows, 'dp', FAR)]
    pallas_call x7 -> x8, Pallas kernels: 16.9 us -> 19.3 us  [call(): pl.pallas_call(body, out_shape=tuple(outs), in_specs=in_specs or [pl.Bloc...]
  transfers between devices with their start and end apart: 11 -> 9, of which waited for: 7 -> 4; matrix products, arithmetic and copies ran while one was open for 0% -> 0% of each run, Pallas kernels for 11% -> 23%
where the time goes in v2:
time: 60.2 us; the launch traced here: 59.9 us
  Pallas kernels  19.3 us (32%)
  blocking collectives  18.1 us (30%)
  starting transfers between devices  12 us (20%)
  waiting for transfers between devices  8.91 us (15%)
  between operations  0.82 us (1%)
  local copies, waits for them, and re-layouts  0.68 us (1%)
    pallas_call x8, Pallas kernels, call(): pl.pallas_call(body, out_shape=tuple(outs), in_specs=in_specs or [pl.Bloc...  19.3 us
    all_to_all x1, blocking collectives, to_experts(): lax.all_to_all(block.reshape(peers, slots // peers, width), 'expert', spl...  18.1 us
    ppermute x1, waiting for transfers between devices, on_device(): x_near = lax.ppermute(x_rows, 'dp', NEAR)  3.55 us
    all_to_all x1, starting transfers between devices, to_experts(): lax.all_to_all(block.reshape(peers, slots // peers, width), 'expert', spl...  3.48 us
    ppermute x1, starting transfers between devices, on_device(): x_far = lax.ppermute(x_rows, 'dp', FAR)  2.59 us
    ppermute x1, waiting for transfers between devices, on_device(): x_onward = lax.ppermute(x_far, 'dp', ONWARD)  2.29 us
    ppermute x1, waiting for transfers between devices, on_device(): near = lax.ppermute(near_load, 'dp', NEAR)  2.08 us
    ppermute x1, starting transfers between devices, on_device(): x_near = lax.ppermute(x_rows, 'dp', NEAR)  1.64 us
  transfers between devices with their start and end apart: 9, of which 4 were waited for; matrix products, arithmetic and copies ran while one was open for 0% of the time, Pallas kernels for 23%

profile of v2, /device:TPU:0, one launch (start us, length us, event | category | flops | bytes accessed | tf_op | source)
XLA Modules:
  0.0 59.9 jit_solution(17298925849122610871)
XLA Ops:
  0.6 0.0 copy-start
  0.6 2.6 %shard_map.102 = bf16[128,3200]{1,0:T(8,128)(2,1)} custom-call(s32[8,16]{1,0:T(8,128)} %bitcast.20, s32[1,8]{1,0:T(1,128)} %bitcast.24, bf16[8,16]{1,0:T(8,128)(2,1)} %bitcast.22, bf16[128,1536]{1,0:T(8,128)(2,1)} %bitcast.29, bf16[128,1536]{1,0:T(8,128)(2,1)} %bitcast.30), custom_call_target="tpu_custom_call" | custom-call | flops 100663296 | bytes 1606432 | tf_op jit(solution)/shard_map/pallas_call | solution.py:41
  3.3 18.1 %all_to_all.10 = bf16[8,16,3200]{2,1,0:T(8,128)(2,1)S(1)} all-to-all(bf16[8,16,3200]{2,1,0:T(8,128)(2,1)} %bitcast.28), channel_id=1, replica_groups=mesh['expert'=8,'dp'=4] {'expert'}, dimensions={0} | all-to-all | bytes 1638400 | tf_op jit(solution)/shard_map/all_to_all | solution.py:251
  21.4 1.0 %shard_map.103 = (bf16[64,1536]{1,0:T(8,128)(2,1)S(1)}, bf16[64,128]{1,0:T(8,128)(2,1)S(1)}, bf16[64,1536]{1,0:T(8,128)(2,1)}) custom-call(bf16[128,3200]{1,0:T(8,128)(2,1)S(1)} %bitcast.16), custom_call_target="tpu_custom_call" | custom-call | flops 25165824 | bytes 1228800 | tf_op jit(solution)/shard_map/pallas_call | solution.py:41
  22.4 1.6 %collective-permute-start.1 = (bf16[64,1536]{1,0:T(8,128)(2,1)S(1)}, bf16[64,1536]{1,0:T(8,128)(2,1)}, u32[]{:S(2)}, u32[]{:S(2)}) collective-permute-start(bf16[64,1536]{1,0:T(8,128)(2,1)S(1)} %get-tuple-element.32.x_ref), channel_id=1, source_target_pairs={{0,1},{1,0},{2,3},{3,2},{4,5},{5,4},{6,7},{7,6},{8,9},{9,8},{10,11... | collective-permute-start | bytes 589832 | tf_op jit(solution)/shard_map/ppermute | solution.py:312
  24.1 2.6 %collective-permute-start.4 = (bf16[64,1536]{1,0:T(8,128)(2,1)S(1)}, bf16[64,1536]{1,0:T(8,128)(2,1)}, u32[]{:S(2)}, u32[]{:S(2)}) collective-permute-start(bf16[64,1536]{1,0:T(8,128)(2,1)S(1)} %get-tuple-element.32.x_ref), channel_id=1, source_target_pairs={{0,2},{2,0},{1,3},{3,1},{4,6},{6,4},{5,7},{7,5},{8,10},{10,8},{9,1... | collective-permute-start | bytes 589832 | tf_op jit(solution)/shard_map/ppermute | solution.py:311
  26.6 0.0 copy-done
  26.7 2.2 %shard_map.104 = (f32[64,768]{1,0:T(8,128)S(1)}, bf16[64,1152]{1,0:T(8,128)(2,1)}, bf16[64,1152]{1,0:T(8,128)(2,1)S(1)}, bf16[64,1536]{1,0:T(8,128)(2,1)}, bf16[64,1152]{1,0:T(8,128)(2,1)S(1)}) custom-call(s32[1]{0:T(128)} %bitcast.index_ref.refs_6_, bf16[128,3200]{1,0:T(8,128)(2,1)S(1)} %bitcast.17, bf16[64,128]{1,0:T(8,128)(2,1)S(1)} %get-tuple-element.34.pack_ref, ...), custom_call_target="tpu_custom_call" | custom-call | flops 176160768 | bytes 4030468 | tf_op jit(solution)/shard_map/pallas_call | solution.py:41
  28.9 0.0 copy-start.6
  28.9 0.6 %copy-done.6 = bf16[64,1152]{1,0:T(8,128)(2,1)} copy-done((bf16[64,1152]{1,0:T(8,128)(2,1)}, bf16[64,1152]{1,0:T(8,128)(2,1)S(1)}, u32[]{:S(2)}) %copy-start.6) | copy-done | bytes 147480
  29.5 0.0 copy-start.1
  29.5 0.0 copy-start.2
  29.5 0.0 copy-start.7
  29.5 0.3 collective-permute-start.2
  29.9 3.6 %collective-permute-done.1.refs_1_ = bf16[64,1536]{1,0:T(8,128)(2,1)} collective-permute-done((bf16[64,1536]{1,0:T(8,128)(2,1)S(1)}, bf16[64,1536]{1,0:T(8,128)(2,1)}, u32[]{:S(2)}, u32[]{:S(2)}) %collective-permute-start.1) | collective-permute-done | bytes 196640 | tf_op jit(solution)/shard_map/ppermute | solution.py:312
  33.4 5.1 %shard_map.105 = bf16[128,1664]{1,0:T(8,128)(2,1)} custom-call(bf16[64,1536]{1,0:T(8,128)(2,1)S(1)} %get-tuple-element.32.x_ref, f32[64,768]{1,0:T(8,128)S(1)} %get-tuple-element.33.grad_ref, bf16[64,128]{1,0:T(8,128)(2,1)S(1)} %get-tuple-element.34.pack_ref, bf16[1536,1536]{1,0:T(8,128)(2,1)} %bitcast.26), custom_call_target="tpu_custom_call" | custom-call | flops 603979776 | bytes 5554176 | tf_op jit(solution)/shard_map/pallas_call | solution.py:41
  38.5 3.5 %all-to-all-start.1 = ((bf16[8,16,1664]{2,1,0:T(8,128)(2,1)}), bf16[8,16,1664]{2,1,0:T(8,128)(2,1)S(1)}, u32[]{:S(2)}, u32[]{:S(2)}) async-start(bf16[8,16,1664]{2,1,0:T(8,128)(2,1)} %bitcast.10), calls=%async_computation.1 | async-start | bytes 851968 | tf_op jit(solution)/shard_map/all_to_all | solution.py:251
  42.0 0.0 copy-done.7
  42.0 0.1 collective-permute-start.5
  42.1 0.7 %collective-permute-start.6 = (bf16[64,1536]{1,0:T(8,128)(2,1)S(1)}, bf16[64,1536]{1,0:T(8,128)(2,1)S(1)}, u32[]{:S(2)}, u32[]{:S(2)}) collective-permute-start(bf16[64,1536]{1,0:T(8,128)(2,1)S(1)} %get-tuple-element.32.x_ref), channel_id=1, source_target_pairs={{1,2},{2,1},{5,6},{6,5},{9,10},{10,9},{13,14},{14,13},{17,18},{18,... | collective-permute-start | bytes 589832 | tf_op jit(solution)/shard_map/ppermute | solution.py:329
  42.8 0.0 collective-permute-done.4.refs_2_
  42.8 1.3 %collective-permute-start.7 = (bf16[64,1536]{1,0:T(8,128)(2,1)}, bf16[64,1536]{1,0:T(8,128)(2,1)S(1)}, u32[]{:S(2)}, u32[]{:S(2)}) collective-permute-start(bf16[64,1536]{1,0:T(8,128)(2,1)} %collective-permute-done.4.refs_2_), channel_id=1, source_target_pairs={{1,0},{2,3},{5,4},{6,7},{9,8},{10,11},{13,12},{14,15},{17,16},{18,... | collective-permute-start | bytes 589832 | tf_op jit(solution)/shard_map/ppermute | solution.py:331
  44.1 0.0 collective-permute-done.2.refs_5_
  44.1 1.3 %collective-permute-start.3 = (bf16[64,1536]{1,0:T(8,128)(2,1)S(1)}, bf16[64,1536]{1,0:T(8,128)(2,1)S(1)}, u32[]{:S(2)}, u32[]{:S(2)}) collective-permute-start(bf16[64,1536]{1,0:T(8,128)(2,1)S(1)} %collective-permute-done.2.refs_5_), channel_id=1, source_target_pairs={{1,0},{2,3},{5,4},{6,7},{9,8},{10,11},{13,12},{14,15},{17,16},{18,... | collective-permute-start | bytes 589832 | tf_op jit(solution)/shard_map/ppermute | solution.py:332
  45.4 0.7 %collective-permute-start = (bf16[64,1152]{1,0:T(8,128)(2,1)S(1)}, bf16[64,1152]{1,0:T(8,128)(2,1)S(1)}, u32[]{:S(2)}, u32[]{:S(2)}) collective-permute-start(bf16[64,1152]{1,0:T(8,128)(2,1)S(1)} %get-tuple-element.31), channel_id=1, source_target_pairs={{1,2},{2,1},{5,6},{6,5},{9,10},{10,9},{13,14},{14,13},{17,18},{18,... | collective-permute-start | bytes 442376 | tf_op jit(solution)/shard_map/ppermute | solution.py:330
  46.1 2.1 %collective-permute-done.5.refs_4_ = bf16[64,1152]{1,0:T(8,128)(2,1)S(1)} collective-permute-done((bf16[64,1152]{1,0:T(8,128)(2,1)S(1)}, bf16[64,1152]{1,0:T(8,128)(2,1)S(1)}, u32[]{:S(2)}, u32[]{:S(2)}) %collective-permute-start.5) | collective-permute-done | bytes 147488 | tf_op jit(solution)/shard_map/ppermute | solution.py:314
  48.2 0.0 copy-done.1
  48.2 0.0 copy-done.2
  48.2 0.0 copy-start.3
  48.2 0.0 copy-start.4
  48.2 0.0 copy-start.5
  48.2 4.3 %shard_map.107 = (bf16[1536,1536]{1,0:T(8,128)(2,1)S(1)}, bf16[192,384]{1,0:T(8,128)(2,1)S(1)}, bf16[192,384]{1,0:T(8,128)(2,1)S(1)}, bf16[192,768]{1,0:T(8,128)(2,1)S(1)}, bf16[192,1536]{1,0:T(8,128)(2,1)S(1)}) custom-call(bf16[64,1536]{1,0:T(8,128)(2,1)S(1)} %copy-done.1, bf16[64,1536]{1,0:T(8,128)(2,1)} %collective-permute-done.1.refs_1_, ...), custom_call_target="tpu_custom_call" | custom-call | flops 905969664 | bytes 11698180 | tf_op jit(solution)/shard_map/pallas_call | solution.py:41
  52.5 0.0 collective-permute-done.6.middle_ref
  52.5 2.3 %collective-permute-done.7.onward_ref = bf16[64,1536]{1,0:T(8,128)(2,1)S(1)} collective-permute-done((bf16[64,1536]{1,0:T(8,128)(2,1)}, bf16[64,1536]{1,0:T(8,128)(2,1)S(1)}, u32[]{:S(2)}, u32[]{:S(2)}) %collective-permute-start.7) | collective-permute-done | bytes 196640 | tf_op jit(solution)/shard_map/ppermute | solution.py:331
  54.8 0.9 %shard_map.108 = (bf16[64,384]{1,0:T(8,128)(2,1)S(1)}, bf16[64,768]{1,0:T(8,128)(2,1)S(1)}, f32[64,768]{1,0:T(8,128)S(1)}, f32[64,768]{1,0:T(8,128)S(1)}) custom-call(bf16[64,1536]{1,0:T(8,128)(2,1)S(1)} %collective-permute-done.6.middle_ref, bf16[64,1536]{1,0:T(8,128)(2,1)S(1)} %collective-permute-done.7.onward_ref, s32[1]{0:T(128)} %bitcast.index_ref.refs_6_, ...), custom_call_target="tpu_custom_call" | custom-call | flops 301989888 | bytes 5652484 | tf_op jit(solution)/shard_map/pallas_call | solution.py:41
  55.8 0.0 all-to-all-done.1
  55.8 0.0 copy-done.3
  55.8 0.0 copy-done.4
  55.8 0.0 copy-done.5
  55.8 1.4 %shard_map.106 = (bf16[128,1536]{1,0:T(8,128)(2,1)}, bf16[8,16]{1,0:T(8,128)(2,1)}) custom-call(s32[8,16]{1,0:T(8,128)S(1)} %bitcast.21, s32[1,8]{1,0:T(1,128)S(1)} %bitcast.25, bf16[8,16]{1,0:T(8,128)(2,1)S(1)} %bitcast.23, bf16[128,1664]{1,0:T(8,128)(2,1)S(1)} %bitcast.19), custom_call_target="tpu_custom_call" | custom-call | flops 50331648 | bytes 820256 | tf_op jit(solution)/shard_map/pallas_call | solution.py:41
  57.2 0.0 collective-permute-done.middle_ref
  57.2 0.9 %collective-permute-done.3.onward_ref = bf16[64,1536]{1,0:T(8,128)(2,1)S(1)} collective-permute-done((bf16[64,1536]{1,0:T(8,128)(2,1)S(1)}, bf16[64,1536]{1,0:T(8,128)(2,1)S(1)}, u32[]{:S(2)}, u32[]{:S(2)}) %collective-permute-start.3) | collective-permute-done | bytes 196640 | tf_op jit(solution)/shard_map/ppermute | solution.py:332
  58.1 1.7 %shard_map.109 = (bf16[384,1536]{1,0:T(8,128)(2,1)}, bf16[768,384]{1,0:T(8,128)(2,1)}) custom-call(bf16[64,1152]{1,0:T(8,128)(2,1)S(1)} %collective-permute-done.middle_ref, bf16[64,1536]{1,0:T(8,128)(2,1)S(1)} %collective-permute-done.3.onward_ref, bf16[192,384]{1,0:T(8,128)(2,1)S(1)} %get-tuple-element.45.refs_0_, ...), custom_call_target="tpu_custom_call" | custom-call | flops 452984832 | bytes 3833856 | tf_op jit(solution)/shard_map/pallas_call | solution.py:41
Async XLA Ops:
  0.6 26.0 %copy-start = (bf16[1,768,1536]{2,1,0:T(8,128)(2,1)S(1)}, bf16[1,768,1536]{2,1,0:T(8,128)(2,1)}, u32[]{:S(2)}) copy-start(bf16[1,768,1536]{2,1,0:T(8,128)(2,1)} %param.13) | copy-start | bytes 7077892
  22.4 11.0 %collective-permute-start.1 = (bf16[64,1536]{1,0:T(8,128)(2,1)S(1)}, bf16[64,1536]{1,0:T(8,128)(2,1)}, u32[]{:S(2)}, u32[]{:S(2)}) collective-permute-start(bf16[64,1536]{1,0:T(8,128)(2,1)S(1)} %get-tuple-element.32.x_ref), channel_id=1, source_target_pairs={{0,1},{1,0},{2,3},{3,2},{4,5},{5,4},{6,7},{7,6},{8,9},{9,8},{10,11... | collective-permute-start | bytes 589832 | tf_op jit(solution)/shard_map/ppermute | solution.py:312
  24.1 18.7 %collective-permute-start.4 = (bf16[64,1536]{1,0:T(8,128)(2,1)S(1)}, bf16[64,1536]{1,0:T(8,128)(2,1)}, u32[]{:S(2)}, u32[]{:S(2)}) collective-permute-start(bf16[64,1536]{1,0:T(8,128)(2,1)S(1)} %get-tuple-element.32.x_ref), channel_id=1, source_target_pairs={{0,2},{2,0},{1,3},{3,1},{4,6},{6,4},{5,7},{7,5},{8,10},{10,8},{9,1... | collective-permute-start | bytes 589832 | tf_op jit(solution)/shard_map/ppermute | solution.py:311
  28.9 0.7 %copy-start.6 = (bf16[64,1152]{1,0:T(8,128)(2,1)}, bf16[64,1152]{1,0:T(8,128)(2,1)S(1)}, u32[]{:S(2)}) copy-start(bf16[64,1152]{1,0:T(8,128)(2,1)S(1)} %get-tuple-element.44) | copy-start | bytes 442372
  29.5 18.6 %copy-start.1 = (bf16[64,1536]{1,0:T(8,128)(2,1)S(1)}, bf16[64,1536]{1,0:T(8,128)(2,1)}, u32[]{:S(2)}) copy-start(bf16[64,1536]{1,0:T(8,128)(2,1)} %get-tuple-element.40.refs_0_) | copy-start | bytes 589828
  29.5 18.6 %copy-start.2 = (bf16[64,1152]{1,0:T(8,128)(2,1)S(1)}, bf16[64,1152]{1,0:T(8,128)(2,1)}, u32[]{:S(2)}) copy-start(bf16[64,1152]{1,0:T(8,128)(2,1)} %get-tuple-element.43.refs_3_) | copy-start | bytes 442372
  29.5 12.5 %copy-start.7 = (bf16[64,1152]{1,0:T(8,128)(2,1)S(1)}, bf16[64,1152]{1,0:T(8,128)(2,1)}, u32[]{:S(2)}) copy-start(bf16[64,1152]{1,0:T(8,128)(2,1)} %copy-done.6) | copy-start | bytes 442372
  29.5 14.6 %collective-permute-start.2 = (bf16[64,1536]{1,0:T(8,128)(2,1)}, bf16[64,1536]{1,0:T(8,128)(2,1)S(1)}, u32[]{:S(2)}, u32[]{:S(2)}) collective-permute-start(bf16[64,1536]{1,0:T(8,128)(2,1)} %get-tuple-element.39), channel_id=1, source_target_pairs={{0,2},{2,0},{1,3},{3,1},{4,6},{6,4},{5,7},{7,5},{8,10},{10,8},{9,1... | collective-permute-start | bytes 589832 | tf_op jit(solution)/shard_map/ppermute | solution.py:313
  38.5 17.3 %all-to-all-start.1 = ((bf16[8,16,1664]{2,1,0:T(8,128)(2,1)}), bf16[8,16,1664]{2,1,0:T(8,128)(2,1)S(1)}, u32[]{:S(2)}, u32[]{:S(2)}) async-start(bf16[8,16,1664]{2,1,0:T(8,128)(2,1)} %bitcast.10), calls=%async_computation.1 | async-start | bytes 851968 | tf_op jit(solution)/shard_map/all_to_all | solution.py:251
  42.0 6.2 %collective-permute-start.5 = (bf16[64,1152]{1,0:T(8,128)(2,1)S(1)}, bf16[64,1152]{1,0:T(8,128)(2,1)S(1)}, u32[]{:S(2)}, u32[]{:S(2)}) collective-permute-start(bf16[64,1152]{1,0:T(8,128)(2,1)S(1)} %copy-done.7), channel_id=1, source_target_pairs={{0,1},{1,0},{2,3},{3,2},{4,5},{5,4},{6,7},{7,6},{8,9},{9,8},{10,11... | collective-permute-start | bytes 442376 | tf_op jit(solution)/shard_map/ppermute | solution.py:314
  42.1 10.4 %collective-permute-start.6 = (bf16[64,1536]{1,0:T(8,128)(2,1)S(1)}, bf16[64,1536]{1,0:T(8,128)(2,1)S(1)}, u32[]{:S(2)}, u32[]{:S(2)}) collective-permute-start(bf16[64,1536]{1,0:T(8,128)(2,1)S(1)} %get-tuple-element.32.x_ref), channel_id=1, source_target_pairs={{1,2},{2,1},{5,6},{6,5},{9,10},{10,9},{13,14},{14,13},{17,18},{18,... | collective-permute-start | bytes 589832 | tf_op jit(solution)/shard_map/ppermute | solution.py:329
  42.8 12.0 %collective-permute-start.7 = (bf16[64,1536]{1,0:T(8,128)(2,1)}, bf16[64,1536]{1,0:T(8,128)(2,1)S(1)}, u32[]{:S(2)}, u32[]{:S(2)}) collective-permute-start(bf16[64,1536]{1,0:T(8,128)(2,1)} %collective-permute-done.4.refs_2_), channel_id=1, source_target_pairs={{1,0},{2,3},{5,4},{6,7},{9,8},{10,11},{13,12},{14,15},{17,16},{18,... | collective-permute-start | bytes 589832 | tf_op jit(solution)/shard_map/ppermute | solution.py:331
  44.1 14.0 %collective-permute-start.3 = (bf16[64,1536]{1,0:T(8,128)(2,1)S(1)}, bf16[64,1536]{1,0:T(8,128)(2,1)S(1)}, u32[]{:S(2)}, u32[]{:S(2)}) collective-permute-start(bf16[64,1536]{1,0:T(8,128)(2,1)S(1)} %collective-permute-done.2.refs_5_), channel_id=1, source_target_pairs={{1,0},{2,3},{5,4},{6,7},{9,8},{10,11},{13,12},{14,15},{17,16},{18,... | collective-permute-start | bytes 589832 | tf_op jit(solution)/shard_map/ppermute | solution.py:332
  45.4 11.8 %collective-permute-start = (bf16[64,1152]{1,0:T(8,128)(2,1)S(1)}, bf16[64,1152]{1,0:T(8,128)(2,1)S(1)}, u32[]{:S(2)}, u32[]{:S(2)}) collective-permute-start(bf16[64,1152]{1,0:T(8,128)(2,1)S(1)} %get-tuple-element.31), channel_id=1, source_target_pairs={{1,2},{2,1},{5,6},{6,5},{9,10},{10,9},{13,14},{14,13},{17,18},{18,... | collective-permute-start | bytes 442376 | tf_op jit(solution)/shard_map/ppermute | solution.py:330
  48.2 7.6 %copy-start.3 = (s32[1,1,8,16]{3,2,1,0:T(8,128)S(1)}, s32[1,1,8,16]{3,2,1,0:T(8,128)}, u32[]{:S(2)}) copy-start(s32[1,1,8,16]{3,2,1,0:T(8,128)} %param.9) | copy-start | bytes 1540
  48.2 7.6 %copy-start.4 = (bf16[1,1,8,16]{3,2,1,0:T(8,128)(2,1)S(1)}, bf16[1,1,8,16]{3,2,1,0:T(8,128)(2,1)}, u32[]{:S(2)}) copy-start(bf16[1,1,8,16]{3,2,1,0:T(8,128)(2,1)} %param.11) | copy-start | bytes 772
  48.2 7.6 %copy-start.5 = (s32[1,1,8]{2,1,0:T(1,128)S(1)}, s32[1,1,8]{2,1,0:T(1,128)}, u32[]{:S(2)}) copy-start(s32[1,1,8]{2,1,0:T(1,128)} %param.10) | copy-start | bytes 100

commit v3 on v2

--- a/solution.py
+++ b/solution.py
@@ -17,7 +17,7 @@
 MIDDLE = ((1, 2), (2, 1))
 FAR = ((0, 2), (2, 0), (1, 3), (3, 1))
 ONWARD = ((1, 0), (2, 3))
-LOADS = ((0,), (1,), (2, 3), (3,))
+LOADS = ((0,), (3,), (1,), (2, 3))
 
 
 def dot_nn(left, right):
@@ -107,32 +107,39 @@
     return jnp.where(used > 0.5, jnp.where(place == row, 1.0, 0.0), 0.0).astype(BF16)
 
 
-def pack_rows(arrived_ref, x_ref, pack_ref, x_keep_hbm, sem):
+def pack_rows(arrived_ref, x_ref, pack_ref):
     width = x_ref.shape[1]
     pack = pack_matrix(arrived_ref[:, 2 * width :])
     pack_ref[...] = pack
     x_ref[...] = dot_nn(pack, arrived_ref[:, :width]).astype(BF16)
-    keep = pltpu.make_async_copy(x_ref, x_keep_hbm, sem)
-    keep.start()
-    keep.wait()
-
-
-def own_hidden_grad(share, index_ref, arrived_ref, pack_ref, w_down_ref, grad_ref, *refs):
-    *load_refs, scaled_ref, own_ref, sem = refs
+
+
+def own_hidden_grad(share, index_ref, arrived_ref, pack_ref, x_ref, w_down_ref, grad_ref, *refs):
+    *load_refs, scaled_ref, own_ref, middle_ref, sems = refs
     inner, width = w_down_ref.shape
+    copies = []
+    if load_refs:
+        own_hbm, near_ref, far_ref, middle_hbm = load_refs
+        for place, target in enumerate((own_hbm, middle_hbm)):
+            x_part = target.at[:, pl.ds(inner + share, width)]
+            copies.append(pltpu.make_async_copy(x_ref, x_part, sems.at[place]))
+            copies[-1].start()
     scaled_ref[...] = dot_nn(pack_ref[...], arrived_ref[:, width : 2 * width]).astype(BF16)
     hidden_grad = dot_nt(scaled_ref[...], w_down_ref[...])
     grad_ref[...] = hidden_grad
     if not load_refs:
         return
-    for load_ref, steps in zip((own_ref, *load_refs[1:]), LOADS):
+    for place, (load_ref, steps) in enumerate(zip((own_ref, middle_ref, near_ref, far_ref), LOADS)):
         load_ref[:, :inner] = hidden_grad.astype(BF16)
-        for place, step in enumerate(steps):
+        for part, step in enumerate(steps):
             start = pl.multiple_of((index_ref[0] ^ step) * share, LANES)
-            load_ref[:, pl.ds(inner + place * share, share)] = scaled_ref[:, pl.ds(start, share)]
-    keep = pltpu.make_async_copy(own_ref, load_refs[0], sem)
-    keep.start()
-    keep.wait()
+            load_ref[:, pl.ds(inner + part * share, share)] = scaled_ref[:, pl.ds(start, share)]
+        if place < 2:
+            load_part = (own_hbm, middle_hbm)[place].at[:, pl.ds(0, inner + share)]
+            copies.append(pltpu.make_async_copy(load_ref, load_part, sems.at[2 + place]))
+            copies[-1].start()
+    for copy in copies:
+        copy.wait()
 
 
 def activations(pre, inner):
@@ -201,11 +208,12 @@
 
 
 def near_rows(share, *refs):
-    x_refs, load_refs, index_ref, w_in_ref = refs[:3], refs[3:6], refs[6], refs[7]
-    w_in_held, x_share_ref, s_share_ref, hidden_ref, in_rows_ref, held, sems = refs[8:]
+    x_refs, load_refs, index_ref, w_in_ref = refs[:2], refs[2:5], refs[5], refs[6]
+    w_in_held, x_share_ref, s_share_ref, hidden_ref, in_rows_ref, held, sems = refs[7:]
     copies = start_parts(w_in_ref, w_in_held, sems)
     inner = hidden_ref.shape[1]
-    for place, ref in enumerate(x_refs):
+    held[:USED, :] = load_refs[0][:, inner + share :]
+    for place, ref in enumerate(x_refs, 1):
         held[place * USED : (place + 1) * USED, :] = ref[...]
     x_share_ref[...] = held[:, pl.ds(pl.multiple_of(index_ref[0] * share, LANES), share)]
     hidden, gate_factor, up_factor = activations(project(held, w_in_held, copies), inner)
@@ -221,7 +229,8 @@
 def third_rows(
     share, middle_ref, onward_ref, index_ref, w_in_ref, x_share_ref, hidden_ref, gate_factor_ref, up_factor_ref, held
 ):
-    held[...] = middle_ref[...] + onward_ref[...]
+    inner = hidden_ref.shape[1]
+    held[...] = middle_ref[:, inner + share :] + onward_ref[...]
     x_share_ref[...] = held[:, pl.ds(pl.multiple_of(index_ref[0] * share, LANES), share)]
     hidden, gate_factor, up_factor = activations(dot_nn(held[...], w_in_ref[...]), hidden_ref.shape[1])
     hidden_ref[...] = hidden
@@ -238,7 +247,7 @@
     third_x_ref, third_hidden_ref, gate_factor_ref, up_factor_ref = third
     x_share[most:, :] = third_x_ref[...]
     hidden[most:, :] = third_hidden_ref[...]
-    s_share[most:, :] = middle_ref[:, inner:] + onward_ref[:, inner + share :]
+    s_share[most:, :] = middle_ref[:, inner : inner + share] + onward_ref[:, inner + share :]
     grad = (middle_ref[:, :inner] + onward_ref[:, :inner]).astype(F32)
     in_rows[most:, :inner] = (grad * gate_factor_ref[...]).astype(BF16)
     in_rows[most:, inner:] = (grad * up_factor_ref[...]).astype(BF16)
@@ -276,35 +285,42 @@
     (sent,) = call(
         pick_rows,
         [shape((slots, 2 * width + LANES), BF16)],
-        picked,
+        [pltpu.with_memory_space_constraint(a, pltpu.HBM) for a in picked],
         4 * slots * n_tokens * width,
         [hbm] * 5,
         [pltpu.VMEM(a.shape, a.dtype) for a in picked] + [pltpu.SemaphoreType.DMA((5,))],
-        56,
+        8,
     )
     arrived = to_experts(sent, peers)
-    x_rows, pack, x_keep = call(
+    x_rows, pack = call(
         pack_rows,
-        [shape((USED, width), BF16), shape((USED, slots), BF16), pltpu.HBM((USED, width), BF16)],
+        [shape((USED, width), BF16), shape((USED, slots), BF16)],
         (arrived,),
         2 * USED * slots * width,
-        None,
-        [pltpu.SemaphoreType.DMA],
-        6,
-        [vmem, vmem, hbm],
-    )
-    sizes = [inner + len(steps) * share for steps in LOADS]
+        vmem=6,
+    )
+    short = inner + share
     hidden_grad, *loads = call(
         functools.partial(own_hidden_grad, share),
         [shape((USED, inner), F32)]
-        + [pltpu.HBM((USED, sizes[0]), BF16)] * on_line
-        + [shape((USED, size), BF16) for size in sizes[1:]] * on_line,
-        (index, arrived, pack, w_down),
+        + [
+            pltpu.HBM((USED, short + width), BF16),
+            shape((USED, short), BF16),
+            shape((USED, short + share), BF16),
+            pltpu.HBM((USED, short + width), BF16),
+        ]
+        * on_line,
+        (index, arrived, pack, x_rows, w_down),
         2 * USED * width * (slots + inner),
-        [smem, vmem, vmem, vmem],
-        [pltpu.VMEM((USED, width), BF16), pltpu.VMEM((USED, sizes[0]), BF16), pltpu.SemaphoreType.DMA],
+        [smem] + [vmem] * 4,
+        [
+            pltpu.VMEM((USED, width), BF16),
+            pltpu.VMEM((USED, short), BF16),
+            pltpu.VMEM((USED, short), BF16),
+            pltpu.SemaphoreType.DMA((4,)),
+        ],
         8,
-        [vmem] + ([hbm] + [vmem] * 3) * on_line,
+        [vmem] + [hbm, vmem, vmem, hbm] * on_line,
     )
     if on_line:
         own, near_load, far_load, middle_load = loads
@@ -312,7 +328,6 @@
         x_near = lax.ppermute(x_rows, "dp", NEAR)
         far = lax.ppermute(far_load, "dp", FAR)
         near = lax.ppermute(near_load, "dp", NEAR)
-        x_near, pack = lax.optimization_barrier((x_near, pack))
     parts = 4
     (sent_back,) = call(
         own_rows,
@@ -323,10 +338,11 @@
         [pltpu.VMEM(w_in.shape, BF16), pltpu.SemaphoreType.DMA((parts,))],
         16,
     )
+    if on_line:
+        x_near, near, sent_back = lax.optimization_barrier((x_near, near, sent_back))
     back = to_experts(sent_back, peers)
     if on_line:
         x_far, sent_back = lax.optimization_barrier((x_far, sent_back))
-        x_middle = lax.ppermute(x_rows, "dp", MIDDLE)
         middle = lax.ppermute(middle_load, "dp", MIDDLE)
         x_onward = lax.ppermute(x_far, "dp", ONWARD)
         onward = lax.ppermute(far, "dp", ONWARD)
@@ -349,9 +365,9 @@
                 shape((first, inner), BF16),
                 shape((first, 2 * inner), BF16),
             ],
-            (x_keep, x_near, x_far, own, near, far, index, w_in_far),
+            (x_near, x_far, own, near, far, index, w_in_far),
             4 * first * inner * width,
-            [vmem] * 6 + [smem, hbm],
+            [vmem] * 5 + [smem, hbm],
             [pltpu.VMEM((first, width), BF16), pltpu.SemaphoreType.DMA((parts,))],
             16,
         )
@@ -363,7 +379,7 @@
                 shape((USED, inner), F32),
                 shape((USED, inner), F32),
             ],
-            (x_middle, x_onward, index, w_in_held),
+            (middle, x_onward, index, w_in_held),
             4 * USED * inner * width,
             [vmem] * 2 + [smem, vmem],
             [pltpu.VMEM((USED, width), BF16)],

time: 60.2 us -> 57.1 us (0.949)
  Pallas kernels: 19.3 us -> 17.7 us
  waiting for transfers between devices: 8.91 us -> 7.94 us
  local copies, waits for them, and re-layouts: 0.68 us -> 0.03 us
    ppermute x1, waiting for transfers between devices: 3.55 us -> 0.01 us  [on_device(): x_near = lax.ppermute(x_rows, 'dp', NEAR)]
    ppermute x1, waiting for transfers between devices: 0.04 us -> 2.92 us  [on_device(): far = lax.ppermute(far_load, 'dp', FAR)]
    ppermute x1, waiting for transfers between devices: 0.01 us -> 2.77 us  [on_device(): x_far = lax.ppermute(x_rows, 'dp', FAR)]
    ppermute x1, waiting for transfers between devices: 2.29 us -> 0.01 us  [on_device(): x_onward = lax.ppermute(x_far, 'dp', ONWARD)]
    pallas_call x8, Pallas kernels: 19.3 us -> 17.7 us  [call(): pl.pallas_call(body, out_shape=tuple(outs), in_specs=in_specs or [pl.Bloc...]
    ppermute x1, waiting for transfers between devices: 0.94 us -> 0.01 us  [on_device(): onward = lax.ppermute(far, 'dp', ONWARD)]
    ppermute x1 -> x0, starting transfers between devices: 0.67 us -> none  [on_device(): x_middle = lax.ppermute(x_rows, 'dp', MIDDLE)]
    unnamed x16 -> x10, local copies, waits for them, and re-layouts: 0.68 us -> 0.03 us
  transfers between devices with their start and end apart: 9 -> 8, of which waited for: 4 -> 3; matrix products, arithmetic and copies ran while one was open for 0% -> 0% of each run, Pallas kernels for 23% -> 25%
where the time goes in v3:
time: 57.1 us; the launch traced here: 56.2 us
  blocking collectives  17.9 us (31%)
  Pallas kernels  17.7 us (31%)
  starting transfers between devices  11.8 us (21%)
  waiting for transfers between devices  7.94 us (14%)
  between operations  0.81 us (1%)
    all_to_all x1, blocking collectives, to_experts(): lax.all_to_all(block.reshape(peers, slots // peers, width), 'expert', spl...  17.9 us
    pallas_call x8, Pallas kernels, call(): pl.pallas_call(body, out_shape=tuple(outs), in_specs=in_specs or [pl.Bloc...  17.7 us
    all_to_all x1, starting transfers between devices, to_experts(): lax.all_to_all(block.reshape(peers, slots // peers, width), 'expert', spl...  3.47 us
    ppermute x1, waiting for transfers between devices, on_device(): far = lax.ppermute(far_load, 'dp', FAR)  2.92 us
    ppermute x1, waiting for transfers between devices, on_device(): x_far = lax.ppermute(x_rows, 'dp', FAR)  2.77 us
    ppermute x1, starting transfers between devices, on_device(): x_far = lax.ppermute(x_rows, 'dp', FAR)  2.58 us
    ppermute x1, waiting for transfers between devices, on_device(): near = lax.ppermute(near_load, 'dp', NEAR)  2.24 us
    ppermute x1, starting transfers between devices, on_device(): x_near = lax.ppermute(x_rows, 'dp', NEAR)  1.64 us
  transfers between devices with their start and end apart: 8, of which 3 were waited for; matrix products, arithmetic and copies ran while one was open for 0% of the time, Pallas kernels for 25%

profile of v3, /device:TPU:0, one launch (start us, length us, event | category | flops | bytes accessed | tf_op | source)
XLA Modules:
  0.0 56.2 jit_solution(10185854210911322081)
XLA Ops:
  0.6 0.0 copy-start
  0.6 1.7 %shard_map.102 = bf16[128,3200]{1,0:T(8,128)(2,1)S(1)} custom-call(s32[8,16]{1,0:T(8,128)} %bitcast.21, s32[1,8]{1,0:T(1,128)} %bitcast.25, bf16[8,16]{1,0:T(8,128)(2,1)} %bitcast.23, bf16[128,1536]{1,0:T(8,128)(2,1)} %bitcast.29, bf16[128,1536]{1,0:T(8,128)(2,1)} %bitcast.30), custom_call_target="tpu_custom_call" | custom-call | flops 100663296 | bytes 1606432 | tf_op jit(solution)/shard_map/pallas_call | solution.py:41
  2.4 17.9 %all_to_all.10 = bf16[8,16,3200]{2,1,0:T(8,128)(2,1)S(1)} all-to-all(bf16[8,16,3200]{2,1,0:T(8,128)(2,1)S(1)} %bitcast.18), channel_id=1, replica_groups=mesh['expert'=8,'dp'=4] {'expert'}, dimensions={0} | all-to-all | bytes 1638400 | tf_op jit(solution)/shard_map/all_to_all | solution.py:260
  20.3 0.4 shard_map.103
  20.6 1.6 %collective-permute-start.1 = (bf16[64,1536]{1,0:T(8,128)(2,1)S(1)}, bf16[64,1536]{1,0:T(8,128)(2,1)}, u32[]{:S(2)}, u32[]{:S(2)}) collective-permute-start(bf16[64,1536]{1,0:T(8,128)(2,1)S(1)} %get-tuple-element.31.x_ref), channel_id=1, source_target_pairs={{0,1},{1,0},{2,3},{3,2},{4,5},{5,4},{6,7},{7,6},{8,9},{9,8},{10,11... | collective-permute-start | bytes 589832 | tf_op jit(solution)/shard_map/ppermute | solution.py:328
  22.3 0.0 copy-done
  22.3 2.3 %shard_map.104 = (f32[64,768]{1,0:T(8,128)S(1)}, bf16[64,2688]{1,0:T(8,128)(2,1)}, bf16[64,1152]{1,0:T(8,128)(2,1)S(1)}, bf16[64,1536]{1,0:T(8,128)(2,1)}, bf16[64,2688]{1,0:T(8,128)(2,1)}) custom-call(s32[1]{0:T(128)} %bitcast.index_ref.refs_5_, bf16[128,3200]{1,0:T(8,128)(2,1)S(1)} %bitcast.17, bf16[64,128]{1,0:T(8,128)(2,1)S(1)} %get-tuple-element.30.pack_ref, ...), custom_call_target="tpu_custom_call" | custom-call | flops 176160768 | bytes 4620292 | tf_op jit(solution)/shard_map/pallas_call | solution.py:41
  24.6 0.0 copy-start.1
  24.6 0.5 collective-permute-start.2
  25.1 2.6 %collective-permute-start.5 = (bf16[64,1536]{1,0:T(8,128)(2,1)S(1)}, bf16[64,1536]{1,0:T(8,128)(2,1)S(1)}, u32[]{:S(2)}, u32[]{:S(2)}) collective-permute-start(bf16[64,1536]{1,0:T(8,128)(2,1)S(1)} %get-tuple-element.31.x_ref), channel_id=1, source_target_pairs={{0,2},{2,0},{1,3},{3,1},{4,6},{6,4},{5,7},{7,5},{8,10},{10,8},{9,1... | collective-permute-start | bytes 589832 | tf_op jit(solution)/shard_map/ppermute | solution.py:327
  27.7 0.3 collective-permute-start.3
  28.0 5.1 %shard_map.105 = bf16[128,1664]{1,0:T(8,128)(2,1)} custom-call(bf16[64,1536]{1,0:T(8,128)(2,1)S(1)} %get-tuple-element.31.x_ref, f32[64,768]{1,0:T(8,128)S(1)} %get-tuple-element.34.grad_ref, bf16[64,128]{1,0:T(8,128)(2,1)S(1)} %get-tuple-element.30.pack_ref, bf16[1536,1536]{1,0:T(8,128)(2,1)} %bitcast.27), custom_call_target="tpu_custom_call" | custom-call | flops 603979776 | bytes 5554176 | tf_op jit(solution)/shard_map/pallas_call | solution.py:41
  33.1 2.2 %collective-permute-done.2.refs_3_ = bf16[64,1152]{1,0:T(8,128)(2,1)S(1)} collective-permute-done((bf16[64,1152]{1,0:T(8,128)(2,1)S(1)}, bf16[64,1152]{1,0:T(8,128)(2,1)S(1)}, u32[]{:S(2)}, u32[]{:S(2)}) %collective-permute-start.2) | collective-permute-done | bytes 147488 | tf_op jit(solution)/shard_map/ppermute | solution.py:330
  35.3 0.0 collective-permute-done.1.refs_0_
  35.3 3.5 %all-to-all-start.1 = ((bf16[8,16,1664]{2,1,0:T(8,128)(2,1)}), bf16[8,16,1664]{2,1,0:T(8,128)(2,1)S(1)}, u32[]{:S(2)}, u32[]{:S(2)}) async-start(bf16[8,16,1664]{2,1,0:T(8,128)(2,1)} %bitcast.10), calls=%async_computation.1 | async-start | bytes 851968 | tf_op jit(solution)/shard_map/all_to_all | solution.py:260
  38.8 0.7 %collective-permute-start = (bf16[64,2688]{1,0:T(8,128)(2,1)}, bf16[64,2688]{1,0:T(8,128)(2,1)S(1)}, u32[]{:S(2)}, u32[]{:S(2)}) collective-permute-start(bf16[64,2688]{1,0:T(8,128)(2,1)} %get-tuple-element.32), channel_id=1, source_target_pairs={{1,2},{2,1},{5,6},{6,5},{9,10},{10,9},{13,14},{14,13},{17,18},{18,... | collective-permute-start | bytes 1032200 | tf_op jit(solution)/shard_map/ppermute | solution.py:346
  39.5 2.8 %collective-permute-done.5.refs_1_ = bf16[64,1536]{1,0:T(8,128)(2,1)S(1)} collective-permute-done((bf16[64,1536]{1,0:T(8,128)(2,1)S(1)}, bf16[64,1536]{1,0:T(8,128)(2,1)S(1)}, u32[]{:S(2)}, u32[]{:S(2)}) %collective-permute-start.5) | collective-permute-done | bytes 196640 | tf_op jit(solution)/shard_map/ppermute | solution.py:327
  42.3 1.3 %collective-permute-start.6 = (bf16[64,1536]{1,0:T(8,128)(2,1)S(1)}, bf16[64,1536]{1,0:T(8,128)(2,1)S(1)}, u32[]{:S(2)}, u32[]{:S(2)}) collective-permute-start(bf16[64,1536]{1,0:T(8,128)(2,1)S(1)} %collective-permute-done.5.refs_1_), channel_id=1, source_target_pairs={{1,0},{2,3},{5,4},{6,7},{9,8},{10,11},{13,12},{14,15},{17,16},{18,... | collective-permute-start | bytes 589832 | tf_op jit(solution)/shard_map/ppermute | solution.py:347
  43.5 2.9 %collective-permute-done.3.refs_4_ = bf16[64,1536]{1,0:T(8,128)(2,1)S(1)} collective-permute-done((bf16[64,1536]{1,0:T(8,128)(2,1)}, bf16[64,1536]{1,0:T(8,128)(2,1)S(1)}, u32[]{:S(2)}, u32[]{:S(2)}) %collective-permute-start.3) | collective-permute-done | bytes 196640 | tf_op jit(solution)/shard_map/ppermute | solution.py:329
  46.5 1.3 %collective-permute-start.4 = (bf16[64,1536]{1,0:T(8,128)(2,1)S(1)}, bf16[64,1536]{1,0:T(8,128)(2,1)S(1)}, u32[]{:S(2)}, u32[]{:S(2)}) collective-permute-start(bf16[64,1536]{1,0:T(8,128)(2,1)S(1)} %collective-permute-done.3.refs_4_), channel_id=1, source_target_pairs={{1,0},{2,3},{5,4},{6,7},{9,8},{10,11},{13,12},{14,15},{17,16},{18,... | collective-permute-start | bytes 589832 | tf_op jit(solution)/shard_map/ppermute | solution.py:348
  47.8 0.0 copy-done.1
  47.8 0.0 copy-start.2
  47.8 0.0 copy-start.3
  47.8 0.0 copy-start.4
  47.8 4.2 %shard_map.107 = (bf16[1536,1536]{1,0:T(8,128)(2,1)S(1)}, bf16[192,384]{1,0:T(8,128)(2,1)S(1)}, bf16[192,384]{1,0:T(8,128)(2,1)S(1)}, bf16[192,768]{1,0:T(8,128)(2,1)S(1)}, bf16[192,1536]{1,0:T(8,128)(2,1)S(1)}) custom-call(bf16[64,1536]{1,0:T(8,128)(2,1)} %collective-permute-done.1.refs_0_, bf16[64,1536]{1,0:T(8,128)(2,1)S(1)} %collective-permute-done.5.refs_1_, ...), custom_call_target="tpu_custom_call" | custom-call | flops 905969664 | bytes 11698180 | tf_op jit(solution)/shard_map/pallas_call | solution.py:41
  52.0 0.0 collective-permute-done.middle_ref
  52.0 0.0 collective-permute-done.6.onward_ref
  52.1 0.9 %shard_map.108 = (bf16[64,384]{1,0:T(8,128)(2,1)S(1)}, bf16[64,768]{1,0:T(8,128)(2,1)S(1)}, f32[64,768]{1,0:T(8,128)S(1)}, f32[64,768]{1,0:T(8,128)S(1)}) custom-call(bf16[64,2688]{1,0:T(8,128)(2,1)S(1)} %collective-permute-done.middle_ref, bf16[64,1536]{1,0:T(8,128)(2,1)S(1)} %collective-permute-done.6.onward_ref, s32[1]{0:T(128)} %bitcast.index_ref.refs_5_, ...), custom_call_target="tpu_custom_call" | custom-call | flops 301989888 | bytes 5799940 | tf_op jit(solution)/shard_map/pallas_call | solution.py:41
  53.0 0.0 all-to-all-done.1
  53.0 0.0 copy-done.2
  53.0 0.0 copy-done.3
  53.0 0.0 copy-done.4
  53.1 1.4 %shard_map.106 = (bf16[128,1536]{1,0:T(8,128)(2,1)}, bf16[8,16]{1,0:T(8,128)(2,1)}) custom-call(s32[8,16]{1,0:T(8,128)S(1)} %bitcast.22, s32[1,8]{1,0:T(1,128)S(1)} %bitcast.26, bf16[8,16]{1,0:T(8,128)(2,1)S(1)} %bitcast.24, bf16[128,1664]{1,0:T(8,128)(2,1)S(1)} %bitcast.20), custom_call_target="tpu_custom_call" | custom-call | flops 50331648 | bytes 820256 | tf_op jit(solution)/shard_map/pallas_call | solution.py:41
  54.4 0.0 collective-permute-done.4.onward_ref
  54.4 1.7 %shard_map.109 = (bf16[384,1536]{1,0:T(8,128)(2,1)}, bf16[768,384]{1,0:T(8,128)(2,1)}) custom-call(bf16[64,2688]{1,0:T(8,128)(2,1)S(1)} %collective-permute-done.middle_ref, bf16[64,1536]{1,0:T(8,128)(2,1)S(1)} %collective-permute-done.4.onward_ref, bf16[192,384]{1,0:T(8,128)(2,1)S(1)} %get-tuple-element.45.refs_0_, ...), custom_call_target="tpu_custom_call" | custom-call | flops 452984832 | bytes 4030464 | tf_op jit(solution)/shard_map/pallas_call | solution.py:41
Async XLA Ops:
  0.6 21.6 %copy-start = (bf16[1,768,1536]{2,1,0:T(8,128)(2,1)S(1)}, bf16[1,768,1536]{2,1,0:T(8,128)(2,1)}, u32[]{:S(2)}) copy-start(bf16[1,768,1536]{2,1,0:T(8,128)(2,1)} %param.13) | copy-start | bytes 7077892
  20.6 14.7 %collective-permute-start.1 = (bf16[64,1536]{1,0:T(8,128)(2,1)S(1)}, bf16[64,1536]{1,0:T(8,128)(2,1)}, u32[]{:S(2)}, u32[]{:S(2)}) collective-permute-start(bf16[64,1536]{1,0:T(8,128)(2,1)S(1)} %get-tuple-element.31.x_ref), channel_id=1, source_target_pairs={{0,1},{1,0},{2,3},{3,2},{4,5},{5,4},{6,7},{7,6},{8,9},{9,8},{10,11... | collective-permute-start | bytes 589832 | tf_op jit(solution)/shard_map/ppermute | solution.py:328
  24.6 23.2 %copy-start.1 = (bf16[64,2688]{1,0:T(8,128)(2,1)S(1)}, bf16[64,2688]{1,0:T(8,128)(2,1)}, u32[]{:S(2)}) copy-start(bf16[64,2688]{1,0:T(8,128)(2,1)} %get-tuple-element.43.refs_2_) | copy-start | bytes 1032196
  24.6 10.7 %collective-permute-start.2 = (bf16[64,1152]{1,0:T(8,128)(2,1)S(1)}, bf16[64,1152]{1,0:T(8,128)(2,1)S(1)}, u32[]{:S(2)}, u32[]{:S(2)}) collective-permute-start(bf16[64,1152]{1,0:T(8,128)(2,1)S(1)} %get-tuple-element.33), channel_id=1, source_target_pairs={{0,1},{1,0},{2,3},{3,2},{4,5},{5,4},{6,7},{7,6},{8,9},{9,8},{10,11... | collective-permute-start | bytes 442376 | tf_op jit(solution)/shard_map/ppermute | solution.py:330
  25.1 17.2 %collective-permute-start.5 = (bf16[64,1536]{1,0:T(8,128)(2,1)S(1)}, bf16[64,1536]{1,0:T(8,128)(2,1)S(1)}, u32[]{:S(2)}, u32[]{:S(2)}) collective-permute-start(bf16[64,1536]{1,0:T(8,128)(2,1)S(1)} %get-tuple-element.31.x_ref), channel_id=1, source_target_pairs={{0,2},{2,0},{1,3},{3,1},{4,6},{6,4},{5,7},{7,5},{8,10},{10,8},{9,1... | collective-permute-start | bytes 589832 | tf_op jit(solution)/shard_map/ppermute | solution.py:327
  27.7 18.8 %collective-permute-start.3 = (bf16[64,1536]{1,0:T(8,128)(2,1)}, bf16[64,1536]{1,0:T(8,128)(2,1)S(1)}, u32[]{:S(2)}, u32[]{:S(2)}) collective-permute-start(bf16[64,1536]{1,0:T(8,128)(2,1)} %get-tuple-element.40), channel_id=1, source_target_pairs={{0,2},{2,0},{1,3},{3,1},{4,6},{6,4},{5,7},{7,5},{8,10},{10,8},{9,1... | collective-permute-start | bytes 589832 | tf_op jit(solution)/shard_map/ppermute | solution.py:329
  35.3 17.7 %all-to-all-start.1 = ((bf16[8,16,1664]{2,1,0:T(8,128)(2,1)}), bf16[8,16,1664]{2,1,0:T(8,128)(2,1)S(1)}, u32[]{:S(2)}, u32[]{:S(2)}) async-start(bf16[8,16,1664]{2,1,0:T(8,128)(2,1)} %bitcast.10), calls=%async_computation.1 | async-start | bytes 851968 | tf_op jit(solution)/shard_map/all_to_all | solution.py:260
  38.8 13.2 %collective-permute-start = (bf16[64,2688]{1,0:T(8,128)(2,1)}, bf16[64,2688]{1,0:T(8,128)(2,1)S(1)}, u32[]{:S(2)}, u32[]{:S(2)}) collective-permute-start(bf16[64,2688]{1,0:T(8,128)(2,1)} %get-tuple-element.32), channel_id=1, source_target_pairs={{1,2},{2,1},{5,6},{6,5},{9,10},{10,9},{13,14},{14,13},{17,18},{18,... | collective-permute-start | bytes 1032200 | tf_op jit(solution)/shard_map/ppermute | solution.py:346
  42.3 9.8 %collective-permute-start.6 = (bf16[64,1536]{1,0:T(8,128)(2,1)S(1)}, bf16[64,1536]{1,0:T(8,128)(2,1)S(1)}, u32[]{:S(2)}, u32[]{:S(2)}) collective-permute-start(bf16[64,1536]{1,0:T(8,128)(2,1)S(1)} %collective-permute-done.5.refs_1_), channel_id=1, source_target_pairs={{1,0},{2,3},{5,4},{6,7},{9,8},{10,11},{13,12},{14,15},{17,16},{18,... | collective-permute-start | bytes 589832 | tf_op jit(solution)/shard_map/ppermute | solution.py:347
  46.5 8.0 %collective-permute-start.4 = (bf16[64,1536]{1,0:T(8,128)(2,1)S(1)}, bf16[64,1536]{1,0:T(8,128)(2,1)S(1)}, u32[]{:S(2)}, u32[]{:S(2)}) collective-permute-start(bf16[64,1536]{1,0:T(8,128)(2,1)S(1)} %collective-permute-done.3.refs_4_), channel_id=1, source_target_pairs={{1,0},{2,3},{5,4},{6,7},{9,8},{10,11},{13,12},{14,15},{17,16},{18,... | collective-permute-start | bytes 589832 | tf_op jit(solution)/shard_map/ppermute | solution.py:348
  47.8 5.3 %copy-start.2 = (s32[1,1,8,16]{3,2,1,0:T(8,128)S(1)}, s32[1,1,8,16]{3,2,1,0:T(8,128)}, u32[]{:S(2)}) copy-start(s32[1,1,8,16]{3,2,1,0:T(8,128)} %param.9) | copy-start | bytes 1540
  47.8 5.3 %copy-start.3 = (bf16[1,1,8,16]{3,2,1,0:T(8,128)(2,1)S(1)}, bf16[1,1,8,16]{3,2,1,0:T(8,128)(2,1)}, u32[]{:S(2)}) copy-start(bf16[1,1,8,16]{3,2,1,0:T(8,128)(2,1)} %param.11) | copy-start | bytes 772
  47.8 5.3 %copy-start.4 = (s32[1,1,8]{2,1,0:T(1,128)S(1)}, s32[1,1,8]{2,1,0:T(1,128)}, u32[]{:S(2)}) copy-start(s32[1,1,8]{2,1,0:T(1,128)} %param.10) | copy-start | bytes 100

commit v4 on v3

--- a/solution.py
+++ b/solution.py
@@ -90,7 +90,6 @@
     hot = token_hot(rows_ref, peer_hot, k_hot, tokens_ref.shape[0]).astype(BF16)
     used = used_column(counts_ref[...], peer_hot, most)
     gate = jnp.where(used, slot_column(gates_ref[...], peer_hot, k_hot), 0.0)
-    out_ref[:, 2 * width :] = jnp.broadcast_to(jnp.where(used, 1.0, 0.0), (slots, LANES)).astype(BF16)
     copies[3].wait()
     out_ref[:, :width] = dot_nn(hot, tokens_ref[...]).astype(BF16)
     copies[4].wait()
@@ -109,7 +108,9 @@
 
 def pack_rows(arrived_ref, x_ref, pack_ref):
     width = x_ref.shape[1]
-    pack = pack_matrix(arrived_ref[:, 2 * width :])
+    size = jnp.max(jnp.abs(arrived_ref[:, width:]), axis=1, keepdims=True).astype(F32)
+    flags = jnp.broadcast_to(jnp.where(size > 0.0, 1.0, 0.0), (arrived_ref.shape[0], LANES))
+    pack = pack_matrix(flags.astype(BF16))
     pack_ref[...] = pack
     x_ref[...] = dot_nn(pack, arrived_ref[:, :width]).astype(BF16)
 
@@ -240,7 +241,7 @@
 
 def grads(middle_ref, onward_ref, *refs):
     first, third = refs[:4], refs[4:8]
-    in_ref, down_ref, x_share, s_share, hidden, in_rows = refs[8:]
+    in_hbm, down_hbm, x_share, s_share, hidden, in_rows, in_ref, down_ref, sems = refs[8:]
     inner, most, share = hidden.shape[1], 3 * USED, x_share.shape[1]
     for whole, part in zip((x_share, s_share, hidden, in_rows), first):
         whole[:most, :] = part[...]
@@ -249,10 +250,18 @@
     hidden[most:, :] = third_hidden_ref[...]
     s_share[most:, :] = middle_ref[:, inner : inner + share] + onward_ref[:, inner + share :]
     grad = (middle_ref[:, :inner] + onward_ref[:, :inner]).astype(F32)
-    in_rows[most:, :inner] = (grad * gate_factor_ref[...]).astype(BF16)
-    in_rows[most:, inner:] = (grad * up_factor_ref[...]).astype(BF16)
+    copies = []
+    for place, factor_ref in enumerate((gate_factor_ref, up_factor_ref)):
+        half = pl.ds(place * inner, inner)
+        in_rows[most:, half] = (grad * factor_ref[...]).astype(BF16)
+        in_ref[:, half] = dot_tn(x_share[...], in_rows[:, half]).astype(BF16)
+        copies.append(pltpu.make_async_copy(in_ref.at[:, half], in_hbm.at[:, half], sems.at[place]))
+        copies[-1].start()
     down_ref[...] = dot_tn(hidden[...], s_share[...]).astype(BF16)
-    in_ref[...] = dot_tn(x_share[...], in_rows[...]).astype(BF16)
+    copies.append(pltpu.make_async_copy(down_ref, down_hbm, sems.at[2]))
+    copies[-1].start()
+    for copy in copies:
+        copy.wait()
 
 
 def to_experts(block, peers):
@@ -284,7 +293,7 @@
     picked = (rows, count, gates, tokens, cot)
     (sent,) = call(
         pick_rows,
-        [shape((slots, 2 * width + LANES), BF16)],
+        [shape((slots, 2 * width), BF16)],
         [pltpu.with_memory_space_constraint(a, pltpu.HBM) for a in picked],
         4 * slots * n_tokens * width,
         [hbm] * 5,
@@ -326,7 +335,6 @@
         own, near_load, far_load, middle_load = loads
         x_far = lax.ppermute(x_rows, "dp", FAR)
         x_near = lax.ppermute(x_rows, "dp", NEAR)
-        far = lax.ppermute(far_load, "dp", FAR)
         near = lax.ppermute(near_load, "dp", NEAR)
     parts = 4
     (sent_back,) = call(
@@ -339,10 +347,11 @@
         16,
     )
     if on_line:
-        x_near, near, sent_back = lax.optimization_barrier((x_near, near, sent_back))
+        far_load, sent_back = lax.optimization_barrier((far_load, sent_back))
+        far = lax.ppermute(far_load, "dp", FAR)
+        x_near, near, x_far, sent_back = lax.optimization_barrier((x_near, near, x_far, sent_back))
     back = to_experts(sent_back, peers)
     if on_line:
-        x_far, sent_back = lax.optimization_barrier((x_far, sent_back))
         middle = lax.ppermute(middle_load, "dp", MIDDLE)
         x_onward = lax.ppermute(x_far, "dp", ONWARD)
         onward = lax.ppermute(far, "dp", ONWARD)
@@ -397,8 +406,12 @@
                 pltpu.VMEM((everyone, share), BF16),
                 pltpu.VMEM((everyone, inner), BF16),
                 pltpu.VMEM((everyone, 2 * inner), BF16),
+                pltpu.VMEM((share, 2 * inner), BF16),
+                pltpu.VMEM((inner, share), BF16),
+                pltpu.SemaphoreType.DMA((3,)),
             ],
             16,
+            [hbm] * 2,
         )
     else:
         x_all = lax.all_gather(x_rows, "dp", axis=0, tiled=True)

time: 57.1 us -> 55.3 us (0.968); the launches traced: 56.2 us -> 55 us
  waiting for transfers between devices: 7.94 us -> 7.09 us
    ppermute x1, waiting for transfers between devices: 2.77 us -> 0.01 us  [on_device(): x_far = lax.ppermute(x_rows, 'dp', FAR)]
    ppermute x1, waiting for transfers between devices: 0.01 us -> 1.3 us  [on_device(): onward = lax.ppermute(far, 'dp', ONWARD)]
    ppermute x1, waiting for transfers between devices: 0.01 us -> 1.12 us  [on_device(): x_onward = lax.ppermute(x_far, 'dp', ONWARD)]
    ppermute x1, waiting for transfers between devices: 2.24 us -> 1.26 us  [on_device(): near = lax.ppermute(near_load, 'dp', NEAR)]
  transfers between devices with their start and end apart: 8 -> 8, of which waited for: 3 -> 4; matrix products, arithmetic and copies ran while one was open for 0% -> 0% of each run, Pallas kernels for 25% -> 25%
where the time goes in v4:
time: 55.3 us; the launch traced here: 55 us
  Pallas kernels  17.7 us (32%)
  blocking collectives  17.5 us (32%)
  starting transfers between devices  11.9 us (22%)
  waiting for transfers between devices  7.09 us (13%)
  between operations  0.8 us (1%)
    pallas_call x8, Pallas kernels, call(): pl.pallas_call(body, out_shape=tuple(outs), in_specs=in_specs or [pl.Bloc...  17.7 us
    all_to_all x1, blocking collectives, to_experts(): lax.all_to_all(block.reshape(peers, slots // peers, width), 'expert', spl...  17.5 us
    all_to_all x1, starting transfers between devices, to_experts(): lax.all_to_all(block.reshape(peers, slots // peers, width), 'expert', spl...  3.47 us
    ppermute x1, waiting for transfers between devices, on_device(): far = lax.ppermute(far_load, 'dp', FAR)  3.4 us
    ppermute x1, starting transfers between devices, on_device(): x_far = lax.ppermute(x_rows, 'dp', FAR)  2.59 us
    ppermute x1, starting transfers between devices, on_device(): x_near = lax.ppermute(x_rows, 'dp', NEAR)  1.64 us
    ppermute x1, waiting for transfers between devices, on_device(): onward = lax.ppermute(far, 'dp', ONWARD)  1.3 us
    ppermute x1, starting transfers between devices, on_device(): x_onward = lax.ppermute(x_far, 'dp', ONWARD)  1.29 us
  transfers between devices with their start and end apart: 8, of which 4 were waited for; matrix products, arithmetic and copies ran while one was open for 0% of the time, Pallas kernels for 25%

profile of v4, /device:TPU:0, one launch (start us, length us, event | category | flops | bytes accessed | tf_op | source)
XLA Modules:
  0.0 55.0 jit_solution(2872380910985093144)
XLA Ops:
  0.6 0.0 copy-start
  0.6 1.7 %shard_map.102 = bf16[128,3072]{1,0:T(8,128)(2,1)S(1)} custom-call(s32[8,16]{1,0:T(8,128)} %bitcast.21, s32[1,8]{1,0:T(1,128)} %bitcast.25, bf16[8,16]{1,0:T(8,128)(2,1)} %bitcast.23, bf16[128,1536]{1,0:T(8,128)(2,1)} %bitcast.29, bf16[128,1536]{1,0:T(8,128)(2,1)} %bitcast.30), custom_call_target="tpu_custom_call" | custom-call | flops 100663296 | bytes 1573664 | tf_op jit(solution)/shard_map/pallas_call | solution.py:41
  2.4 17.5 %all_to_all.10 = bf16[8,16,3072]{2,1,0:T(8,128)(2,1)S(1)} all-to-all(bf16[8,16,3072]{2,1,0:T(8,128)(2,1)S(1)} %bitcast.18), channel_id=1, replica_groups=mesh['expert'=8,'dp'=4] {'expert'}, dimensions={0} | all-to-all | bytes 1572864 | tf_op jit(solution)/shard_map/all_to_all | solution.py:269
  19.9 0.5 shard_map.103
  20.4 1.6 %collective-permute-start.1 = (bf16[64,1536]{1,0:T(8,128)(2,1)S(1)}, bf16[64,1536]{1,0:T(8,128)(2,1)}, u32[]{:S(2)}, u32[]{:S(2)}) collective-permute-start(bf16[64,1536]{1,0:T(8,128)(2,1)S(1)} %get-tuple-element.33.x_ref), channel_id=1, source_target_pairs={{0,1},{1,0},{2,3},{3,2},{4,5},{5,4},{6,7},{7,6},{8,9},{9,8},{10,11... | collective-permute-start | bytes 589832 | tf_op jit(solution)/shard_map/ppermute | solution.py:337
  22.0 2.6 %collective-permute-start.3 = (bf16[64,1536]{1,0:T(8,128)(2,1)S(1)}, bf16[64,1536]{1,0:T(8,128)(2,1)S(1)}, u32[]{:S(2)}, u32[]{:S(2)}) collective-permute-start(bf16[64,1536]{1,0:T(8,128)(2,1)S(1)} %get-tuple-element.33.x_ref), channel_id=1, source_target_pairs={{0,2},{2,0},{1,3},{3,1},{4,6},{6,4},{5,7},{7,5},{8,10},{10,8},{9,1... | collective-permute-start | bytes 589832 | tf_op jit(solution)/shard_map/ppermute | solution.py:336
  24.6 0.0 copy-done
  24.6 2.3 %shard_map.104 = (f32[64,768]{1,0:T(8,128)S(1)}, bf16[64,2688]{1,0:T(8,128)(2,1)}, bf16[64,1152]{1,0:T(8,128)(2,1)S(1)}, bf16[64,1536]{1,0:T(8,128)(2,1)}, bf16[64,2688]{1,0:T(8,128)(2,1)}) custom-call(s32[1]{0:T(128)} %bitcast.index_ref.refs_5_, bf16[128,3072]{1,0:T(8,128)(2,1)S(1)} %bitcast.17, bf16[64,128]{1,0:T(8,128)(2,1)S(1)} %get-tuple-element.32.pack_ref, ...), custom_call_target="tpu_custom_call" | custom-call | flops 176160768 | bytes 4587524 | tf_op jit(solution)/shard_map/pallas_call | solution.py:41
  26.9 0.0 copy-start.1
  26.9 0.5 collective-permute-start.2
  27.4 5.1 %shard_map.105 = bf16[128,1664]{1,0:T(8,128)(2,1)} custom-call(bf16[64,1536]{1,0:T(8,128)(2,1)S(1)} %get-tuple-element.33.x_ref, f32[64,768]{1,0:T(8,128)S(1)} %get-tuple-element.37.grad_ref, bf16[64,128]{1,0:T(8,128)(2,1)S(1)} %get-tuple-element.32.pack_ref, bf16[1536,1536]{1,0:T(8,128)(2,1)} %bitcast.27), custom_call_target="tpu_custom_call" | custom-call | flops 603979776 | bytes 5554176 | tf_op jit(solution)/shard_map/pallas_call | solution.py:41
  32.5 0.4 collective-permute-start.4
  32.9 1.3 %collective-permute-done.2.refs_3_ = bf16[64,1152]{1,0:T(8,128)(2,1)S(1)} collective-permute-done((bf16[64,1152]{1,0:T(8,128)(2,1)S(1)}, bf16[64,1152]{1,0:T(8,128)(2,1)S(1)}, u32[]{:S(2)}, u32[]{:S(2)}) %collective-permute-start.2) | collective-permute-done | bytes 147488 | tf_op jit(solution)/shard_map/ppermute | solution.py:338
  34.2 0.0 collective-permute-done.1.refs_0_
  34.2 0.0 collective-permute-done.3.refs_1_
  34.2 3.5 %all-to-all-start.1 = ((bf16[8,16,1664]{2,1,0:T(8,128)(2,1)}), bf16[8,16,1664]{2,1,0:T(8,128)(2,1)S(1)}, u32[]{:S(2)}, u32[]{:S(2)}) async-start(bf16[8,16,1664]{2,1,0:T(8,128)(2,1)} %bitcast.10), calls=%async_computation.1 | async-start | bytes 851968 | tf_op jit(solution)/shard_map/all_to_all | solution.py:269
  37.7 0.7 %collective-permute-start = (bf16[64,2688]{1,0:T(8,128)(2,1)}, bf16[64,2688]{1,0:T(8,128)(2,1)S(1)}, u32[]{:S(2)}, u32[]{:S(2)}) collective-permute-start(bf16[64,2688]{1,0:T(8,128)(2,1)} %get-tuple-element.34), channel_id=1, source_target_pairs={{1,2},{2,1},{5,6},{6,5},{9,10},{10,9},{13,14},{14,13},{17,18},{18,... | collective-permute-start | bytes 1032200 | tf_op jit(solution)/shard_map/ppermute | solution.py:355
  38.3 1.3 %collective-permute-start.6 = (bf16[64,1536]{1,0:T(8,128)(2,1)S(1)}, bf16[64,1536]{1,0:T(8,128)(2,1)S(1)}, u32[]{:S(2)}, u32[]{:S(2)}) collective-permute-start(bf16[64,1536]{1,0:T(8,128)(2,1)S(1)} %collective-permute-done.3.refs_1_), channel_id=1, source_target_pairs={{1,0},{2,3},{5,4},{6,7},{9,8},{10,11},{13,12},{14,15},{17,16},{18,... | collective-permute-start | bytes 589832 | tf_op jit(solution)/shard_map/ppermute | solution.py:356
  39.6 3.4 %collective-permute-done.4.refs_4_ = bf16[64,1536]{1,0:T(8,128)(2,1)S(1)} collective-permute-done((bf16[64,1536]{1,0:T(8,128)(2,1)}, bf16[64,1536]{1,0:T(8,128)(2,1)S(1)}, u32[]{:S(2)}, u32[]{:S(2)}) %collective-permute-start.4) | collective-permute-done | bytes 196640 | tf_op jit(solution)/shard_map/ppermute | solution.py:351
  43.0 1.3 %collective-permute-start.5 = (bf16[64,1536]{1,0:T(8,128)(2,1)S(1)}, bf16[64,1536]{1,0:T(8,128)(2,1)S(1)}, u32[]{:S(2)}, u32[]{:S(2)}) collective-permute-start(bf16[64,1536]{1,0:T(8,128)(2,1)S(1)} %collective-permute-done.4.refs_4_), channel_id=1, source_target_pairs={{1,0},{2,3},{5,4},{6,7},{9,8},{10,11},{13,12},{14,15},{17,16},{18,... | collective-permute-start | bytes 589832 | tf_op jit(solution)/shard_map/ppermute | solution.py:357
  44.3 0.0 copy-done.1
  44.3 0.0 copy-start.2
  44.4 0.0 copy-start.3
  44.4 0.0 copy-start.4
  44.4 4.2 %shard_map.107 = (bf16[1536,1536]{1,0:T(8,128)(2,1)S(1)}, bf16[192,384]{1,0:T(8,128)(2,1)S(1)}, bf16[192,384]{1,0:T(8,128)(2,1)S(1)}, bf16[192,768]{1,0:T(8,128)(2,1)S(1)}, bf16[192,1536]{1,0:T(8,128)(2,1)S(1)}) custom-call(bf16[64,1536]{1,0:T(8,128)(2,1)} %collective-permute-done.1.refs_0_, bf16[64,1536]{1,0:T(8,128)(2,1)S(1)} %collective-permute-done.3.refs_1_, ...), custom_call_target="tpu_custom_call" | custom-call | flops 905969664 | bytes 11698180 | tf_op jit(solution)/shard_map/pallas_call | solution.py:41
  48.6 0.0 collective-permute-done.middle_ref
  48.6 1.1 %collective-permute-done.6.onward_ref = bf16[64,1536]{1,0:T(8,128)(2,1)S(1)} collective-permute-done((bf16[64,1536]{1,0:T(8,128)(2,1)S(1)}, bf16[64,1536]{1,0:T(8,128)(2,1)S(1)}, u32[]{:S(2)}, u32[]{:S(2)}) %collective-permute-start.6) | collective-permute-done | bytes 196640 | tf_op jit(solution)/shard_map/ppermute | solution.py:356
  49.7 0.9 %shard_map.108 = (bf16[64,384]{1,0:T(8,128)(2,1)S(1)}, bf16[64,768]{1,0:T(8,128)(2,1)S(1)}, f32[64,768]{1,0:T(8,128)S(1)}, f32[64,768]{1,0:T(8,128)S(1)}) custom-call(bf16[64,2688]{1,0:T(8,128)(2,1)S(1)} %collective-permute-done.middle_ref, bf16[64,1536]{1,0:T(8,128)(2,1)S(1)} %collective-permute-done.6.onward_ref, s32[1]{0:T(128)} %bitcast.index_ref.refs_5_, ...), custom_call_target="tpu_custom_call" | custom-call | flops 301989888 | bytes 5799940 | tf_op jit(solution)/shard_map/pallas_call | solution.py:41
  50.7 0.0 all-to-all-done.1
  50.7 0.0 copy-done.2
  50.7 0.0 copy-done.3
  50.7 0.0 copy-done.4
  50.7 1.4 %shard_map.106 = (bf16[128,1536]{1,0:T(8,128)(2,1)}, bf16[8,16]{1,0:T(8,128)(2,1)}) custom-call(s32[8,16]{1,0:T(8,128)S(1)} %bitcast.22, s32[1,8]{1,0:T(1,128)S(1)} %bitcast.26, bf16[8,16]{1,0:T(8,128)(2,1)S(1)} %bitcast.24, bf16[128,1664]{1,0:T(8,128)(2,1)S(1)} %bitcast.20), custom_call_target="tpu_custom_call" | custom-call | flops 50331648 | bytes 820256 | tf_op jit(solution)/shard_map/pallas_call | solution.py:41
  52.1 1.3 %collective-permute-done.5.onward_ref = bf16[64,1536]{1,0:T(8,128)(2,1)S(1)} collective-permute-done((bf16[64,1536]{1,0:T(8,128)(2,1)S(1)}, bf16[64,1536]{1,0:T(8,128)(2,1)S(1)}, u32[]{:S(2)}, u32[]{:S(2)}) %collective-permute-start.5) | collective-permute-done | bytes 196640 | tf_op jit(solution)/shard_map/ppermute | solution.py:357
  53.4 1.6 %shard_map.109 = (bf16[384,1536]{1,0:T(8,128)(2,1)}, bf16[768,384]{1,0:T(8,128)(2,1)}) custom-call(bf16[64,2688]{1,0:T(8,128)(2,1)S(1)} %collective-permute-done.middle_ref, bf16[64,1536]{1,0:T(8,128)(2,1)S(1)} %collective-permute-done.5.onward_ref, bf16[192,384]{1,0:T(8,128)(2,1)S(1)} %get-tuple-element.49.refs_0_, ...), custom_call_target="tpu_custom_call" | custom-call | flops 452984832 | bytes 4030464 | tf_op jit(solution)/shard_map/pallas_call | solution.py:41
Async XLA Ops:
  0.6 24.0 %copy-start = (bf16[1,768,1536]{2,1,0:T(8,128)(2,1)S(1)}, bf16[1,768,1536]{2,1,0:T(8,128)(2,1)}, u32[]{:S(2)}) copy-start(bf16[1,768,1536]{2,1,0:T(8,128)(2,1)} %param.13) | copy-start | bytes 7077892
  20.4 13.8 %collective-permute-start.1 = (bf16[64,1536]{1,0:T(8,128)(2,1)S(1)}, bf16[64,1536]{1,0:T(8,128)(2,1)}, u32[]{:S(2)}, u32[]{:S(2)}) collective-permute-start(bf16[64,1536]{1,0:T(8,128)(2,1)S(1)} %get-tuple-element.33.x_ref), channel_id=1, source_target_pairs={{0,1},{1,0},{2,3},{3,2},{4,5},{5,4},{6,7},{7,6},{8,9},{9,8},{10,11... | collective-permute-start | bytes 589832 | tf_op jit(solution)/shard_map/ppermute | solution.py:337
  22.0 12.2 %collective-permute-start.3 = (bf16[64,1536]{1,0:T(8,128)(2,1)S(1)}, bf16[64,1536]{1,0:T(8,128)(2,1)S(1)}, u32[]{:S(2)}, u32[]{:S(2)}) collective-permute-start(bf16[64,1536]{1,0:T(8,128)(2,1)S(1)} %get-tuple-element.33.x_ref), channel_id=1, source_target_pairs={{0,2},{2,0},{1,3},{3,1},{4,6},{6,4},{5,7},{7,5},{8,10},{10,8},{9,1... | collective-permute-start | bytes 589832 | tf_op jit(solution)/shard_map/ppermute | solution.py:336
  26.9 17.4 %copy-start.1 = (bf16[64,2688]{1,0:T(8,128)(2,1)S(1)}, bf16[64,2688]{1,0:T(8,128)(2,1)}, u32[]{:S(2)}) copy-start(bf16[64,2688]{1,0:T(8,128)(2,1)} %get-tuple-element.47.refs_2_) | copy-start | bytes 1032196
  26.9 7.3 %collective-permute-start.2 = (bf16[64,1152]{1,0:T(8,128)(2,1)S(1)}, bf16[64,1152]{1,0:T(8,128)(2,1)S(1)}, u32[]{:S(2)}, u32[]{:S(2)}) collective-permute-start(bf16[64,1152]{1,0:T(8,128)(2,1)S(1)} %get-tuple-element.35), channel_id=1, source_target_pairs={{0,1},{1,0},{2,3},{3,2},{4,5},{5,4},{6,7},{7,6},{8,9},{9,8},{10,11... | collective-permute-start | bytes 442376 | tf_op jit(solution)/shard_map/ppermute | solution.py:338
  32.5 10.5 %collective-permute-start.4 = (bf16[64,1536]{1,0:T(8,128)(2,1)}, bf16[64,1536]{1,0:T(8,128)(2,1)S(1)}, u32[]{:S(2)}, u32[]{:S(2)}) collective-permute-start(bf16[64,1536]{1,0:T(8,128)(2,1)} %get-tuple-element.44), channel_id=1, source_target_pairs={{0,2},{2,0},{1,3},{3,1},{4,6},{6,4},{5,7},{7,5},{8,10},{10,8},{9,1... | collective-permute-start | bytes 589832 | tf_op jit(solution)/shard_map/ppermute | solution.py:351
  34.2 16.5 %all-to-all-start.1 = ((bf16[8,16,1664]{2,1,0:T(8,128)(2,1)}), bf16[8,16,1664]{2,1,0:T(8,128)(2,1)S(1)}, u32[]{:S(2)}, u32[]{:S(2)}) async-start(bf16[8,16,1664]{2,1,0:T(8,128)(2,1)} %bitcast.10), calls=%async_computation.1 | async-start | bytes 851968 | tf_op jit(solution)/shard_map/all_to_all | solution.py:269
  37.7 11.0 %collective-permute-start = (bf16[64,2688]{1,0:T(8,128)(2,1)}, bf16[64,2688]{1,0:T(8,128)(2,1)S(1)}, u32[]{:S(2)}, u32[]{:S(2)}) collective-permute-start(bf16[64,2688]{1,0:T(8,128)(2,1)} %get-tuple-element.34), channel_id=1, source_target_pairs={{1,2},{2,1},{5,6},{6,5},{9,10},{10,9},{13,14},{14,13},{17,18},{18,... | collective-permute-start | bytes 1032200 | tf_op jit(solution)/shard_map/ppermute | solution.py:355
  38.3 11.4 %collective-permute-start.6 = (bf16[64,1536]{1,0:T(8,128)(2,1)S(1)}, bf16[64,1536]{1,0:T(8,128)(2,1)S(1)}, u32[]{:S(2)}, u32[]{:S(2)}) collective-permute-start(bf16[64,1536]{1,0:T(8,128)(2,1)S(1)} %collective-permute-done.3.refs_1_), channel_id=1, source_target_pairs={{1,0},{2,3},{5,4},{6,7},{9,8},{10,11},{13,12},{14,15},{17,16},{18,... | collective-permute-start | bytes 589832 | tf_op jit(solution)/shard_map/ppermute | solution.py:356
  43.0 10.4 %collective-permute-start.5 = (bf16[64,1536]{1,0:T(8,128)(2,1)S(1)}, bf16[64,1536]{1,0:T(8,128)(2,1)S(1)}, u32[]{:S(2)}, u32[]{:S(2)}) collective-permute-start(bf16[64,1536]{1,0:T(8,128)(2,1)S(1)} %collective-permute-done.4.refs_4_), channel_id=1, source_target_pairs={{1,0},{2,3},{5,4},{6,7},{9,8},{10,11},{13,12},{14,15},{17,16},{18,... | collective-permute-start | bytes 589832 | tf_op jit(solution)/shard_map/ppermute | solution.py:357
  44.3 6.4 %copy-start.2 = (s32[1,1,8,16]{3,2,1,0:T(8,128)S(1)}, s32[1,1,8,16]{3,2,1,0:T(8,128)}, u32[]{:S(2)}) copy-start(s32[1,1,8,16]{3,2,1,0:T(8,128)} %param.9) | copy-start | bytes 1540
  44.4 6.4 %copy-start.3 = (bf16[1,1,8,16]{3,2,1,0:T(8,128)(2,1)S(1)}, bf16[1,1,8,16]{3,2,1,0:T(8,128)(2,1)}, u32[]{:S(2)}) copy-start(bf16[1,1,8,16]{3,2,1,0:T(8,128)(2,1)} %param.11) | copy-start | bytes 772
  44.4 6.4 %copy-start.4 = (s32[1,1,8]{2,1,0:T(1,128)S(1)}, s32[1,1,8]{2,1,0:T(1,128)}, u32[]{:S(2)}) copy-start(s32[1,1,8]{2,1,0:T(1,128)} %param.10) | copy-start | bytes 100

commit v5 on v4

--- a/solution.py
+++ b/solution.py
@@ -115,32 +115,17 @@
     x_ref[...] = dot_nn(pack, arrived_ref[:, :width]).astype(BF16)
 
 
-def own_hidden_grad(share, index_ref, arrived_ref, pack_ref, x_ref, w_down_ref, grad_ref, *refs):
-    *load_refs, scaled_ref, own_ref, middle_ref, sems = refs
+def own_hidden_grad(share, index_ref, arrived_ref, pack_ref, _, w_down_ref, grad_ref, *refs):
+    *load_refs, scaled_ref = refs
     inner, width = w_down_ref.shape
-    copies = []
-    if load_refs:
-        own_hbm, near_ref, far_ref, middle_hbm = load_refs
-        for place, target in enumerate((own_hbm, middle_hbm)):
-            x_part = target.at[:, pl.ds(inner + share, width)]
-            copies.append(pltpu.make_async_copy(x_ref, x_part, sems.at[place]))
-            copies[-1].start()
     scaled_ref[...] = dot_nn(pack_ref[...], arrived_ref[:, width : 2 * width]).astype(BF16)
     hidden_grad = dot_nt(scaled_ref[...], w_down_ref[...])
     grad_ref[...] = hidden_grad
-    if not load_refs:
-        return
-    for place, (load_ref, steps) in enumerate(zip((own_ref, middle_ref, near_ref, far_ref), LOADS)):
+    for load_ref, steps in zip(load_refs, LOADS):
         load_ref[:, :inner] = hidden_grad.astype(BF16)
         for part, step in enumerate(steps):
             start = pl.multiple_of((index_ref[0] ^ step) * share, LANES)
             load_ref[:, pl.ds(inner + part * share, share)] = scaled_ref[:, pl.ds(start, share)]
-        if place < 2:
-            load_part = (own_hbm, middle_hbm)[place].at[:, pl.ds(0, inner + share)]
-            copies.append(pltpu.make_async_copy(load_ref, load_part, sems.at[2 + place]))
-            copies[-1].start()
-    for copy in copies:
-        copy.wait()
 
 
 def activations(pre, inner):
@@ -173,10 +158,19 @@
     return total
 
 
-def own_rows(x_ref, grad_ref, pack_ref, w_in_hbm, out_ref, w_in_ref, sems):
+def own_rows(x_ref, grad_ref, pack_ref, w_in_hbm, *refs):
+    *load_refs, w_in_ref, sems, load_sems = refs
+    count = len(load_refs) // 2
+    out_ref = load_refs[count]
     inner = grad_ref.shape[1]
     width = w_in_ref.shape[0]
     copies = start_parts(w_in_hbm, w_in_ref, sems)
+    moves = []
+    for load_ref, target in zip(load_refs[:count], load_refs[count + 1 :]):
+        size = load_ref.shape[1]
+        for source, span in ((load_ref, pl.ds(0, size)), (x_ref, pl.ds(size, width))):
+            moves.append(pltpu.make_async_copy(source, target.at[:, span], load_sems.at[len(moves)]))
+            moves[-1].start()
     hidden_grad = grad_ref[...]
     hidden, gate_factor, up_factor = activations(project(x_ref, w_in_ref, copies), inner)
     gate_rows = (hidden_grad * gate_factor).astype(BF16)
@@ -192,6 +186,8 @@
     pack = pack_ref[...]
     out_ref[:, :width] = dot_tn(pack, slot_grad).astype(BF16)
     out_ref[:, width:] = dot_tn(pack, tail).astype(BF16)
+    for move in moves:
+        move.wait()
 
 
 def combine_tokens(rows_ref, counts_ref, gates_ref, back_ref, token_ref, gate_ref):
@@ -313,10 +309,10 @@
         functools.partial(own_hidden_grad, share),
         [shape((USED, inner), F32)]
         + [
-            pltpu.HBM((USED, short + width), BF16),
+            shape((USED, short), BF16),
+            shape((USED, short), BF16),
             shape((USED, short), BF16),
             shape((USED, short + share), BF16),
-            pltpu.HBM((USED, short + width), BF16),
         ]
         * on_line,
         (index, arrived, pack, x_rows, w_down),
@@ -324,34 +320,33 @@
         [smem] + [vmem] * 4,
         [
             pltpu.VMEM((USED, width), BF16),
-            pltpu.VMEM((USED, short), BF16),
-            pltpu.VMEM((USED, short), BF16),
-            pltpu.SemaphoreType.DMA((4,)),
         ],
         8,
-        [vmem] + [hbm, vmem, vmem, hbm] * on_line,
     )
     if on_line:
-        own, near_load, far_load, middle_load = loads
+        own, middle_load, near_load, far_load = loads
         x_far = lax.ppermute(x_rows, "dp", FAR)
         x_near = lax.ppermute(x_rows, "dp", NEAR)
         near = lax.ppermute(near_load, "dp", NEAR)
     parts = 4
-    (sent_back,) = call(
+    sent_back, *loads = call(
         own_rows,
-        [shape((slots, width + LANES), BF16)],
-        (x_rows, hidden_grad, pack, w_in_far),
+        [shape((slots, width + LANES), BF16)] + [pltpu.HBM((USED, short + width), BF16)] * 2 * on_line,
+        (x_rows, hidden_grad, pack, w_in_far, *loads[:2]),
         2 * USED * inner * width * 4,
-        [vmem] * 3 + [hbm],
-        [pltpu.VMEM(w_in.shape, BF16), pltpu.SemaphoreType.DMA((parts,))],
+        [vmem] * 3 + [hbm] + [vmem] * 2 * on_line,
+        [pltpu.VMEM(w_in.shape, BF16), pltpu.SemaphoreType.DMA((parts,)), pltpu.SemaphoreType.DMA((4,))],
         16,
+        [vmem] + [hbm] * 2 * on_line,
     )
     if on_line:
-        far_load, sent_back = lax.optimization_barrier((far_load, sent_back))
+        own, middle_load = loads
+    if on_line:
         far = lax.ppermute(far_load, "dp", FAR)
-        x_near, near, x_far, sent_back = lax.optimization_barrier((x_near, near, x_far, sent_back))
+        x_near, x_far, sent_back = lax.optimization_barrier((x_near, x_far, sent_back))
     back = to_experts(sent_back, peers)
     if on_line:
+        middle_load, near, sent_back = lax.optimization_barrier((middle_load, near, sent_back))
         middle = lax.ppermute(middle_load, "dp", MIDDLE)
         x_onward = lax.ppermute(x_far, "dp", ONWARD)
         onward = lax.ppermute(far, "dp", ONWARD)

time: 55.3 us -> 53.9 us (0.975)
  waiting for transfers between devices: 7.09 us -> 5.17 us
  local copies, waits for them, and re-layouts: 0.03 us -> 0.99 us
    ppermute x1, waiting for transfers between devices: 1.26 us -> 0.01 us  [on_device(): near = lax.ppermute(near_load, 'dp', NEAR)]
    unnamed x10, local copies, waits for them, and re-layouts: 0.03 us -> 0.99 us
    ppermute x1, waiting for transfers between devices: 3.4 us -> 2.6 us  [on_device(): far = lax.ppermute(far_load, 'dp', FAR)]
    ppermute x1, waiting for transfers between devices: 1.12 us -> 0.4 us  [on_device(): x_onward = lax.ppermute(x_far, 'dp', ONWARD)]
  transfers between devices with their start and end apart: 8 -> 8, of which waited for: 4 -> 5; matrix products, arithmetic and copies ran while one was open for 0% -> 0% of each run, Pallas kernels for 25% -> 25%
where the time goes in v5:
time: 53.9 us; the launch traced here: 53.6 us
  blocking collectives  17.5 us (32%)
  Pallas kernels  17.4 us (32%)
  starting transfers between devices  11.7 us (22%)
  waiting for transfers between devices  5.17 us (10%)
  local copies, waits for them, and re-layouts  0.99 us (2%)
  between operations  0.77 us (1%)
    all_to_all x1, blocking collectives, to_experts(): lax.all_to_all(block.reshape(peers, slots // peers, width), 'expert', spl...  17.5 us
    pallas_call x8, Pallas kernels, call(): pl.pallas_call(body, out_shape=tuple(outs), in_specs=in_specs or [pl.Bloc...  17.4 us
    all_to_all x1, starting transfers between devices, to_experts(): lax.all_to_all(block.reshape(peers, slots // peers, width), 'expert', spl...  3.46 us
    ppermute x1, waiting for transfers between devices, on_device(): far = lax.ppermute(far_load, 'dp', FAR)  2.6 us
    ppermute x1, starting transfers between devices, on_device(): x_far = lax.ppermute(x_rows, 'dp', FAR)  2.59 us
    ppermute x1, starting transfers between devices, on_device(): x_near = lax.ppermute(x_rows, 'dp', NEAR)  1.64 us
    ppermute x1, waiting for transfers between devices, on_device(): onward = lax.ppermute(far, 'dp', ONWARD)  1.29 us
    ppermute x1, starting transfers between devices, on_device(): x_onward = lax.ppermute(x_far, 'dp', ONWARD)  1.29 us
  transfers between devices with their start and end apart: 8, of which 5 were waited for; matrix products, arithmetic and copies ran while one was open for 0% of the time, Pallas kernels for 25%

profile of v5, /device:TPU:0, one launch (start us, length us, event | category | flops | bytes accessed | tf_op | source)
XLA Modules:
  0.0 53.6 jit_solution(6163369096854402299)
XLA Ops:
  0.6 0.0 copy-start
  0.6 1.7 %shard_map.102 = bf16[128,3072]{1,0:T(8,128)(2,1)S(1)} custom-call(s32[8,16]{1,0:T(8,128)} %bitcast.21, s32[1,8]{1,0:T(1,128)} %bitcast.25, bf16[8,16]{1,0:T(8,128)(2,1)} %bitcast.23, bf16[128,1536]{1,0:T(8,128)(2,1)} %bitcast.29, bf16[128,1536]{1,0:T(8,128)(2,1)} %bitcast.30), custom_call_target="tpu_custom_call" | custom-call | flops 100663296 | bytes 1573664 | tf_op jit(solution)/shard_map/pallas_call | solution.py:41
  2.4 17.5 %all_to_all.10 = bf16[8,16,3072]{2,1,0:T(8,128)(2,1)S(1)} all-to-all(bf16[8,16,3072]{2,1,0:T(8,128)(2,1)S(1)} %bitcast.18), channel_id=1, replica_groups=mesh['expert'=8,'dp'=4] {'expert'}, dimensions={0} | all-to-all | bytes 1572864 | tf_op jit(solution)/shard_map/all_to_all | solution.py:265
  19.9 0.5 shard_map.103
  20.4 1.6 %collective-permute-start.1 = (bf16[64,1536]{1,0:T(8,128)(2,1)S(1)}, bf16[64,1536]{1,0:T(8,128)(2,1)S(1)}, u32[]{:S(2)}, u32[]{:S(2)}) collective-permute-start(bf16[64,1536]{1,0:T(8,128)(2,1)S(1)} %get-tuple-element.34._.x_ref), channel_id=1, source_target_pairs={{0,1},{1,0},{2,3},{3,2},{4,5},{5,4},{6,7},{7,6},{8,9},{9,8},{10,11... | collective-permute-start | bytes 589832 | tf_op jit(solution)/shard_map/ppermute | solution.py:329
  22.0 2.6 %collective-permute-start.2 = (bf16[64,1536]{1,0:T(8,128)(2,1)S(1)}, bf16[64,1536]{1,0:T(8,128)(2,1)}, u32[]{:S(2)}, u32[]{:S(2)}) collective-permute-start(bf16[64,1536]{1,0:T(8,128)(2,1)S(1)} %get-tuple-element.34._.x_ref), channel_id=1, source_target_pairs={{0,2},{2,0},{1,3},{3,1},{4,6},{6,4},{5,7},{7,5},{8,10},{10,8},{9,1... | collective-permute-start | bytes 589832 | tf_op jit(solution)/shard_map/ppermute | solution.py:328
  24.6 0.0 copy-done
  24.6 1.6 %shard_map.104 = (f32[64,768]{1,0:T(8,128)S(1)}, bf16[64,1152]{1,0:T(8,128)(2,1)S(1)}, bf16[64,1152]{1,0:T(8,128)(2,1)S(1)}, bf16[64,1152]{1,0:T(8,128)(2,1)}, bf16[64,1536]{1,0:T(8,128)(2,1)}) custom-call(s32[1]{0:T(128)} %bitcast.7.index_ref.refs_5_, bf16[128,3072]{1,0:T(8,128)(2,1)S(1)} %bitcast.17, bf16[64,128]{1,0:T(8,128)(2,1)S(1)} %get-tuple-element.35.pack_ref, ...), custom_call_target="tpu_custom_call" | custom-call | flops 176160768 | bytes 4194308 | tf_op jit(solution)/shard_map/pallas_call | solution.py:41
  26.2 0.4 collective-permute-start
  26.7 0.3 collective-permute-start.4
  27.0 5.4 %shard_map.105 = (bf16[128,1664]{1,0:T(8,128)(2,1)}, bf16[64,2688]{1,0:T(8,128)(2,1)}, bf16[64,2688]{1,0:T(8,128)(2,1)}) custom-call(bf16[64,1536]{1,0:T(8,128)(2,1)S(1)} %get-tuple-element.34._.x_ref, f32[64,768]{1,0:T(8,128)S(1)} %get-tuple-element.36.grad_ref, bf16[64,128]{1,0:T(8,128)(2,1)S(1)} %get-tuple-element.35.pack_ref, ...), custom_call_target="tpu_custom_call" | custom-call | flops 603979776 | bytes 6537216 | tf_op jit(solution)/shard_map/pallas_call | solution.py:41
  32.4 0.4 collective-permute-done.1.refs_0_
  32.8 0.4 collective-permute-done.2.refs_1_
  33.2 3.5 %all-to-all-start.1 = ((bf16[8,16,1664]{2,1,0:T(8,128)(2,1)}), bf16[8,16,1664]{2,1,0:T(8,128)(2,1)S(1)}, u32[]{:S(2)}, u32[]{:S(2)}) async-start(bf16[8,16,1664]{2,1,0:T(8,128)(2,1)} %bitcast.10), calls=%async_computation.1 | async-start | bytes 851968 | tf_op jit(solution)/shard_map/all_to_all | solution.py:265
  36.7 0.0 collective-permute-done.refs_3_
  36.7 0.7 %collective-permute-start.3 = (bf16[64,2688]{1,0:T(8,128)(2,1)}, bf16[64,2688]{1,0:T(8,128)(2,1)S(1)}, u32[]{:S(2)}, u32[]{:S(2)}) collective-permute-start(bf16[64,2688]{1,0:T(8,128)(2,1)} %get-tuple-element.43), channel_id=1, source_target_pairs={{1,2},{2,1},{5,6},{6,5},{9,10},{10,9},{13,14},{14,13},{17,18},{18,... | collective-permute-start | bytes 1032200 | tf_op jit(solution)/shard_map/ppermute | solution.py:350
  37.4 1.3 %collective-permute-start.6 = (bf16[64,1536]{1,0:T(8,128)(2,1)}, bf16[64,1536]{1,0:T(8,128)(2,1)S(1)}, u32[]{:S(2)}, u32[]{:S(2)}) collective-permute-start(bf16[64,1536]{1,0:T(8,128)(2,1)} %collective-permute-done.2.refs_1_), channel_id=1, source_target_pairs={{1,0},{2,3},{5,4},{6,7},{9,8},{10,11},{13,12},{14,15},{17,16},{18,... | collective-permute-start | bytes 589832 | tf_op jit(solution)/shard_map/ppermute | solution.py:351
  38.7 2.6 %collective-permute-done.4.refs_4_ = bf16[64,1536]{1,0:T(8,128)(2,1)S(1)} collective-permute-done((bf16[64,1536]{1,0:T(8,128)(2,1)}, bf16[64,1536]{1,0:T(8,128)(2,1)S(1)}, u32[]{:S(2)}, u32[]{:S(2)}) %collective-permute-start.4) | collective-permute-done | bytes 196640 | tf_op jit(solution)/shard_map/ppermute | solution.py:345
  41.3 1.3 %collective-permute-start.5 = (bf16[64,1536]{1,0:T(8,128)(2,1)S(1)}, bf16[64,1536]{1,0:T(8,128)(2,1)S(1)}, u32[]{:S(2)}, u32[]{:S(2)}) collective-permute-start(bf16[64,1536]{1,0:T(8,128)(2,1)S(1)} %collective-permute-done.4.refs_4_), channel_id=1, source_target_pairs={{1,0},{2,3},{5,4},{6,7},{9,8},{10,11},{13,12},{14,15},{17,16},{18,... | collective-permute-start | bytes 589832 | tf_op jit(solution)/shard_map/ppermute | solution.py:352
  42.6 0.0 copy-start.1
  42.6 1.0 %copy-done.1 = bf16[64,2688]{1,0:T(8,128)(2,1)S(1)} copy-done((bf16[64,2688]{1,0:T(8,128)(2,1)S(1)}, bf16[64,2688]{1,0:T(8,128)(2,1)}, u32[]{:S(2)}) %copy-start.1) | copy-done | bytes 344088
  43.6 0.0 copy-start.2
  43.6 0.0 copy-start.3
  43.6 0.0 copy-start.4
  43.6 4.2 %shard_map.107 = (bf16[1536,1536]{1,0:T(8,128)(2,1)S(1)}, bf16[192,384]{1,0:T(8,128)(2,1)S(1)}, bf16[192,384]{1,0:T(8,128)(2,1)S(1)}, bf16[192,768]{1,0:T(8,128)(2,1)S(1)}, bf16[192,1536]{1,0:T(8,128)(2,1)S(1)}) custom-call(bf16[64,1536]{1,0:T(8,128)(2,1)S(1)} %collective-permute-done.1.refs_0_, bf16[64,1536]{1,0:T(8,128)(2,1)} %collective-permute-done.2.refs_1_, ...), custom_call_target="tpu_custom_call" | custom-call | flops 905969664 | bytes 11698180 | tf_op jit(solution)/shard_map/pallas_call | solution.py:41
  47.9 0.4 collective-permute-done.6.onward_ref
  48.3 0.0 collective-permute-done.3.middle_ref
  48.3 0.9 %shard_map.108 = (bf16[64,384]{1,0:T(8,128)(2,1)S(1)}, bf16[64,768]{1,0:T(8,128)(2,1)S(1)}, f32[64,768]{1,0:T(8,128)S(1)}, f32[64,768]{1,0:T(8,128)S(1)}) custom-call(bf16[64,2688]{1,0:T(8,128)(2,1)S(1)} %collective-permute-done.3.middle_ref, bf16[64,1536]{1,0:T(8,128)(2,1)S(1)} %collective-permute-done.6.onward_ref, s32[1]{0:T(128)} %bitcast.7.index_ref.refs_5_, ...), custom_call_target="tpu_custom_call" | custom-call | flops 301989888 | bytes 5799940 | tf_op jit(solution)/shard_map/pallas_call | solution.py:41
  49.2 0.0 all-to-all-done.1
  49.2 0.0 copy-done.2
  49.2 0.0 copy-done.3
  49.2 0.0 copy-done.4
  49.3 1.4 %shard_map.106 = (bf16[128,1536]{1,0:T(8,128)(2,1)}, bf16[8,16]{1,0:T(8,128)(2,1)}) custom-call(s32[8,16]{1,0:T(8,128)S(1)} %bitcast.22, s32[1,8]{1,0:T(1,128)S(1)} %bitcast.26, bf16[8,16]{1,0:T(8,128)(2,1)S(1)} %bitcast.24, bf16[128,1664]{1,0:T(8,128)(2,1)S(1)} %bitcast.20), custom_call_target="tpu_custom_call" | custom-call | flops 50331648 | bytes 820256 | tf_op jit(solution)/shard_map/pallas_call | solution.py:41
  50.6 1.3 %collective-permute-done.5.onward_ref = bf16[64,1536]{1,0:T(8,128)(2,1)S(1)} collective-permute-done((bf16[64,1536]{1,0:T(8,128)(2,1)S(1)}, bf16[64,1536]{1,0:T(8,128)(2,1)S(1)}, u32[]{:S(2)}, u32[]{:S(2)}) %collective-permute-start.5) | collective-permute-done | bytes 196640 | tf_op jit(solution)/shard_map/ppermute | solution.py:352
  51.9 1.6 %shard_map.109 = (bf16[384,1536]{1,0:T(8,128)(2,1)}, bf16[768,384]{1,0:T(8,128)(2,1)}) custom-call(bf16[64,2688]{1,0:T(8,128)(2,1)S(1)} %collective-permute-done.3.middle_ref, bf16[64,1536]{1,0:T(8,128)(2,1)S(1)} %collective-permute-done.5.onward_ref, bf16[192,384]{1,0:T(8,128)(2,1)S(1)} %get-tuple-element.53.refs_0_, ...), custom_call_target="tpu_custom_call" | custom-call | flops 452984832 | bytes 4030464 | tf_op jit(solution)/shard_map/pallas_call | solution.py:41
Async XLA Ops:
  0.6 24.0 %copy-start = (bf16[1,768,1536]{2,1,0:T(8,128)(2,1)S(1)}, bf16[1,768,1536]{2,1,0:T(8,128)(2,1)}, u32[]{:S(2)}) copy-start(bf16[1,768,1536]{2,1,0:T(8,128)(2,1)} %param.13) | copy-start | bytes 7077892
  20.4 12.4 %collective-permute-start.1 = (bf16[64,1536]{1,0:T(8,128)(2,1)S(1)}, bf16[64,1536]{1,0:T(8,128)(2,1)S(1)}, u32[]{:S(2)}, u32[]{:S(2)}) collective-permute-start(bf16[64,1536]{1,0:T(8,128)(2,1)S(1)} %get-tuple-element.34._.x_ref), channel_id=1, source_target_pairs={{0,1},{1,0},{2,3},{3,2},{4,5},{5,4},{6,7},{7,6},{8,9},{9,8},{10,11... | collective-permute-start | bytes 589832 | tf_op jit(solution)/shard_map/ppermute | solution.py:329
  22.0 11.2 %collective-permute-start.2 = (bf16[64,1536]{1,0:T(8,128)(2,1)S(1)}, bf16[64,1536]{1,0:T(8,128)(2,1)}, u32[]{:S(2)}, u32[]{:S(2)}) collective-permute-start(bf16[64,1536]{1,0:T(8,128)(2,1)S(1)} %get-tuple-element.34._.x_ref), channel_id=1, source_target_pairs={{0,2},{2,0},{1,3},{3,1},{4,6},{6,4},{5,7},{7,5},{8,10},{10,8},{9,1... | collective-permute-start | bytes 589832 | tf_op jit(solution)/shard_map/ppermute | solution.py:328
  26.2 10.5 %collective-permute-start = (bf16[64,1152]{1,0:T(8,128)(2,1)}, bf16[64,1152]{1,0:T(8,128)(2,1)S(1)}, u32[]{:S(2)}, u32[]{:S(2)}) collective-permute-start(bf16[64,1152]{1,0:T(8,128)(2,1)} %get-tuple-element.40), channel_id=1, source_target_pairs={{0,1},{1,0},{2,3},{3,2},{4,5},{5,4},{6,7},{7,6},{8,9},{9,8},{10,11... | collective-permute-start | bytes 442376 | tf_op jit(solution)/shard_map/ppermute | solution.py:330
  26.7 14.6 %collective-permute-start.4 = (bf16[64,1536]{1,0:T(8,128)(2,1)}, bf16[64,1536]{1,0:T(8,128)(2,1)S(1)}, u32[]{:S(2)}, u32[]{:S(2)}) collective-permute-start(bf16[64,1536]{1,0:T(8,128)(2,1)} %get-tuple-element.48), channel_id=1, source_target_pairs={{0,2},{2,0},{1,3},{3,1},{4,6},{6,4},{5,7},{7,5},{8,10},{10,8},{9,1... | collective-permute-start | bytes 589832 | tf_op jit(solution)/shard_map/ppermute | solution.py:345
  33.2 16.0 %all-to-all-start.1 = ((bf16[8,16,1664]{2,1,0:T(8,128)(2,1)}), bf16[8,16,1664]{2,1,0:T(8,128)(2,1)S(1)}, u32[]{:S(2)}, u32[]{:S(2)}) async-start(bf16[8,16,1664]{2,1,0:T(8,128)(2,1)} %bitcast.10), calls=%async_computation.1 | async-start | bytes 851968 | tf_op jit(solution)/shard_map/all_to_all | solution.py:265
  36.7 11.5 %collective-permute-start.3 = (bf16[64,2688]{1,0:T(8,128)(2,1)}, bf16[64,2688]{1,0:T(8,128)(2,1)S(1)}, u32[]{:S(2)}, u32[]{:S(2)}) collective-permute-start(bf16[64,2688]{1,0:T(8,128)(2,1)} %get-tuple-element.43), channel_id=1, source_target_pairs={{1,2},{2,1},{5,6},{6,5},{9,10},{10,9},{13,14},{14,13},{17,18},{18,... | collective-permute-start | bytes 1032200 | tf_op jit(solution)/shard_map/ppermute | solution.py:350
  37.4 10.8 %collective-permute-start.6 = (bf16[64,1536]{1,0:T(8,128)(2,1)}, bf16[64,1536]{1,0:T(8,128)(2,1)S(1)}, u32[]{:S(2)}, u32[]{:S(2)}) collective-permute-start(bf16[64,1536]{1,0:T(8,128)(2,1)} %collective-permute-done.2.refs_1_), channel_id=1, source_target_pairs={{1,0},{2,3},{5,4},{6,7},{9,8},{10,11},{13,12},{14,15},{17,16},{18,... | collective-permute-start | bytes 589832 | tf_op jit(solution)/shard_map/ppermute | solution.py:351
  41.3 10.6 %collective-permute-start.5 = (bf16[64,1536]{1,0:T(8,128)(2,1)S(1)}, bf16[64,1536]{1,0:T(8,128)(2,1)S(1)}, u32[]{:S(2)}, u32[]{:S(2)}) collective-permute-start(bf16[64,1536]{1,0:T(8,128)(2,1)S(1)} %collective-permute-done.4.refs_4_), channel_id=1, source_target_pairs={{1,0},{2,3},{5,4},{6,7},{9,8},{10,11},{13,12},{14,15},{17,16},{18,... | collective-permute-start | bytes 589832 | tf_op jit(solution)/shard_map/ppermute | solution.py:352
  42.6 1.0 %copy-start.1 = (bf16[64,2688]{1,0:T(8,128)(2,1)S(1)}, bf16[64,2688]{1,0:T(8,128)(2,1)}, u32[]{:S(2)}) copy-start(bf16[64,2688]{1,0:T(8,128)(2,1)} %get-tuple-element.51.refs_2_) | copy-start | bytes 1032196
  43.6 5.6 %copy-start.2 = (s32[1,1,8,16]{3,2,1,0:T(8,128)S(1)}, s32[1,1,8,16]{3,2,1,0:T(8,128)}, u32[]{:S(2)}) copy-start(s32[1,1,8,16]{3,2,1,0:T(8,128)} %param.9) | copy-start | bytes 1540
  43.6 5.6 %copy-start.3 = (bf16[1,1,8,16]{3,2,1,0:T(8,128)(2,1)S(1)}, bf16[1,1,8,16]{3,2,1,0:T(8,128)(2,1)}, u32[]{:S(2)}) copy-start(bf16[1,1,8,16]{3,2,1,0:T(8,128)(2,1)} %param.11) | copy-start | bytes 772
  43.6 5.6 %copy-start.4 = (s32[1,1,8]{2,1,0:T(1,128)S(1)}, s32[1,1,8]{2,1,0:T(1,128)}, u32[]{:S(2)}) copy-start(s32[1,1,8]{2,1,0:T(1,128)} %param.10) | copy-start | bytes 100

commit v6 on v5

--- a/solution.py
+++ b/solution.py
@@ -73,26 +73,26 @@
 
 
 def pick_rows(*refs):
-    sources, out_ref, held, sems = refs[:5], refs[5], refs[6:11], refs[11]
+    sources, gates_ref, out_ref, held, sems = refs[:4], refs[4], refs[5], refs[6:10], refs[10]
     copies = [
         pltpu.make_async_copy(source, target, sems.at[place])
         for place, (source, target) in enumerate(zip(sources, held))
     ]
     for copy in copies:
         copy.start()
-    rows_ref, counts_ref, gates_ref, tokens_ref, cot_ref = held
+    rows_ref, counts_ref, tokens_ref, cot_ref = held
     peers, most = rows_ref.shape
     slots = peers * most
     width = tokens_ref.shape[1]
     peer_hot, k_hot = slot_maps(peers, most)
-    for copy in copies[:3]:
+    for copy in copies[:2]:
         copy.wait()
     hot = token_hot(rows_ref, peer_hot, k_hot, tokens_ref.shape[0]).astype(BF16)
     used = used_column(counts_ref[...], peer_hot, most)
     gate = jnp.where(used, slot_column(gates_ref[...], peer_hot, k_hot), 0.0)
+    copies[2].wait()
+    out_ref[:, :width] = dot_nn(hot, tokens_ref[...]).astype(BF16)
     copies[3].wait()
-    out_ref[:, :width] = dot_nn(hot, tokens_ref[...]).astype(BF16)
-    copies[4].wait()
     out_ref[:, width : 2 * width] = (dot_nn(hot, cot_ref[...]) * gate).astype(BF16)
 
 
@@ -286,14 +286,14 @@
     hbm = pl.BlockSpec(memory_space=pltpu.HBM)
 
     w_in_far = pltpu.with_memory_space_constraint(w_in, pltpu.HBM)
-    picked = (rows, count, gates, tokens, cot)
+    picked = (rows, count, tokens, cot)
     (sent,) = call(
         pick_rows,
         [shape((slots, 2 * width), BF16)],
-        [pltpu.with_memory_space_constraint(a, pltpu.HBM) for a in picked],
+        [pltpu.with_memory_space_constraint(a, pltpu.HBM) for a in picked] + [gates],
         4 * slots * n_tokens * width,
-        [hbm] * 5,
-        [pltpu.VMEM(a.shape, a.dtype) for a in picked] + [pltpu.SemaphoreType.DMA((5,))],
+        [hbm] * 4 + [vmem],
+        [pltpu.VMEM(a.shape, a.dtype) for a in picked] + [pltpu.SemaphoreType.DMA((4,))],
         8,
     )
     arrived = to_experts(sent, peers)

time: 53.9 us -> 54.6 us (1.013)
  local copies, waits for them, and re-layouts: 0.99 us -> 1.82 us
    unnamed x10 -> x12, local copies, waits for them, and re-layouts: 0.99 us -> 1.82 us
where the time goes in v6:
time: 54.6 us; the launch traced here: 54.2 us
  blocking collectives  17.5 us (32%)
  Pallas kernels  17.2 us (32%)
  starting transfers between devices  11.7 us (21%)
  waiting for transfers between devices  5.18 us (9%)
  local copies, waits for them, and re-layouts  1.82 us (3%)
  between operations  0.78 us (1%)
    all_to_all x1, blocking collectives, to_experts(): lax.all_to_all(block.reshape(peers, slots // peers, width), 'expert', spl...  17.5 us
    pallas_call x8, Pallas kernels, call(): pl.pallas_call(body, out_shape=tuple(outs), in_specs=in_specs or [pl.Bloc...  17.2 us
    all_to_all x1, starting transfers between devices, to_experts(): lax.all_to_all(block.reshape(peers, slots // peers, width), 'expert', spl...  3.46 us
    ppermute x1, waiting for transfers between devices, on_device(): far = lax.ppermute(far_load, 'dp', FAR)  2.6 us
    ppermute x1, starting transfers between devices, on_device(): x_far = lax.ppermute(x_rows, 'dp', FAR)  2.59 us
    unnamed x12, local copies, waits for them, and re-layouts  1.82 us
    ppermute x1, starting transfers between devices, on_device(): x_near = lax.ppermute(x_rows, 'dp', NEAR)  1.64 us
    ppermute x1, waiting for transfers between devices, on_device(): onward = lax.ppermute(far, 'dp', ONWARD)  1.3 us
  transfers between devices with their start and end apart: 8, of which 5 were waited for; matrix products, arithmetic and copies ran while one was open for 0% of the time, Pallas kernels for 25%

profile of v6, /device:TPU:0, one launch (start us, length us, event | category | flops | bytes accessed | tf_op | source)
XLA Modules:
  0.0 54.2 jit_solution(10451740982645454611)
XLA Ops:
  0.6 0.0 copy-start
  0.6 0.0 copy-start.3
  0.7 0.8 %copy-done.3 = bf16[1,1,8,16]{3,2,1,0:T(8,128)(2,1)S(1)} copy-done((bf16[1,1,8,16]{3,2,1,0:T(8,128)(2,1)S(1)}, bf16[1,1,8,16]{3,2,1,0:T(8,128)(2,1)}, u32[]{:S(2)}) %copy-start.3) | copy-done | bytes 280
  1.5 1.6 %shard_map.102 = bf16[128,3072]{1,0:T(8,128)(2,1)S(1)} custom-call(s32[8,16]{1,0:T(8,128)} %bitcast.21, s32[1,8]{1,0:T(1,128)} %bitcast.25, bf16[128,1536]{1,0:T(8,128)(2,1)} %bitcast.29, bf16[128,1536]{1,0:T(8,128)(2,1)} %bitcast.30, bf16[8,16]{1,0:T(8,128)(2,1)S(1)} %bitcast.23), custom_call_target="tpu_custom_call" | custom-call | flops 100663296 | bytes 1573664 | tf_op jit(solution)/shard_map/pallas_call | solution.py:41
  3.0 17.5 %all_to_all.10 = bf16[8,16,3072]{2,1,0:T(8,128)(2,1)S(1)} all-to-all(bf16[8,16,3072]{2,1,0:T(8,128)(2,1)S(1)} %bitcast.18), channel_id=1, replica_groups=mesh['expert'=8,'dp'=4] {'expert'}, dimensions={0} | all-to-all | bytes 1572864 | tf_op jit(solution)/shard_map/all_to_all | solution.py:265
  20.6 0.5 shard_map.103
  21.0 1.6 %collective-permute-start.1 = (bf16[64,1536]{1,0:T(8,128)(2,1)S(1)}, bf16[64,1536]{1,0:T(8,128)(2,1)S(1)}, u32[]{:S(2)}, u32[]{:S(2)}) collective-permute-start(bf16[64,1536]{1,0:T(8,128)(2,1)S(1)} %get-tuple-element.34._.x_ref), channel_id=1, source_target_pairs={{0,1},{1,0},{2,3},{3,2},{4,5},{5,4},{6,7},{7,6},{8,9},{9,8},{10,11... | collective-permute-start | bytes 589832 | tf_op jit(solution)/shard_map/ppermute | solution.py:329
  22.7 2.6 %collective-permute-start.2 = (bf16[64,1536]{1,0:T(8,128)(2,1)S(1)}, bf16[64,1536]{1,0:T(8,128)(2,1)}, u32[]{:S(2)}, u32[]{:S(2)}) collective-permute-start(bf16[64,1536]{1,0:T(8,128)(2,1)S(1)} %get-tuple-element.34._.x_ref), channel_id=1, source_target_pairs={{0,2},{2,0},{1,3},{3,1},{4,6},{6,4},{5,7},{7,5},{8,10},{10,8},{9,1... | collective-permute-start | bytes 589832 | tf_op jit(solution)/shard_map/ppermute | solution.py:328
  25.3 0.0 copy-done
  25.3 1.6 %shard_map.104 = (f32[64,768]{1,0:T(8,128)S(1)}, bf16[64,1152]{1,0:T(8,128)(2,1)S(1)}, bf16[64,1152]{1,0:T(8,128)(2,1)S(1)}, bf16[64,1152]{1,0:T(8,128)(2,1)}, bf16[64,1536]{1,0:T(8,128)(2,1)}) custom-call(s32[1]{0:T(128)} %bitcast.7.index_ref.refs_5_, bf16[128,3072]{1,0:T(8,128)(2,1)S(1)} %bitcast.17, bf16[64,128]{1,0:T(8,128)(2,1)S(1)} %get-tuple-element.35.pack_ref, ...), custom_call_target="tpu_custom_call" | custom-call | flops 176160768 | bytes 4194308 | tf_op jit(solution)/shard_map/pallas_call | solution.py:41
  26.9 0.4 collective-permute-start
  27.3 0.3 collective-permute-start.4
  27.7 5.4 %shard_map.105 = (bf16[128,1664]{1,0:T(8,128)(2,1)}, bf16[64,2688]{1,0:T(8,128)(2,1)}, bf16[64,2688]{1,0:T(8,128)(2,1)}) custom-call(bf16[64,1536]{1,0:T(8,128)(2,1)S(1)} %get-tuple-element.34._.x_ref, f32[64,768]{1,0:T(8,128)S(1)} %get-tuple-element.36.grad_ref, bf16[64,128]{1,0:T(8,128)(2,1)S(1)} %get-tuple-element.35.pack_ref, ...), custom_call_target="tpu_custom_call" | custom-call | flops 603979776 | bytes 6537216 | tf_op jit(solution)/shard_map/pallas_call | solution.py:41
  33.0 0.4 collective-permute-done.1.refs_0_
  33.5 0.4 collective-permute-done.2.refs_1_
  33.9 3.5 %all-to-all-start.1 = ((bf16[8,16,1664]{2,1,0:T(8,128)(2,1)}), bf16[8,16,1664]{2,1,0:T(8,128)(2,1)S(1)}, u32[]{:S(2)}, u32[]{:S(2)}) async-start(bf16[8,16,1664]{2,1,0:T(8,128)(2,1)} %bitcast.10), calls=%async_computation.1 | async-start | bytes 851968 | tf_op jit(solution)/shard_map/all_to_all | solution.py:265
  37.4 0.0 collective-permute-done.refs_3_
  37.4 0.7 %collective-permute-start.3 = (bf16[64,2688]{1,0:T(8,128)(2,1)}, bf16[64,2688]{1,0:T(8,128)(2,1)S(1)}, u32[]{:S(2)}, u32[]{:S(2)}) collective-permute-start(bf16[64,2688]{1,0:T(8,128)(2,1)} %get-tuple-element.43), channel_id=1, source_target_pairs={{1,2},{2,1},{5,6},{6,5},{9,10},{10,9},{13,14},{14,13},{17,18},{18,... | collective-permute-start | bytes 1032200 | tf_op jit(solution)/shard_map/ppermute | solution.py:350
  38.1 1.3 %collective-permute-start.6 = (bf16[64,1536]{1,0:T(8,128)(2,1)}, bf16[64,1536]{1,0:T(8,128)(2,1)S(1)}, u32[]{:S(2)}, u32[]{:S(2)}) collective-permute-start(bf16[64,1536]{1,0:T(8,128)(2,1)} %collective-permute-done.2.refs_1_), channel_id=1, source_target_pairs={{1,0},{2,3},{5,4},{6,7},{9,8},{10,11},{13,12},{14,15},{17,16},{18,... | collective-permute-start | bytes 589832 | tf_op jit(solution)/shard_map/ppermute | solution.py:351
  39.4 2.6 %collective-permute-done.4.refs_4_ = bf16[64,1536]{1,0:T(8,128)(2,1)S(1)} collective-permute-done((bf16[64,1536]{1,0:T(8,128)(2,1)}, bf16[64,1536]{1,0:T(8,128)(2,1)S(1)}, u32[]{:S(2)}, u32[]{:S(2)}) %collective-permute-start.4) | collective-permute-done | bytes 196640 | tf_op jit(solution)/shard_map/ppermute | solution.py:345
  42.0 1.3 %collective-permute-start.5 = (bf16[64,1536]{1,0:T(8,128)(2,1)S(1)}, bf16[64,1536]{1,0:T(8,128)(2,1)S(1)}, u32[]{:S(2)}, u32[]{:S(2)}) collective-permute-start(bf16[64,1536]{1,0:T(8,128)(2,1)S(1)} %collective-permute-done.4.refs_4_), channel_id=1, source_target_pairs={{1,0},{2,3},{5,4},{6,7},{9,8},{10,11},{13,12},{14,15},{17,16},{18,... | collective-permute-start | bytes 589832 | tf_op jit(solution)/shard_map/ppermute | solution.py:352
  43.3 0.0 copy-start.1
  43.3 1.0 %copy-done.1 = bf16[64,2688]{1,0:T(8,128)(2,1)S(1)} copy-done((bf16[64,2688]{1,0:T(8,128)(2,1)S(1)}, bf16[64,2688]{1,0:T(8,128)(2,1)}, u32[]{:S(2)}) %copy-start.1) | copy-done | bytes 344088
  44.2 0.0 copy-start.2
  44.2 0.0 copy-start.4
  44.3 0.0 copy-start.5
  44.3 4.2 %shard_map.107 = (bf16[1536,1536]{1,0:T(8,128)(2,1)S(1)}, bf16[192,384]{1,0:T(8,128)(2,1)S(1)}, bf16[192,384]{1,0:T(8,128)(2,1)S(1)}, bf16[192,768]{1,0:T(8,128)(2,1)S(1)}, bf16[192,1536]{1,0:T(8,128)(2,1)S(1)}) custom-call(bf16[64,1536]{1,0:T(8,128)(2,1)S(1)} %collective-permute-done.1.refs_0_, bf16[64,1536]{1,0:T(8,128)(2,1)} %collective-permute-done.2.refs_1_, ...), custom_call_target="tpu_custom_call" | custom-call | flops 905969664 | bytes 11698180 | tf_op jit(solution)/shard_map/pallas_call | solution.py:41
  48.5 0.4 collective-permute-done.6.onward_ref
  48.9 0.0 collective-permute-done.3.middle_ref
  48.9 0.9 %shard_map.108 = (bf16[64,384]{1,0:T(8,128)(2,1)S(1)}, bf16[64,768]{1,0:T(8,128)(2,1)S(1)}, f32[64,768]{1,0:T(8,128)S(1)}, f32[64,768]{1,0:T(8,128)S(1)}) custom-call(bf16[64,2688]{1,0:T(8,128)(2,1)S(1)} %collective-permute-done.3.middle_ref, bf16[64,1536]{1,0:T(8,128)(2,1)S(1)} %collective-permute-done.6.onward_ref, s32[1]{0:T(128)} %bitcast.7.index_ref.refs_5_, ...), custom_call_target="tpu_custom_call" | custom-call | flops 301989888 | bytes 5799940 | tf_op jit(solution)/shard_map/pallas_call | solution.py:41
  49.9 0.0 all-to-all-done.1
  49.9 0.0 copy-done.2
  49.9 0.0 copy-done.4
  49.9 0.0 copy-done.5
  49.9 1.4 %shard_map.106 = (bf16[128,1536]{1,0:T(8,128)(2,1)}, bf16[8,16]{1,0:T(8,128)(2,1)}) custom-call(s32[8,16]{1,0:T(8,128)S(1)} %bitcast.22, s32[1,8]{1,0:T(1,128)S(1)} %bitcast.26, bf16[8,16]{1,0:T(8,128)(2,1)S(1)} %bitcast.24, bf16[128,1664]{1,0:T(8,128)(2,1)S(1)} %bitcast.20), custom_call_target="tpu_custom_call" | custom-call | flops 50331648 | bytes 820256 | tf_op jit(solution)/shard_map/pallas_call | solution.py:41
  51.3 1.3 %collective-permute-done.5.onward_ref = bf16[64,1536]{1,0:T(8,128)(2,1)S(1)} collective-permute-done((bf16[64,1536]{1,0:T(8,128)(2,1)S(1)}, bf16[64,1536]{1,0:T(8,128)(2,1)S(1)}, u32[]{:S(2)}, u32[]{:S(2)}) %collective-permute-start.5) | collective-permute-done | bytes 196640 | tf_op jit(solution)/shard_map/ppermute | solution.py:352
  52.6 1.6 %shard_map.109 = (bf16[384,1536]{1,0:T(8,128)(2,1)}, bf16[768,384]{1,0:T(8,128)(2,1)}) custom-call(bf16[64,2688]{1,0:T(8,128)(2,1)S(1)} %collective-permute-done.3.middle_ref, bf16[64,1536]{1,0:T(8,128)(2,1)S(1)} %collective-permute-done.5.onward_ref, bf16[192,384]{1,0:T(8,128)(2,1)S(1)} %get-tuple-element.53.refs_0_, ...), custom_call_target="tpu_custom_call" | custom-call | flops 452984832 | bytes 4030464 | tf_op jit(solution)/shard_map/pallas_call | solution.py:41
Async XLA Ops:
  0.6 24.6 %copy-start = (bf16[1,768,1536]{2,1,0:T(8,128)(2,1)S(1)}, bf16[1,768,1536]{2,1,0:T(8,128)(2,1)}, u32[]{:S(2)}) copy-start(bf16[1,768,1536]{2,1,0:T(8,128)(2,1)} %param.13) | copy-start | bytes 7077892
  0.6 0.8 %copy-start.3 = (bf16[1,1,8,16]{3,2,1,0:T(8,128)(2,1)S(1)}, bf16[1,1,8,16]{3,2,1,0:T(8,128)(2,1)}, u32[]{:S(2)}) copy-start(bf16[1,1,8,16]{3,2,1,0:T(8,128)(2,1)} %param.11) | copy-start | bytes 772
  21.0 12.4 %collective-permute-start.1 = (bf16[64,1536]{1,0:T(8,128)(2,1)S(1)}, bf16[64,1536]{1,0:T(8,128)(2,1)S(1)}, u32[]{:S(2)}, u32[]{:S(2)}) collective-permute-start(bf16[64,1536]{1,0:T(8,128)(2,1)S(1)} %get-tuple-element.34._.x_ref), channel_id=1, source_target_pairs={{0,1},{1,0},{2,3},{3,2},{4,5},{5,4},{6,7},{7,6},{8,9},{9,8},{10,11... | collective-permute-start | bytes 589832 | tf_op jit(solution)/shard_map/ppermute | solution.py:329
  22.7 11.2 %collective-permute-start.2 = (bf16[64,1536]{1,0:T(8,128)(2,1)S(1)}, bf16[64,1536]{1,0:T(8,128)(2,1)}, u32[]{:S(2)}, u32[]{:S(2)}) collective-permute-start(bf16[64,1536]{1,0:T(8,128)(2,1)S(1)} %get-tuple-element.34._.x_ref), channel_id=1, source_target_pairs={{0,2},{2,0},{1,3},{3,1},{4,6},{6,4},{5,7},{7,5},{8,10},{10,8},{9,1... | collective-permute-start | bytes 589832 | tf_op jit(solution)/shard_map/ppermute | solution.py:328
  26.9 10.5 %collective-permute-start = (bf16[64,1152]{1,0:T(8,128)(2,1)}, bf16[64,1152]{1,0:T(8,128)(2,1)S(1)}, u32[]{:S(2)}, u32[]{:S(2)}) collective-permute-start(bf16[64,1152]{1,0:T(8,128)(2,1)} %get-tuple-element.40), channel_id=1, source_target_pairs={{0,1},{1,0},{2,3},{3,2},{4,5},{5,4},{6,7},{7,6},{8,9},{9,8},{10,11... | collective-permute-start | bytes 442376 | tf_op jit(solution)/shard_map/ppermute | solution.py:330
  27.3 14.6 %collective-permute-start.4 = (bf16[64,1536]{1,0:T(8,128)(2,1)}, bf16[64,1536]{1,0:T(8,128)(2,1)S(1)}, u32[]{:S(2)}, u32[]{:S(2)}) collective-permute-start(bf16[64,1536]{1,0:T(8,128)(2,1)} %get-tuple-element.48), channel_id=1, source_target_pairs={{0,2},{2,0},{1,3},{3,1},{4,6},{6,4},{5,7},{7,5},{8,10},{10,8},{9,1... | collective-permute-start | bytes 589832 | tf_op jit(solution)/shard_map/ppermute | solution.py:345
  33.9 16.0 %all-to-all-start.1 = ((bf16[8,16,1664]{2,1,0:T(8,128)(2,1)}), bf16[8,16,1664]{2,1,0:T(8,128)(2,1)S(1)}, u32[]{:S(2)}, u32[]{:S(2)}) async-start(bf16[8,16,1664]{2,1,0:T(8,128)(2,1)} %bitcast.10), calls=%async_computation.1 | async-start | bytes 851968 | tf_op jit(solution)/shard_map/all_to_all | solution.py:265
  37.4 11.5 %collective-permute-start.3 = (bf16[64,2688]{1,0:T(8,128)(2,1)}, bf16[64,2688]{1,0:T(8,128)(2,1)S(1)}, u32[]{:S(2)}, u32[]{:S(2)}) collective-permute-start(bf16[64,2688]{1,0:T(8,128)(2,1)} %get-tuple-element.43), channel_id=1, source_target_pairs={{1,2},{2,1},{5,6},{6,5},{9,10},{10,9},{13,14},{14,13},{17,18},{18,... | collective-permute-start | bytes 1032200 | tf_op jit(solution)/shard_map/ppermute | solution.py:350
  38.1 10.8 %collective-permute-start.6 = (bf16[64,1536]{1,0:T(8,128)(2,1)}, bf16[64,1536]{1,0:T(8,128)(2,1)S(1)}, u32[]{:S(2)}, u32[]{:S(2)}) collective-permute-start(bf16[64,1536]{1,0:T(8,128)(2,1)} %collective-permute-done.2.refs_1_), channel_id=1, source_target_pairs={{1,0},{2,3},{5,4},{6,7},{9,8},{10,11},{13,12},{14,15},{17,16},{18,... | collective-permute-start | bytes 589832 | tf_op jit(solution)/shard_map/ppermute | solution.py:351
  42.0 10.6 %collective-permute-start.5 = (bf16[64,1536]{1,0:T(8,128)(2,1)S(1)}, bf16[64,1536]{1,0:T(8,128)(2,1)S(1)}, u32[]{:S(2)}, u32[]{:S(2)}) collective-permute-start(bf16[64,1536]{1,0:T(8,128)(2,1)S(1)} %collective-permute-done.4.refs_4_), channel_id=1, source_target_pairs={{1,0},{2,3},{5,4},{6,7},{9,8},{10,11},{13,12},{14,15},{17,16},{18,... | collective-permute-start | bytes 589832 | tf_op jit(solution)/shard_map/ppermute | solution.py:352
  43.3 1.0 %copy-start.1 = (bf16[64,2688]{1,0:T(8,128)(2,1)S(1)}, bf16[64,2688]{1,0:T(8,128)(2,1)}, u32[]{:S(2)}) copy-start(bf16[64,2688]{1,0:T(8,128)(2,1)} %get-tuple-element.51.refs_2_) | copy-start | bytes 1032196
  44.2 5.6 %copy-start.2 = (s32[1,1,8,16]{3,2,1,0:T(8,128)S(1)}, s32[1,1,8,16]{3,2,1,0:T(8,128)}, u32[]{:S(2)}) copy-start(s32[1,1,8,16]{3,2,1,0:T(8,128)} %param.9) | copy-start | bytes 1540
  44.2 5.6 %copy-start.4 = (bf16[1,1,8,16]{3,2,1,0:T(8,128)(2,1)S(1)}, bf16[1,1,8,16]{3,2,1,0:T(8,128)(2,1)}, u32[]{:S(2)}) copy-start(bf16[1,1,8,16]{3,2,1,0:T(8,128)(2,1)} %param.11) | copy-start | bytes 772
  44.3 5.6 %copy-start.5 = (s32[1,1,8]{2,1,0:T(1,128)S(1)}, s32[1,1,8]{2,1,0:T(1,128)}, u32[]{:S(2)}) copy-start(s32[1,1,8]{2,1,0:T(1,128)} %param.10) | copy-start | bytes 100
